TPU v7x, 32 devices: a whole 2x2x4 slice. The times are simulated.
32 devices in a mesh: dp: 4 (over x, core), fsdp: 8 (over z, y).
Axes of the slice: x: 2, y: 2, z: 4, core: 2. Of those that a mesh axis runs over, the one named last changes fastest.
Arguments:
- residues: bfloat16 [128, 32, 768], P(('dp', 'fsdp')), may hold values from -6 to 6
- pairs: bfloat16 [128, 32, 32, 256], P(('dp', 'fsdp')), may hold values from -6 to 6
- lengths: int32 [128], P(('dp', 'fsdp')), may hold values from 8 to 32, as said below
- time_bins: int32 [128], P(('dp', 'fsdp')), may hold values from 0 to 255
- cath_labels: int32 [128], P(('dp', 'fsdp')), may hold values from 0 to 1471
- residue_cotangent: bfloat16 [128, 32, 768], P(('dp', 'fsdp')), may hold values from -6 to 6
- pair_cotangent: bfloat16 [128, 32, 32, 256], P(('dp', 'fsdp')), may hold values from -6 to 6
- time_table: bfloat16 [256, 768], P('fsdp'), may hold values from -4 to 4
- cath_table: bfloat16 [1472, 768], P('fsdp'), may hold values from -4 to 4
- attn_modulation: bfloat16 [768, 1536], P('fsdp'), may hold values from -0.21875 to 0.21875
- attn_gate: bfloat16 [768, 768], P('fsdp'), may hold values from -0.21875 to 0.21875
- qkv_weight: bfloat16 [768, 2304], P('fsdp'), may hold values from -0.21875 to 0.21875
- bias_gain: bfloat16 [256], P('fsdp'), may hold values from 0.25 to 1.75
- bias_weight: bfloat16 [256, 12], P('fsdp'), may hold values from -0.375 to 0.375
- out_weight: bfloat16 [768, 768], P('fsdp'), may hold values from -1 to 1
- ffn_modulation: bfloat16 [768, 1536], P('fsdp'), may hold values from -0.21875 to 0.21875
- ffn_gate: bfloat16 [768, 768], P('fsdp'), may hold values from -0.21875 to 0.21875
- gate_up: bfloat16 [768, 6144], P('fsdp'), may hold values from -0.21875 to 0.21875
- down_weight: bfloat16 [3072, 768], P('fsdp'), may hold values from -0.3125 to 0.3125
- outer_gain: bfloat16 [768], P('fsdp'), may hold values from 0.25 to 1.75
- outer_weight: bfloat16 [768, 512], P('fsdp'), may hold values from -0.21875 to 0.21875
- outer_out: bfloat16 [256, 256], P('fsdp'), may hold values from -0.375 to 0.375
- pair_gain: bfloat16 [256], P('fsdp'), may hold values from 0.25 to 1.75
- pair_gate_up: bfloat16 [256, 2048], P('fsdp'), may hold values from -0.375 to 0.375
- pair_down: bfloat16 [1024, 256], P('fsdp'), may hold values from -0.3125 to 0.3125
Outputs:
- residues_out: bfloat16 [128, 32, 768], P(('dp', 'fsdp'))
- pairs_out: bfloat16 [128, 32, 32, 256], P(('dp', 'fsdp'))
- residues_grad: float32 [128, 32, 768], P(('dp', 'fsdp'))
- pairs_grad: float32 [128, 32, 32, 256], P(('dp', 'fsdp'))
- grad_time_table: float32 [256, 768], P('fsdp')
- grad_cath_table: float32 [1472, 768], P('fsdp')
- grad_attn_modulation: float32 [768, 1536], P('fsdp')
- grad_attn_gate: float32 [768, 768], P('fsdp')
- grad_qkv_weight: float32 [768, 2304], P('fsdp')
- grad_bias_gain: float32 [256], P('fsdp')
- grad_bias_weight: float32 [256, 12], P('fsdp')
- grad_out_weight: float32 [768, 768], P('fsdp')
- grad_ffn_modulation: float32 [768, 1536], P('fsdp')
- grad_ffn_gate: float32 [768, 768], P('fsdp')
- grad_gate_up: float32 [768, 6144], P('fsdp')
- grad_down_weight: float32 [3072, 768], P('fsdp')
- grad_outer_gain: float32 [768], P('fsdp')
- grad_outer_weight: float32 [768, 512], P('fsdp')
- grad_outer_out: float32 [256, 256], P('fsdp')
- grad_pair_gain: float32 [256], P('fsdp')
- grad_pair_gate_up: float32 [256, 2048], P('fsdp')
- grad_pair_down: float32 [1024, 256], P('fsdp')
Inputs may be any that keep to these rules, and one draw needn't show every extreme that they name: `lengths`: each chain holds 32, 16 or 8 residues; slots at and past that number are padding.
All inputs are finite; a program needn't handle non-finite values.
Results may differ from a plain program's by a relative error of at most 0.03.
Values may be sent and summed in bfloat16 or wider, within the bound.
No kernel may reach another device: no remote copies, remote signals or barrier semaphores. Data moves between devices by JAX's collectives and lax.ppermute only.
A program may use at most 256 MiB of HBM per device.

v0:
```python
import functools
import math

import jax
import jax.numpy as jnp
from jax import lax
from jax.experimental import pallas as pl
from jax.experimental.pallas import tpu as pltpu
from jax.sharding import PartitionSpec as P

EPSILON = 1e-05
F32 = jnp.float32
BF16 = jnp.bfloat16
VMEM_LIMIT = 56 * 1024 * 1024


def norm_parts(values):
    center = values - jnp.mean(values, -1, keepdims=True)
    inverse = lax.rsqrt(jnp.mean(center * center, -1, keepdims=True) + EPSILON)
    return center * inverse, inverse


def norm_back(normed, inverse, upstream):
    return inverse * (
        upstream
        - jnp.mean(upstream, -1, keepdims=True)
        - normed * jnp.mean(upstream * normed, -1, keepdims=True)
    )


def dot(left, right):
    return jnp.dot(left, right, preferred_element_type=F32)


def dot_nt(left, right):
    return lax.dot_general(left, right, (((1,), (1,)), ((), ())), preferred_element_type=F32)


def dot_tn(left, right):
    return lax.dot_general(left, right, (((0,), (0,)), ((), ())), preferred_element_type=F32)


def params():
    return pltpu.CompilerParams(vmem_limit_bytes=VMEM_LIMIT)


def whole(shape):
    return pl.BlockSpec(shape, lambda *_: (0,) * len(shape))


SMEM = pl.BlockSpec(memory_space=pltpu.SMEM)


def call_whole(kernel, name, outs, *operands):
    specs = [SMEM if a.dtype == jnp.int32 else whole(a.shape) for a in operands]
    return pl.pallas_call(
        kernel,
        grid=(1,),
        name=name,
        in_specs=specs,
        out_specs=[whole(o.shape) for o in outs],
        out_shape=outs,
        compiler_params=params(),
    )(*operands)


def struct(shape, dtype):
    return jax.ShapeDtypeStruct(shape, dtype)


def swap(values, axis, size, bit):
    return lax.ppermute(values, axis, [(i, i ^ bit) for i in range(size)])


def pick(values, index, axis):
    return lax.dynamic_index_in_dim(values, index, axis, keepdims=False)


def ordered(bit, own, other, axis):
    first = jnp.where(bit == 0, own, other)
    second = jnp.where(bit == 0, other, own)
    return jnp.stack([first, second], axis)


class Place:
    def __init__(self, n_dp, n_f):
        self.n_dp, self.n_f, self.ring = n_dp, n_f, n_f // 2
        self.d = lax.axis_index("dp")
        self.f = lax.axis_index("fsdp")
        self.core, self.x = self.d % 2, self.d // 2
        self.y, self.r = self.f % 2, self.f // 2

    def swap_core(self, values):
        return swap(values, "dp", self.n_dp, 1)

    def swap_x(self, values):
        return swap(values, "dp", self.n_dp, 2)

    def swap_y(self, values):
        return swap(values, "fsdp", self.n_f, 1)

    def shift_ring(self, values):
        return lax.ppermute(
            values, "fsdp", [(i, (i + 2) % self.n_f) for i in range(self.n_f)]
        )

    def gather_f(self, values):
        ring = self.ring
        held = jnp.zeros((ring,) + values.shape, values.dtype)
        held = lax.dynamic_update_index_in_dim(held, values, self.r, 0)
        moving = values
        for step in range(ring - 1):
            moving = self.shift_ring(moving)
            held = lax.dynamic_update_index_in_dim(
                held, moving, (self.r - 1 - step) % ring, 0
            )
        both = ordered(self.y, held, self.swap_y(held), 1)
        return both.reshape((self.n_f,) + values.shape)

    def gather_quarters(self, quarter):
        held = self.gather_f(quarter)
        held = ordered(self.x, held, self.swap_x(held), 1)
        held = ordered(self.core, held, self.swap_core(held), 2)
        return held.reshape((self.n_f, 4) + quarter.shape)

    def sum_f(self, values):
        bit = 1
        while bit < self.n_f:
            values = values + swap(values, "fsdp", self.n_f, bit)
            bit *= 2
        return values

    def gather_bits(self, values, axis, size, index):
        held = values[None]
        bit = 1
        while bit < size:
            other = swap(held, axis, size, bit)
            on = (index // bit) % 2
            held = ordered(on, held, other, 0).reshape((2 * held.shape[0],) + values.shape)
            bit *= 2
        return held

    def gather_bits_f(self, values):
        return self.gather_bits(values, "fsdp", self.n_f, self.f)

    def gather_bits_d(self, values):
        return self.gather_bits(values, "dp", self.n_dp, self.d)

    def rows_gather(self, values):
        mine = jnp.concatenate([values, self.swap_x(values)], 0)
        return jnp.concatenate([mine, self.swap_core(mine)], 0)

    def rows_reduce(self, mine, theirs):
        half = mine.shape[0] // 2
        mine = mine + self.swap_core(theirs).astype(F32)
        return mine[:half], self.swap_x(mine[half:].astype(BF16))

    def halve(self, values, axis, index, swapper):
        keep = pick(values, index, axis)
        other = swapper(pick(values, 1 - index, axis))
        return (keep.astype(F32) + other.astype(F32)).astype(BF16)

    def reduce_f(self, values):
        ring = self.ring
        rest = values.shape[1:]
        values = self.halve(values.reshape((ring, 2) + rest), 1, self.y, self.swap_y)
        moving = pick(values, (self.r - 1) % ring, 0)
        for step in range(ring - 1):
            own = pick(values, (self.r - 2 - step) % ring, 0)
            moving = (
                self.shift_ring(moving).astype(F32) + own.astype(F32)
            ).astype(BF16)
        return moving

    def reduce_all(self, values):
        n_f, rows, width = values.shape
        values = values.reshape(n_f, 2, 2, rows // 4, width)
        values = self.halve(values, 2, self.core, self.swap_core)
        values = self.halve(values, 1, self.x, self.swap_x)
        values = self.reduce_f(values)
        return self.spread_d(values).reshape(rows, width)

    def spread_d(self, values):
        held = ordered(self.x, values, self.swap_x(values), 0)
        held = ordered(self.core, held, self.swap_core(held), 1)
        return held.reshape((4,) + values.shape)


def to_blocks(values):
    rows, width = values.shape
    blocks = values.reshape(rows, width // 256, 256)
    return jnp.transpose(blocks, (1, 0, 2)).reshape(rows * (width // 256), 256)


def from_blocks(held, rows, width):
    lead = held.shape[:-2]
    blocks = held.reshape(lead + (width // 256, rows, 256))
    return jnp.swapaxes(blocks, -3, -2).reshape(lead + (rows, width))


def choose_matrix(group, part, member):
    row = lax.broadcasted_iota(jnp.int32, (1536, 384), 0)
    col = lax.broadcasted_iota(jnp.int32, (1536, 384), 1)
    want = (col // part) * group + member * part + col % part
    return jnp.where(row == want, 1.0, 0.0).astype(BF16)


def split_kernel(group, part, place_ref, full_ref, out_ref):
    choose = choose_matrix(group, part, place_ref[0])
    for chunk in range(full_ref.shape[1] // 1536):
        out_ref[:, chunk * 384 : chunk * 384 + 384] = dot(
            full_ref[:, chunk * 1536 : chunk * 1536 + 1536], choose
        ).astype(BF16)


def join_kernel(group, part, pieces_ref, out_ref):
    for member in range(4):
        choose = choose_matrix(group, part, member)
        for chunk in range(out_ref.shape[1] // 1536):
            span = slice(chunk * 1536, chunk * 1536 + 1536)
            term = dot_nt(pieces_ref[member][:, chunk * 384 : chunk * 384 + 384], choose)
            if member == 0:
                out_ref[:, span] = term
            else:
                out_ref[:, span] += term


def bias_kernel(pairs_ref, gain_ref, weight_ref, out_ref):
    normed, _ = norm_parts(pairs_ref[...].astype(F32))
    low = (normed * gain_ref[...]).astype(BF16)
    out_ref[...] = dot_nt(weight_ref[...], low)


def head_mask(heads, length, width):
    head_size = width // heads
    row = lax.broadcasted_iota(jnp.int32, (heads * length, width), 0) // length
    col = lax.broadcasted_iota(jnp.int32, (heads * length, width), 1) // head_size
    return row == col


def spread_heads(rows, mask, heads):
    return jnp.where(mask, jnp.concatenate([rows] * heads, 0), jnp.zeros((), rows.dtype))


def fold_heads(wide, mask, heads):
    kept = jnp.where(mask, wide, 0.0)
    return jnp.sum(kept.reshape(heads, wide.shape[0] // heads, wide.shape[1]), 0)


def keep_of(lengths_ref, chain, length):
    row = lax.broadcasted_iota(jnp.int32, (length, 1), 0)
    return (row < lengths_ref[chain]).astype(F32)


def attention_kernel(
    heads,
    lengths_ref,
    res_ref,
    mod_ref,
    qkv_w_ref,
    out_w_ref,
    bias_ref,
    first_in_ref,
    qkv_ref,
    prob_ref,
    attended_ref,
    branch_ref,
    first_out_ref,
    second_in_ref,
):
    chains, length, width = res_ref.shape
    factor = 1.0 / math.sqrt(width // heads)
    mask = head_mask(heads, length, width)
    for c in range(chains):
        rows = slice(c * length, (c + 1) * length)
        normed, _ = norm_parts(res_ref[c].astype(F32))
        scale = mod_ref[c : c + 1, :width]
        shift = mod_ref[c : c + 1, width : 2 * width]
        first_in_ref[rows] = (normed * (1.0 + scale) + shift).astype(BF16)
    qkv_ref[...] = dot(first_in_ref[...], qkv_w_ref[...]).astype(BF16)
    for c in range(chains):
        rows = slice(c * length, (c + 1) * length)
        queries = spread_heads(qkv_ref[rows, :width], mask, heads)
        keys = qkv_ref[rows, width : 2 * width]
        value_rows = qkv_ref[rows, 2 * width :]
        scores = dot_nt(queries, keys) * factor + bias_ref[c]
        column = lax.broadcasted_iota(jnp.int32, scores.shape, 1)
        scores = jnp.where(column < lengths_ref[c], scores, -1000000000.0)
        exps = jnp.exp(scores - jnp.max(scores, -1, keepdims=True))
        prob = exps / jnp.sum(exps, -1, keepdims=True)
        prob_ref[c] = prob
        wide = dot(prob.astype(BF16), value_rows)
        attended_ref[rows] = fold_heads(wide, mask, heads).astype(BF16)
    branch_ref[...] = dot(attended_ref[...], out_w_ref[...])
    for c in range(chains):
        rows = slice(c * length, (c + 1) * length)
        keep = keep_of(lengths_ref, c, length)
        gate = mod_ref[c : c + 1, 2 * width : 3 * width]
        first_out = res_ref[c].astype(F32) + keep * gate * branch_ref[rows]
        first_out_ref[rows] = first_out
        normed, _ = norm_parts(first_out)
        scale = mod_ref[c : c + 1, 3 * width : 4 * width]
        shift = mod_ref[c : c + 1, 4 * width : 5 * width]
        second_in_ref[rows] = (normed * (1.0 + scale) + shift).astype(BF16)


def silu_parts(gate):
    logistic = jax.nn.sigmoid(gate)
    act = gate * logistic
    return act, logistic + act * (1.0 - logistic)


def transition_kernel(rows_ref, weight_ref, gate_ref, up_ref, hidden_ref, mine_ref, theirs_ref):
    width = rows_ref.shape[1]
    part = (weight_ref.shape[1] - width) // 2
    half = mine_ref.shape[0]
    rows = rows_ref[...]
    gate = dot(rows, weight_ref[:, :part])
    up = dot(rows, weight_ref[:, part : 2 * part])
    gate_ref[...] = gate
    up_ref[...] = up
    hidden = (gate * jax.nn.sigmoid(gate) * up).astype(BF16)
    hidden_ref[...] = hidden
    down = weight_ref[:, 2 * part :]
    mine_ref[...] = dot(hidden[:half], down)
    theirs_ref[...] = dot(hidden[half:], down).astype(BF16)


def outer_kernel(
    lengths_ref,
    first_out_ref,
    branch_own_ref,
    branch_other_ref,
    mod_ref,
    gain_ref,
    weight_ref,
    branch_ref,
    second_out_ref,
    res_out_ref,
    outer_in_ref,
    sides_ref,
):
    chains, width = mod_ref.shape[0], first_out_ref.shape[1]
    length = first_out_ref.shape[0] // chains
    branch = branch_own_ref[...] + branch_other_ref[...].astype(F32)
    branch_ref[...] = branch
    for c in range(chains):
        rows = slice(c * length, (c + 1) * length)
        keep = keep_of(lengths_ref, c, length)
        gate = mod_ref[c : c + 1, 5 * width : 6 * width]
        second_out_ref[rows] = first_out_ref[rows] + keep * gate * branch[rows]
    second_out = second_out_ref[...]
    res_out_ref[...] = second_out.astype(BF16)
    normed, _ = norm_parts(second_out)
    outer_in_ref[...] = (normed * gain_ref[...]).astype(BF16)
    sides_ref[...] = dot(outer_in_ref[...], weight_ref[...])


def pair_kernel(
    lengths_ref,
    left_ref,
    right_ref,
    pairs_ref,
    cot_ref,
    gain_ref,
    outer_w_ref,
    gate_up_ref,
    down_ref,
    pair_out_ref,
    pair_grad_ref,
    left_grad_ref,
    right_grad_ref,
    g_gate_up_ref,
    g_down_ref,
    g_outer_ref,
    g_gain_ref,
    acc_gate_up,
    acc_down,
    acc_outer,
    acc_gain,
):
    chain, block = pl.program_id(0), pl.program_id(1)
    _, count, length, width = pairs_ref.shape
    rows = count * length
    hidden = down_ref.shape[0]
    size = lengths_ref[chain]

    @pl.when((chain == 0) & (block == 0))
    def _():
        acc_gate_up[...] = jnp.zeros_like(acc_gate_up)
        acc_down[...] = jnp.zeros_like(acc_down)
        acc_outer[...] = jnp.zeros_like(acc_outer)
        acc_gain[...] = jnp.zeros_like(acc_gain)

    @pl.when(block == 0)
    def _():
        right_grad_ref[...] = jnp.zeros_like(right_grad_ref)

    @pl.when(block * count >= size)
    def _():
        pair_out_ref[...] = pairs_ref[...]
        pair_grad_ref[...] = cot_ref[...].astype(F32)
        left_grad_ref[...] = jnp.zeros_like(left_grad_ref)

    @pl.when(block * count < size)
    def _():
        row_i = lax.broadcasted_iota(jnp.int32, (count, length, width), 0) + block * count
        row_j = lax.broadcasted_iota(jnp.int32, (count, length, width), 1)
        kept = ((row_i < size) & (row_j < size)).reshape(rows, width)
        left = left_ref[0]
        right = right_ref[0]
        outer = (left[:, None, :] * right[None, :, :]).reshape(rows, width).astype(BF16)
        term = dot(outer, outer_w_ref[...])
        pair_one = pairs_ref[0].reshape(rows, width).astype(F32) + jnp.where(kept, term, 0.0)
        normed, inverse = norm_parts(pair_one)
        gain = gain_ref[...]
        low = (normed * gain).astype(BF16)
        both = dot(low, gate_up_ref[...])
        gate, up = both[:, :hidden], both[:, hidden:]
        act, slope = silu_parts(gate)
        hid = (act * up).astype(BF16)
        pair_two = pair_one + jnp.where(kept, dot(hid, down_ref[...]), 0.0)
        pair_out_ref[0] = pair_two.astype(BF16).reshape(count, length, width)
        cot = cot_ref[0].reshape(rows, width)
        branch_grad = jnp.where(kept, cot, jnp.zeros((), BF16))
        acc_down[...] += dot_tn(branch_grad, hid)
        hid_grad = dot_nt(branch_grad, down_ref[...])
        gate_grad = (hid_grad * up * slope).astype(BF16)
        up_grad = (hid_grad * act).astype(BF16)
        acc_gate_up[:, :hidden] += dot_tn(low, gate_grad)
        acc_gate_up[:, hidden:] += dot_tn(low, up_grad)
        low_grad = dot_nt(gate_grad, gate_up_ref[:, :hidden]) + dot_nt(
            up_grad, gate_up_ref[:, hidden:]
        )
        acc_gain[...] += jnp.sum(low_grad * normed, 0, keepdims=True)
        one_grad = cot.astype(F32) + norm_back(normed, inverse, low_grad * gain)
        pair_grad_ref[0] = one_grad.reshape(count, length, width)
        outer_grad = jnp.where(kept, one_grad, 0.0).astype(BF16)
        acc_outer[...] += dot_tn(outer, outer_grad)
        prod = dot_nt(outer_grad, outer_w_ref[...]).reshape(count, length, width)
        left_grad_ref[0] = jnp.sum(prod * right[None], 1)
        right_grad_ref[0] += jnp.sum(prod * left[:, None, :], 0)

    @pl.when((chain == pl.num_programs(0) - 1) & (block == pl.num_programs(1) - 1))
    def _():
        g_gate_up_ref[...] = acc_gate_up[...].astype(BF16)
        g_down_ref[...] = acc_down[...].astype(BF16)
        g_outer_ref[...] = acc_outer[...].astype(BF16)
        g_gain_ref[...] = acc_gain[...]


def outer_back_kernel(
    lengths_ref,
    left_grad_ref,
    right_grad_ref,
    outer_in_ref,
    weight_ref,
    gain_ref,
    second_out_ref,
    cot_ref,
    branch_ref,
    mod_ref,
    g_weight_ref,
    g_gain_ref,
    second_grad_ref,
    branch_grad_ref,
    gate_pre_ref,
):
    chains, width = mod_ref.shape[0], second_out_ref.shape[1]
    length = second_out_ref.shape[0] // chains
    sides = jnp.concatenate([left_grad_ref[...], right_grad_ref[...]], 1).astype(BF16)
    upstream = dot_nt(sides, weight_ref[...])
    normed, inverse = norm_parts(second_out_ref[...])
    g_gain_ref[...] = jnp.sum(upstream * normed, 0, keepdims=True)
    second_grad_ref[...] = cot_ref[...].astype(F32) + norm_back(
        normed, inverse, upstream * gain_ref[...]
    )
    for c in range(chains):
        rows = slice(c * length, (c + 1) * length)
        keep = keep_of(lengths_ref, c, length)
        gate = mod_ref[c : c + 1, 5 * width : 6 * width]
        grad = keep * second_grad_ref[rows]
        branch_grad_ref[rows] = (gate * grad).astype(BF16)
        gate_pre_ref[c : c + 1] = (
            jnp.sum(branch_ref[rows] * grad, 0, keepdims=True) * gate * (1.0 - gate)
        )
    g_weight_ref[...] = dot_tn(outer_in_ref[...], sides).astype(BF16)


def transition_back_kernel(
    grad_ref, gate_ref, up_ref, weight_ref, gate_grad_ref, up_grad_ref, mine_ref, theirs_ref
):
    part = gate_ref.shape[1]
    half = mine_ref.shape[0]
    hid_grad = dot_nt(grad_ref[...], weight_ref[:, 2 * part :])
    act, slope = silu_parts(gate_ref[...])
    gate_grad = (hid_grad * up_ref[...] * slope).astype(BF16)
    up_grad = (hid_grad * act).astype(BF16)
    gate_grad_ref[...] = gate_grad
    up_grad_ref[...] = up_grad
    total = dot_nt(gate_grad, weight_ref[:, :part]) + dot_nt(up_grad, weight_ref[:, part : 2 * part])
    mine_ref[...] = total[:half]
    theirs_ref[...] = total[half:].astype(BF16)


def transition_grads_kernel(rows_ref, hidden_ref, grad_ref, gate_grad_ref, up_grad_ref, out_ref):
    part = gate_grad_ref.shape[1]
    rows = rows_ref[...]
    out_ref[:, :part] = dot_tn(rows, gate_grad_ref[...]).astype(BF16)
    out_ref[:, part : 2 * part] = dot_tn(rows, up_grad_ref[...]).astype(BF16)
    out_ref[:, 2 * part :] = dot_tn(hidden_ref[...], grad_ref[...]).astype(BF16)


def attention_back_kernel(
    heads,
    lengths_ref,
    own_ref,
    other_ref,
    mod_ref,
    first_out_ref,
    second_grad_ref,
    branch_ref,
    res_ref,
    qkv_ref,
    prob_ref,
    out_w_ref,
    qkv_w_ref,
    branch_grad_ref,
    qkv_grad_ref,
    scores_grad_ref,
    res_grad_ref,
    pre_ref,
    attended_grad,
    first_grad,
):
    chains, length, width = res_ref.shape
    factor = 1.0 / math.sqrt(width // heads)
    mask = head_mask(heads, length, width)
    for c in range(chains):
        rows = slice(c * length, (c + 1) * length)
        keep = keep_of(lengths_ref, c, length)
        upstream = own_ref[rows] + other_ref[rows].astype(F32)
        normed, inverse = norm_parts(first_out_ref[rows])
        pre_ref[c : c + 1, 3 * width : 4 * width] = jnp.sum(upstream * normed, 0, keepdims=True)
        pre_ref[c : c + 1, 4 * width : 5 * width] = jnp.sum(upstream, 0, keepdims=True)
        scale = mod_ref[c : c + 1, 3 * width : 4 * width]
        grad = second_grad_ref[rows] + norm_back(normed, inverse, upstream * (1.0 + scale))
        first_grad[rows] = grad
        gate = mod_ref[c : c + 1, 2 * width : 3 * width]
        kept = keep * grad
        branch_grad_ref[rows] = (gate * kept).astype(BF16)
        pre_ref[c : c + 1, 2 * width : 3 * width] = (
            jnp.sum(branch_ref[rows] * kept, 0, keepdims=True) * gate * (1.0 - gate)
        )
    attended_grad[...] = dot_nt(branch_grad_ref[...], out_w_ref[...]).astype(BF16)
    for c in range(chains):
        rows = slice(c * length, (c + 1) * length)
        queries = spread_heads(qkv_ref[rows, :width], mask, heads)
        keys = qkv_ref[rows, width : 2 * width]
        value_rows = qkv_ref[rows, 2 * width :]
        upstream = spread_heads(attended_grad[rows], mask, heads)
        prob = prob_ref[c]
        prob_grad = dot_nt(upstream, value_rows)
        scores_grad = (
            prob * (prob_grad - jnp.sum(prob_grad * prob, -1, keepdims=True))
        ).astype(BF16)
        scores_grad_ref[c] = scores_grad
        query_grad = fold_heads(dot(scores_grad, keys), mask, heads) * factor
        key_grad = dot_tn(scores_grad, queries) * factor
        value_grad = dot_tn(prob.astype(BF16), upstream)
        qkv_grad_ref[rows, :width] = query_grad.astype(BF16)
        qkv_grad_ref[rows, width : 2 * width] = key_grad.astype(BF16)
        qkv_grad_ref[rows, 2 * width :] = value_grad.astype(BF16)
    first_in_grad = dot_nt(qkv_grad_ref[...], qkv_w_ref[...])
    for c in range(chains):
        rows = slice(c * length, (c + 1) * length)
        upstream = first_in_grad[rows]
        normed, inverse = norm_parts(res_ref[c].astype(F32))
        pre_ref[c : c + 1, :width] = jnp.sum(upstream * normed, 0, keepdims=True)
        pre_ref[c : c + 1, width : 2 * width] = jnp.sum(upstream, 0, keepdims=True)
        scale = mod_ref[c : c + 1, :width]
        res_grad_ref[rows] = first_grad[rows] + norm_back(
            normed, inverse, upstream * (1.0 + scale)
        )


def weight_grad_kernel(in_ref, grad_ref, out_ref):
    out_ref[...] = dot_tn(in_ref[...], grad_ref[...]).astype(BF16)


def pair_last_kernel(
    pairs_ref, one_grad_ref, scores_grad_ref, gain_ref, weight_ref, out_ref, g_weight_ref, g_gain_ref
):
    normed, inverse = norm_parts(pairs_ref[...].astype(F32))
    gain = gain_ref[...]
    low = (normed * gain).astype(BF16)
    scores_grad = scores_grad_ref[...]
    upstream = dot_tn(scores_grad, weight_ref[...])
    out_ref[...] = one_grad_ref[...] + norm_back(normed, inverse, upstream * gain)

    @pl.when(pl.program_id(0) == 0)
    def _():
        g_weight_ref[...] = jnp.zeros_like(g_weight_ref)
        g_gain_ref[...] = jnp.zeros_like(g_gain_ref)

    g_weight_ref[...] += dot(scores_grad, low)
    g_gain_ref[...] += jnp.sum(upstream * normed, 0, keepdims=True)


def on_device(
    n_dp,
    n_f,
    residues,
    pairs,
    lengths,
    time_bins,
    cath_labels,
    residue_cotangent,
    pair_cotangent,
    time_table,
    cath_table,
    attn_modulation,
    attn_gate,
    qkv_weight,
    bias_gain,
    bias_weight,
    out_weight,
    ffn_modulation,
    ffn_gate,
    gate_up,
    down_weight,
    outer_gain,
    outer_weight,
    outer_out,
    pair_gain,
    pair_gate_up,
    pair_down,
):
    place = Place(n_dp, n_f)
    d, f = place.d, place.f
    chains, length, width = residues.shape
    rows = chains * length
    heads = bias_weight.shape[1]
    pair_width = outer_out.shape[1]
    pair_rows = chains * length * length
    time_rows, cath_rows = time_table.shape[0], cath_table.shape[0]
    mod_rows = attn_modulation.shape[0]
    hid_rows = down_weight.shape[0]
    hid_part = hid_rows // 4

    my_gate_up = pl.pallas_call(
        functools.partial(split_kernel, hid_rows, hid_part),
        name="split_gate_up",
        grid=(1,),
        in_specs=[SMEM, whole(gate_up.shape)],
        out_specs=whole((mod_rows, gate_up.shape[1] // 4)),
        out_shape=struct((mod_rows, gate_up.shape[1] // 4), BF16),
        compiler_params=params(),
    )(d.reshape(1).astype(jnp.int32), gate_up)
    my_down = pick(down_weight.reshape(4, hid_part, width), d, 0)
    ffn_weight = lax.all_gather(
        jnp.concatenate([my_gate_up, my_down], 1), "fsdp", axis=0, tiled=True
    )

    small = jnp.concatenate(
        [
            time_bins.astype(F32),
            cath_labels.astype(F32),
            bias_gain.astype(F32),
            pair_gain.astype(F32),
            outer_gain.astype(F32),
            bias_weight.astype(F32).reshape(-1),
        ]
    )
    small = place.sum_f(
        lax.dynamic_update_index_in_dim(jnp.zeros((n_f, small.shape[0]), F32), small, f, 0)
    )
    at = 0

    def take(size):
        nonlocal at
        part = small[:, at : at + size]
        at += size
        return part

    bins = take(chains).reshape(-1).astype(jnp.int32)
    labels = take(chains).reshape(-1).astype(jnp.int32)
    bias_gain_row = take(bias_gain.shape[0]).reshape(1, pair_width)
    pair_gain_row = take(pair_gain.shape[0]).reshape(1, pair_width)
    outer_gain_row = take(outer_gain.shape[0]).reshape(1, width)
    bias_w = take(bias_weight.size).reshape(pair_width, heads)
    bias_w_t = jnp.pad(bias_w.T, ((0, 16 - heads), (0, 0))).astype(BF16)

    quarter = mod_rows // 4
    qkv_q = pick(qkv_weight.reshape(4, quarter, qkv_weight.shape[1]), d, 0)
    qkv_full = place.gather_quarters(qkv_q).reshape(width, qkv_weight.shape[1])

    others = (out_weight, outer_weight, outer_out, pair_gate_up, pair_down)
    quarters = [pick(w.reshape(4, w.shape[0] // 4, w.shape[1]), d, 0) for w in others]
    packed = jnp.concatenate([to_blocks(q) for q in quarters], 0)
    held = place.gather_quarters(packed)
    unpacked, start = [], 0
    for q in quarters:
        count = q.shape[0] * q.shape[1] // 256
        block = from_blocks(held[:, :, start : start + count], *q.shape)
        unpacked.append(block.reshape(-1, q.shape[1]))
        start += count
    out_full, outer_w_full, outer_out_full, pair_gate_up_full, pair_down_full = unpacked

    time_hot = (
        (bins[:, None] - f * time_rows) == jnp.arange(time_rows)[None, :]
    ).astype(BF16)
    cath_hot = (
        (labels[:, None] - f * cath_rows) == jnp.arange(cath_rows)[None, :]
    ).astype(BF16)
    condition = place.sum_f(dot(time_hot, time_table) + dot(cath_hot, cath_table))
    cond_cols = lax.dynamic_slice_in_dim(condition.astype(BF16), f * mod_rows, mod_rows, 1)
    mods = jnp.concatenate(
        [
            dot(cond_cols, w)
            for w in (attn_modulation, attn_gate, ffn_modulation, ffn_gate)
        ],
        1,
    ).astype(BF16)
    mods = mods.reshape(n_f, chains, 6 * width)
    bit = n_f // 2
    while bit >= 1:
        mods = place.halve(
            mods.reshape((2, bit) + mods.shape[1:]),
            0,
            (f // bit) % 2,
            functools.partial(swap, axis="fsdp", size=n_f, bit=bit),
        )
        bit //= 2
    mods = mods.reshape(chains, 6 * width).astype(F32)
    gated = jnp.arange(6 * width)[None, :] // width
    mods = jnp.where((gated == 2) | (gated == 5), jax.nn.sigmoid(mods), mods)

    n_group = n_f * chains
    back_small = jnp.concatenate(
        [bins.astype(F32)[:, None], labels.astype(F32)[:, None], cond_cols.astype(F32)], 1
    )
    back_small = place.gather_bits_d(back_small).reshape(n_dp * n_group, -1)
    bins_all = back_small[:, 0].astype(jnp.int32)
    labels_all = back_small[:, 1].astype(jnp.int32)
    cond_all = back_small[:, 2:].astype(BF16)

    pairs_flat = pairs.reshape(pair_rows, pair_width)
    block = 512
    bias = pl.pallas_call(
        bias_kernel,
        name="pair_bias",
        grid=(pair_rows // block,),
        in_specs=[
            pl.BlockSpec((block, pair_width), lambda i: (i, 0)),
            whole((1, pair_width)),
            whole((16, pair_width)),
        ],
        out_specs=pl.BlockSpec((16, block), lambda i: (0, i)),
        out_shape=struct((16, pair_rows), F32),
        compiler_params=params(),
    )(pairs_flat, bias_gain_row, bias_w_t)
    bias = bias[:heads].reshape(heads, chains, length, length)
    bias = jnp.transpose(bias, (1, 0, 2, 3)).reshape(chains, heads * length, length)
    first_in, qkv, prob, attended, first_branch, first_out, second_in = call_whole(
        functools.partial(attention_kernel, heads),
        "attention",
        [
            struct((rows, width), BF16),
            struct((rows, 3 * width), BF16),
            struct((chains, heads * length, length), F32),
            struct((rows, width), BF16),
            struct((rows, width), F32),
            struct((rows, width), F32),
            struct((rows, width), BF16),
        ],
        lengths,
        residues,
        mods,
        qkv_full,
        out_full,
        bias,
    )

    rows_all = place.rows_gather(second_in)
    part = ffn_weight.shape[1] - width
    part //= 2
    gate, up, hidden, mine, theirs = call_whole(
        transition_kernel,
        "transition",
        [
            struct((4 * rows, part), F32),
            struct((4 * rows, part), F32),
            struct((4 * rows, part), BF16),
            struct((2 * rows, width), F32),
            struct((2 * rows, width), BF16),
        ],
        rows_all,
        ffn_weight,
    )
    branch_own, branch_other = place.rows_reduce(mine, theirs)
    second_branch, second_out, res_out, outer_in, sides = call_whole(
        outer_kernel,
        "outer_sides",
        [
            struct((rows, width), F32),
            struct((rows, width), F32),
            struct((rows, width), BF16),
            struct((rows, width), BF16),
            struct((rows, 2 * pair_width), F32),
        ],
        lengths,
        first_out,
        branch_own,
        branch_other,
        mods,
        outer_gain_row,
        outer_w_full,
    )

    sides = sides.reshape(chains, length, 2 * pair_width)
    count = 8
    pair_hidden = pair_down_full.shape[0]
    pair_block = pl.BlockSpec((1, count, length, pair_width), lambda c, b: (c, b, 0, 0))
    (
        pair_out,
        pair_grad,
        left_grad,
        right_grad,
        g_pair_gate_up,
        g_pair_down_t,
        g_outer_out,
        g_pair_gain,
    ) = pl.pallas_call(
        pair_kernel,
        name="pairs",
        grid=(chains, length // count),
        in_specs=[
            SMEM,
            pl.BlockSpec((1, count, pair_width), lambda c, b: (c, b, 0)),
            pl.BlockSpec((1, length, pair_width), lambda c, b: (c, 0, 1)),
            pair_block,
            pair_block,
            whole((1, pair_width)),
            whole(outer_out_full.shape),
            whole(pair_gate_up_full.shape),
            whole(pair_down_full.shape),
        ],
        out_specs=[
            pair_block,
            pair_block,
            pl.BlockSpec((1, count, pair_width), lambda c, b: (c, b, 0)),
            pl.BlockSpec((1, length, pair_width), lambda c, b: (c, 0, 0)),
            whole(pair_gate_up_full.shape),
            whole((pair_width, pair_hidden)),
            whole(outer_out_full.shape),
            whole((1, pair_width)),
        ],
        out_shape=[
            struct(pairs.shape, BF16),
            struct(pairs.shape, F32),
            struct((chains, length, pair_width), F32),
            struct((chains, length, pair_width), F32),
            struct(pair_gate_up_full.shape, BF16),
            struct((pair_width, pair_hidden), BF16),
            struct(outer_out_full.shape, BF16),
            struct((1, pair_width), F32),
        ],
        scratch_shapes=[
            pltpu.VMEM(pair_gate_up_full.shape, F32),
            pltpu.VMEM((pair_width, pair_hidden), F32),
            pltpu.VMEM(outer_out_full.shape, F32),
            pltpu.VMEM((1, pair_width), F32),
        ],
        compiler_params=params(),
    )(
        lengths,
        sides,
        sides,
        pairs,
        pair_cotangent,
        pair_gain_row,
        outer_out_full,
        pair_gate_up_full,
        pair_down_full,
    )

    g_outer_w, g_outer_gain, second_grad, branch_two_grad, second_pre = call_whole(
        outer_back_kernel,
        "outer_sides_back",
        [
            struct((width, 2 * pair_width), BF16),
            struct((1, width), F32),
            struct((rows, width), F32),
            struct((rows, width), BF16),
            struct((chains, width), F32),
        ],
        lengths,
        left_grad.reshape(rows, pair_width),
        right_grad.reshape(rows, pair_width),
        outer_in,
        outer_w_full,
        outer_gain_row,
        second_out,
        residue_cotangent.reshape(rows, width),
        second_branch,
        mods,
    )

    def by_owner(grad):
        w = grad.shape[1]
        blocks = grad.reshape(n_f, grad.shape[0] // n_f, w // 256, 256)
        return jnp.swapaxes(blocks, 1, 2).reshape(n_f, -1, 256)

    def gain_rows(grad):
        own = grad.reshape(n_f, 1, -1).astype(BF16)
        return jnp.pad(own, ((0, 0), (0, 3), (0, 256 - own.shape[2])))

    pair_terms = [
        by_owner(g_pair_gate_up),
        by_owner(g_pair_down_t.T),
        by_owner(g_outer_out),
        by_owner(g_outer_w),
        gain_rows(g_pair_gain),
        gain_rows(g_outer_gain),
    ]
    pair_sums = place.reduce_all(jnp.concatenate(pair_terms, 1)).astype(F32)
    at = 0

    def take_rows(shape):
        nonlocal at
        n = shape[0] * shape[1] // 256
        piece = from_blocks(pair_sums[at : at + n], *shape)
        at += n
        return piece

    out_pair_gate_up = take_rows(pair_gate_up.shape)
    out_pair_down = take_rows(pair_down.shape)
    out_outer_out = take_rows(outer_out.shape)
    out_outer_w = take_rows(outer_weight.shape)
    out_pair_gain = pair_sums[at, : pair_gain.shape[0]]
    out_outer_gain = pair_sums[at + 4, : outer_gain.shape[0]]

    grads_all = place.rows_gather(branch_two_grad)
    gate_grad, up_grad, mine, theirs = call_whole(
        transition_back_kernel,
        "transition_back",
        [
            struct((4 * rows, part), BF16),
            struct((4 * rows, part), BF16),
            struct((2 * rows, width), F32),
            struct((2 * rows, width), BF16),
        ],
        grads_all,
        gate,
        up,
        ffn_weight,
    )
    own, other = place.rows_reduce(mine, theirs)
    (g_ffn,) = call_whole(
        transition_grads_kernel,
        "transition_grads",
        [struct((width, 2 * part + width), BF16)],
        rows_all,
        hidden,
        grads_all,
        gate_grad,
        up_grad,
    )

    branch_one_grad, qkv_grad, scores_grad, res_grad, pre = pl.pallas_call(
        functools.partial(attention_back_kernel, heads),
        name="attention_back",
        grid=(1,),
        in_specs=[SMEM]
        + [
            whole(a.shape)
            for a in (
                own,
                other,
                mods,
                first_out,
                second_grad,
                first_branch,
                residues,
                qkv,
                prob,
                out_full,
                qkv_full,
            )
        ],
        out_specs=[
            whole((rows, width)),
            whole((rows, 3 * width)),
            whole((chains, heads * length, length)),
            whole((rows, width)),
            whole((chains, 5 * width)),
        ],
        out_shape=[
            struct((rows, width), BF16),
            struct((rows, 3 * width), BF16),
            struct((chains, heads * length, length), BF16),
            struct((rows, width), F32),
            struct((chains, 5 * width), F32),
        ],
        scratch_shapes=[pltpu.VMEM((rows, width), BF16), pltpu.VMEM((rows, width), F32)],
        compiler_params=params(),
    )(
        lengths,
        own,
        other,
        mods,
        first_out,
        second_grad,
        first_branch,
        residues,
        qkv,
        prob,
        out_full,
        qkv_full,
    )
    (g_qkv,) = call_whole(
        weight_grad_kernel, "qkv_grads", [struct((width, 3 * width), BF16)], first_in, qkv_grad
    )
    (g_out,) = call_whole(
        weight_grad_kernel, "out_grads", [struct((width, width), BF16)], attended, branch_one_grad
    )

    pre = jnp.concatenate([pre, second_pre], 1).astype(BF16)
    pre_group = place.gather_bits_f(pre).reshape(n_group, 6 * width)
    mod_weights = (attn_modulation, attn_gate, ffn_modulation, ffn_gate)
    spans, at_col = [], 0
    for w in mod_weights:
        spans.append(slice(at_col, at_col + w.shape[1]))
        at_col += w.shape[1]
    cond_grad = sum(dot_nt(pre_group[:, s], w) for s, w in zip(spans, mod_weights))
    cond_grad = place.gather_bits_f(cond_grad.astype(BF16))
    cond_grad = jnp.transpose(cond_grad, (1, 0, 2)).reshape(n_group, width)
    cond_grad = place.gather_bits_d(cond_grad).reshape(n_dp * n_group, width)
    pre_all = place.gather_bits_d(pre_group).reshape(n_dp * n_group, 6 * width)
    g_mods = dot_tn(cond_all, pre_all)
    time_all = (
        (bins_all[:, None] - f * time_rows) == jnp.arange(time_rows)[None, :]
    ).astype(BF16)
    cath_all = (
        (labels_all[:, None] - f * cath_rows) == jnp.arange(cath_rows)[None, :]
    ).astype(BF16)
    out_time = dot_tn(time_all, cond_grad)
    out_cath = dot_tn(cath_all, cond_grad)

    attn_sums = place.reduce_all(
        jnp.concatenate([g_qkv, g_out], 1).reshape(n_f, mod_rows, 4 * width)
    ).astype(F32)
    out_qkv = attn_sums[:, : 3 * width]
    out_out = attn_sums[:, 3 * width :]

    ffn_sums = place.spread_d(place.reduce_f(g_ffn.reshape(n_f, mod_rows, 2 * part + width)))
    (out_gate_up,) = call_whole(
        functools.partial(join_kernel, hid_rows, hid_part),
        "join_gate_up",
        [struct(gate_up.shape, F32)],
        ffn_sums[:, :, : 2 * part],
    )
    out_down = ffn_sums[:, :, 2 * part :].astype(F32).reshape(hid_rows, width)

    scores_t = jnp.transpose(
        scores_grad.reshape(chains, heads, length, length), (1, 0, 2, 3)
    ).reshape(heads, pair_rows)
    scores_t = jnp.pad(scores_t, ((0, 16 - heads), (0, 0)))
    pairs_grad, g_bias_w, g_bias_gain = pl.pallas_call(
        pair_last_kernel,
        name="pairs_last",
        grid=(pair_rows // block,),
        in_specs=[
            pl.BlockSpec((block, pair_width), lambda i: (i, 0)),
            pl.BlockSpec((block, pair_width), lambda i: (i, 0)),
            pl.BlockSpec((16, block), lambda i: (0, i)),
            whole((1, pair_width)),
            whole((16, pair_width)),
        ],
        out_specs=[
            pl.BlockSpec((block, pair_width), lambda i: (i, 0)),
            whole((16, pair_width)),
            whole((1, pair_width)),
        ],
        out_shape=[
            struct((pair_rows, pair_width), F32),
            struct((16, pair_width), F32),
            struct((1, pair_width), F32),
        ],
        compiler_params=params(),
    )(pairs_flat, pair_grad.reshape(pair_rows, pair_width), scores_t, bias_gain_row, bias_w_t)

    bias_terms = jnp.concatenate([g_bias_w[:heads], g_bias_gain], 0)
    for axis, size in (("dp", n_dp), ("fsdp", n_f)):
        bit = 1
        while bit < size:
            bias_terms = bias_terms + swap(bias_terms, axis, size, bit)
            bit *= 2
    bias_rows = bias_weight.shape[0]
    mine = lax.dynamic_slice_in_dim(bias_terms, f * bias_rows, bias_rows, 1)
    out_bias_w = mine[:heads].T
    out_bias_gain = mine[heads]

    return (
        res_out.reshape(residues.shape),
        pair_out,
        res_grad.reshape(residues.shape),
        pairs_grad.reshape(pairs.shape),
        out_time,
        out_cath,
        g_mods[:, spans[0]],
        g_mods[:, spans[1]],
        out_qkv,
        out_bias_gain,
        out_bias_w,
        out_out,
        g_mods[:, spans[2]],
        g_mods[:, spans[3]],
        out_gate_up,
        out_down,
        out_outer_gain,
        out_outer_w,
        out_outer_out,
        out_pair_gain,
        out_pair_gate_up,
        out_pair_down,
    )


def solution(mesh):
    chains3 = P(("dp", "fsdp"), None, None)
    chains4 = P(("dp", "fsdp"), None, None, None)
    chains1 = P(("dp", "fsdp"))
    table = P("fsdp", None)
    line = P("fsdp")
    weights = (
        table,
        table,
        table,
        table,
        table,
        line,
        table,
        table,
        table,
        table,
        table,
        table,
        line,
        table,
        table,
        line,
        table,
        table,
    )
    return jax.shard_map(
        functools.partial(on_device, mesh.shape["dp"], mesh.shape["fsdp"]),
        mesh=mesh,
        in_specs=(chains3, chains4, chains1, chains1, chains1, chains3, chains4) + weights,
        out_specs=(chains3, chains4, chains3, chains4) + weights,
        check_vma=False,
    )
```

profile of v0, /device:TPU:1, one launch (start us, length us, event | category | flops | bytes accessed | tf_op | source)
XLA Modules:
  0.0 511.5 jit_solution(13228962250940550230)
XLA Ops:
  11.1 2.1 collective-permute-start.15
  17.7 2.1 concatenate.63
  21.2 3.0 split_gate_up.1
  24.3 1.8 pad_maximum_fusion.11
  30.1 2.3 collective-permute-done.2
  35.0 6.7 %pair_bias.1 = f32[16,4096]{1,0:T(8,128)} custom-call(bf16[4096,256]{1,0:T(8,128)(2,1)} %bitcast.405, f32[1,256]{1,0:T(1,128)} %reshape.450.gain_ref, bf16[16,256]{1,0:T(8,128)(2,1)} %pad.17.weight_ref), custom_call_target="tpu_custom_call" | custom-call | tf_op jit(solution)/shard_map/pair_bias/pallas_call | solution.py:750
  46.7 4.5 collective-permute-done.10
  51.3 4.7 collective-permute-done.16
  56.8 1.9 collective-permute-start.5
  58.7 2.0 collective-permute-done.11
  62.1 6.4 %collective-permute-done.5 = f32[32,768]{1,0:T(8,128)S(1)} collective-permute-done((f32[32,768]{1,0:T(8,128)S(1)}, f32[32,768]{1,0:T(8,128)S(1)}, u32[]{:S(2)}, u32[]{:S(2)}) %collective-permute-start.5) | collective-permute-done | bytes 98336 | tf_op jit(solution)/shard_map/ppermute | solution.py:72
  71.0 14.6 %collective-permute-done.6 = bf16[4,4,4608]{2,1,0:T(4,128)(2,1)S(1)} collective-permute-done((bf16[4,4,4608]{2,1,0:T(4,128)(2,1)S(1)}, bf16[4,4,4608]{2,1,0:T(4,128)(2,1)S(1)}, u32[]{:S(2)}, u32[]{:S(2)}) %collective-permute-start.6) | collective-permute-done | bytes 147488 | tf_op jit(solution)/shard_map/ppermute | solution.py:72
  87.3 5.1 collective-permute-done.7
  92.5 6.9 %collective-permute-done.18 = bf16[4,224,256]{2,1,0:T(8,128)(2,1)S(1)} collective-permute-done((bf16[4,224,256]{2,1,0:T(8,128)(2,1)S(1)}, bf16[4,224,256]{2,1,0:T(8,128)(2,1)S(1)}, u32[]{:S(2)}, u32[]{:S(2)}) %collective-permute-start.18) | collective-permute-done | bytes 458784 | tf_op jit(solution)/shard_map/ppermute | solution.py:72
  100.7 1.9 collective-permute-done.13
  103.0 10.8 %collective-permute-start.14 = (bf16[8,2,24,2304]{3,2,1,0:T(8,128)(2,1)S(1)}, bf16[8,2,24,2304]{3,2,1,0:T(8,128)(2,1)S(1)}, u32[]{:S(2)}, u32[]{:S(2)}) collective-permute-start(bf16[8,2,24,2304]{3,2,1,0:T(8,128)(2,1)S(1)} %pad_maximum_fusion.4), channel_id=1, source_target_pairs={{0,8},{8,0},{16,24},{24,16},{1,9},{9,1},{17,25},{25,17},{2,10},{10... | collective-permute-start | bytes 5308424 | tf_op jit(solution)/shard_map/ppermute | solution.py:72
  115.0 7.2 %collective-permute-done.19 = bf16[8,224,256]{2,1,0:T(8,128)(2,1)S(1)} collective-permute-done((bf16[8,224,256]{2,1,0:T(8,128)(2,1)S(1)}, bf16[8,224,256]{2,1,0:T(8,128)(2,1)S(1)}, u32[]{:S(2)}, u32[]{:S(2)}) %collective-permute-start.19) | collective-permute-done | bytes 917536 | tf_op jit(solution)/shard_map/ppermute | solution.py:72
  122.6 5.7 %collective-permute-start.20 = (bf16[8,2,224,256]{3,2,0,1:T(8,128)(2,1)S(1)}, bf16[8,2,224,256]{3,2,0,1:T(8,128)(2,1)S(1)}, u32[]{:S(2)}, u32[]{:S(2)}) collective-permute-start(bf16[8,2,224,256]{3,2,0,1:T(8,128)(2,1)S(1)} %pad_maximum_fusion.3), channel_id=1, source_target_pairs={{0,8},{8,0},{16,24},{24,16},{1,9},{9,1},{17,25},{25,17},{2,10},{10... | collective-permute-start | bytes 5505032 | tf_op jit(solution)/shard_map/ppermute | solution.py:72
  129.3 2.1 pad_maximum_fusion.2
  135.7 6.5 %attention.1 = (bf16[128,768]{1,0:T(8,128)(2,1)}, bf16[128,2304]{1,0:T(8,128)(2,1)}, f32[4,384,32]{2,1,0:T(8,128)}, bf16[128,768]{1,0:T(8,128)(2,1)}, f32[128,76...) custom-call(s32[4]{0:T(128)} %lengths_ref.9, bf16[4,32,768]{2,1,0:T(8,128)(2,1)} %res_ref.3, ...), custom_call_target="tpu_custom_call" | custom-call | tf_op jit(solution)/shard_map/attention/pallas_call | solution.py:56
  143.4 5.1 collective-permute-done.21
  153.0 5.5 %transition.1 = (f32[512,768]{1,0:T(8,128)}, f32[512,768]{1,0:T(8,128)}, bf16[512,768]{1,0:T(8,128)(2,1)}, f32[256,768]{1,0:T(8,128)}, bf16[256,768]{1,0:T(8,128)(2,1)}) custom-call(bf16[512,768]{1,0:T(8,128)(2,1)} %copy-done.13, bf16[768,2304]{1,0:T(8,128)(2,1)} %all-gather.2.cloned.1.call-done.weight_ref), custom_call_target="tpu_custom_call" | custom-call | tf_op jit(solution)/shard_map/transition/pallas_call | solution.py:56
  166.5 2.3 slice.176
  168.8 1.9 slice.177
  175.5 2.7 outer_sides.1
  178.1 37.8 %pairs.1 = (bf16[4,32,32,256]{3,2,1,0:T(8,128)(2,1)}, f32[4,32,32,256]{3,2,1,0:T(8,128)}, f32[4,32,256]{2,1,0:T(8,128)}, f32[4,32,256]{2,1,0:T(8,128)}, bf16[256...) custom-call(s32[4]{0:T(128)} %lengths_ref.9, ...), custom_call_target="tpu_custom_call" | custom-call | tf_op jit(solution)/shard_map/pairs/pallas_call | solution.py:834
  216.0 3.3 outer_sides_back.1
  220.9 4.8 collective-permute-done.25
  230.4 6.8 %transition_back.1 = (bf16[512,768]{1,0:T(8,128)(2,1)}, bf16[512,768]{1,0:T(8,128)(2,1)}, f32[256,768]{1,0:T(8,128)}, bf16[256,768]{1,0:T(8,128)(2,1)}) custom-call(bf16[512,768]{1,0:T(8,128)(2,1)} %copy-done.12, f32[512,768]{1,0:T(8,128)} %get-tuple-element.77.gate_ref, f32[512,768]{1,0:T(8,128)} %get-tuple-element.78.up_ref, ...), custom_call_target="tpu_custom_call" | custom-call | tf_op jit(solution)/shard_map/transition_back/pallas_call | solution.py:56
  237.9 2.3 reshape.484
  243.2 8.9 %concatenate.81 = bf16[8,616,256]{2,1,0:T(8,128)(2,1)S(1)} concatenate(bf16[8,256,256]{2,1,0:T(8,128)(2,1)} %bitcast.427, bf16[8,128,256]{2,1,0:T(8,128)(2,1)S(1)} %bitcast.439, bf16[8,32,256]{2,1,0:T(8,128)(2,1)} %bitcast.464, bf16[8,192,256]{2,1,0:T(8,128)(2,1)} %bitcast.433, bf16[8,4,256]{2,1,0:T(4,128)(2,1)S(1)} %pad.19, bf16[8,4,256]{2,1,0:T(4,128)(2,1)S(1)} %pad.20), dimensions={1} | concatenate | bytes 5046272 | tf_op jit(solution)/shard_map/concatenate | solution.py:927
  255.6 5.9 %transition_grads.1 = bf16[768,2304]{1,0:T(8,128)(2,1)} custom-call(bf16[512,768]{1,0:T(8,128)(2,1)} %copy-done.13, bf16[512,768]{1,0:T(8,128)(2,1)} %get-tuple-element.97.hidden_ref, bf16[512,768]{1,0:T(8,128)(2,1)} %copy-done.12, bf16[512,768]{1,0:T(8,128)(2,1)} %get-tuple-element.98.gate_grad_ref, bf16[512,768]{1,0:T(8,128)(2,1)} %get-tuple-element.99.up_grad_ref), custom_call_target="tpu_custom_call" | custom-call | tf_op jit(solution)/shard_map/transition_grads/pallas_call | solution.py:56
  263.0 9.1 %attention_back.1 = (bf16[128,768]{1,0:T(8,128)(2,1)}, bf16[128,2304]{1,0:T(8,128)(2,1)}, bf16[4,384,32]{2,1,0:T(8,128)(2,1)}, f32[128,768]{1,0:T(8,128)}, f32[4,3840]{1,0:T(4,128)}) custom-call(s32[4]{0:T(128)} %lengths_ref.9, f32[128,768]{1,0:T(8,128)} %slice.178.own_ref, bf16[128,768]{1,0:T(8,128)(2,1)} %copy-done.24, ...), custom_call_target="tpu_custom_call" | custom-call | tf_op jit(solution)/shard_map/attention_back/pallas_call | solution.py:971
  274.2 9.0 %pairs_last.1 = (f32[4096,256]{1,0:T(8,128)}, f32[16,256]{1,0:T(8,128)}, f32[1,256]{1,0:T(1,128)}) custom-call(bf16[4096,256]{1,0:T(8,128)(2,1)} %bitcast.406, f32[4096,256]{1,0:T(8,128)} %bitcast.428, bf16[16,4096]{1,0:T(8,128)(2,1)} %pad.18.scores_grad_ref, f32[1,256]{1,0:T(1,128)} %reshape.450.gain_ref, bf16[16,256]{1,0:T(8,128)(2,1)} %pad.17.weight_ref), custom_call_target="tpu_custom_call" | custom-call | tf_op jit(solution)/shard_map/pairs_last/pallas_call | solution.py:1070
  284.6 4.6 collective-permute-start.31
  292.3 4.1 qkv_grads.1
  296.4 2.5 out_grads.1
  299.9 2.9 pad_maximum_fusion
  302.9 28.9 %collective-permute-done.51 = f32[13,256]{1,0:T(8,128)S(1)} collective-permute-done((f32[13,256]{1,0:T(8,128)S(1)}, f32[13,256]{1,0:T(8,128)S(1)}, u32[]{:S(2)}, u32[]{:S(2)}) %collective-permute-start.51) | collective-permute-done | bytes 13344 | tf_op jit(solution)/shard_map/ppermute | solution.py:72
  332.0 1.9 collective-permute-start.33
  335.4 1.9 collective-permute-start.41
  337.7 3.2 collective-permute-done.33
  347.2 1.8 collective-permute-done.34
  349.7 2.1 collective-permute-done.35
  352.4 3.3 collective-permute-done.36
  355.9 5.4 %collective-permute-start.37 = (bf16[1,32,768]{2,1,0:T(8,128)(2,1)S(1)}, bf16[1,32,768]{2,1,0:T(8,128)(2,1)S(1)}, u32[]{:S(2)}, u32[]{:S(2)}) collective-permute-start(bf16[1,32,768]{2,1,0:T(8,128)(2,1)S(1)} %broadcast_in_dim_reshape.3), channel_id=1, source_target_pairs={{0,8},{8,0},{16,24},{24,16},{1,9},{9,1},{17,25},{25,17},{2,10},{10... | collective-permute-start | bytes 147464 | tf_op jit(solution)/shard_map/ppermute | solution.py:72
  365.7 1.9 collective-permute-done.38
  369.8 11.2 %collective-permute-done.61 = bf16[8,154,256]{2,0,1:T(8,128)(2,1)S(1)} collective-permute-done((bf16[8,154,256]{2,0,1:T(8,128)(2,1)S(1)}, bf16[8,154,256]{2,0,1:T(8,128)(2,1)S(1)}, u32[]{:S(2)}, u32[]{:S(2)}) %collective-permute-start.61) | collective-permute-done | bytes 630816 | tf_op jit(solution)/shard_map/ppermute | solution.py:72
  383.5 6.4 %collective-permute-done.62 = bf16[4,154,256]{2,1,0:T(8,128)(2,1)S(1)} collective-permute-done((bf16[4,154,256]{2,1,0:T(8,128)(2,1)S(1)}, bf16[4,154,256]{2,1,0:T(8,128)(2,1)S(1)}, u32[]{:S(2)}, u32[]{:S(2)}) %collective-permute-start.62) | collective-permute-done | bytes 315424 | tf_op jit(solution)/shard_map/ppermute | solution.py:72
  391.0 4.2 collective-permute-done.63
  398.7 2.3 fusion.1
  401.6 4.5 collective-permute-done.65
  409.9 6.4 %collective-permute-start.67 = (bf16[2,154,256]{2,1,0:T(8,128)(2,1)S(1)}, bf16[2,154,256]{2,1,0:T(8,128)(2,1)S(1)}, u32[]{:S(2)}, u32[]{:S(2)}) collective-permute-start(bf16[2,154,256]{2,1,0:T(8,128)(2,1)S(1)} %pad_maximum_fusion.17), channel_id=1, source_target_pairs={{0,8},{8,0},{16,24},{24,16},{1,9},{9,1},{17,25},{25,17},{2,10},{10... | collective-permute-start | bytes 473096 | tf_op jit(solution)/shard_map/ppermute | solution.py:72
  416.5 2.6 fusion
  422.4 2.0 reshape.516
  433.2 13.9 %collective-permute-done.42 = bf16[8,24,3072]{2,1,0:T(8,128)(2,1)} collective-permute-done((bf16[8,24,3072]{2,1,0:T(8,128)(2,1)}, bf16[8,24,3072]{2,1,0:T(8,128)(2,1)}, u32[]{:S(2)}, u32[]{:S(2)}) %collective-permute-start.42) | collective-permute-done | bytes 1179680 | tf_op jit(solution)/shard_map/ppermute | solution.py:72
  450.8 11.0 %collective-permute-done.43 = bf16[4,24,3072]{2,1,0:T(8,128)(2,1)S(1)} collective-permute-done((bf16[4,24,3072]{2,1,0:T(8,128)(2,1)S(1)}, bf16[4,24,3072]{2,1,0:T(8,128)(2,1)S(1)}, u32[]{:S(2)}, u32[]{:S(2)}) %collective-permute-start.43) | collective-permute-done | bytes 589856 | tf_op jit(solution)/shard_map/ppermute | solution.py:72
  462.2 5.7 %collective-permute-done.44 = bf16[24,3072]{1,0:T(8,128)(2,1)S(1)} collective-permute-done((bf16[24,3072]{1,0:T(8,128)(2,1)S(1)}, bf16[24,3072]{1,0:T(8,128)(2,1)S(1)}, u32[]{:S(2)}, u32[]{:S(2)}) %collective-permute-start.44) | collective-permute-done | bytes 147488 | tf_op jit(solution)/shard_map/ppermute | solution.py:103
  468.0 4.0 collective-permute-start.59
  472.0 1.7 collective-permute-done.45
  475.3 4.6 collective-permute-done.46
  481.2 3.1 collective-permute-done.47
  484.3 7.1 %collective-permute-start.48 = (bf16[2,24,3072]{2,1,0:T(8,128)(2,1)S(1)}, bf16[2,24,3072]{2,1,0:T(8,128)(2,1)S(1)}, u32[]{:S(2)}, u32[]{:S(2)}) collective-permute-start(bf16[2,24,3072]{2,1,0:T(8,128)(2,1)S(1)} %pad_maximum_fusion.15), channel_id=1, source_target_pairs={{0,8},{8,0},{16,24},{24,16},{1,9},{9,1},{17,25},{25,17},{2,10},{10... | collective-permute-start | bytes 884744 | tf_op jit(solution)/shard_map/ppermute | solution.py:72
  492.7 8.6 %join_gate_up.1 = f32[96,6144]{1,0:T(8,128)} custom-call(bf16[4,96,1536]{2,1,0:T(8,128)(2,1)} %slice.195.pieces_ref), custom_call_target="tpu_custom_call" | custom-call | tf_op jit(solution)/shard_map/join_gate_up/pallas_call | solution.py:56
  (391 shorter events, 128.1 us)
Async XLA Ops:
  7.2 144.9 %all-gather.2.cloned.1.call-start = ((), (), s32[]{:S(2)}) async-start(), calls=%async_computation | async-start | bytes 3981312 | tf_op jit(solution)/shard_map/all_gather | solution.py:661
  11.1 34.1 %collective-permute-start.15 = (bf16[224,256]{1,0:T(8,128)(2,1)S(1)}, bf16[224,256]{1,0:T(8,128)(2,1)S(1)}, u32[]{:S(2)}, u32[]{:S(2)}) collective-permute-start(bf16[224,256]{1,0:T(8,128)(2,1)S(1)} %constant_dynamic-update-slice_fusion.4), channel_id=1, source_target_pairs={{0,2},{1,3},{2,4},{3,5},{4,6},{5,7},{6,0},{7,1},{8,10},{9,11},{10,... | collective-permute-start | bytes 344072 | tf_op jit(solution)/shard_map/ppermute | solution.py:103
  14.2 29.7 %collective-permute-start.9 = (bf16[24,2304]{1,0:T(8,128)(2,1)S(1)}, bf16[24,2304]{1,0:T(8,128)(2,1)S(1)}, u32[]{:S(2)}, u32[]{:S(2)}) collective-permute-start(bf16[24,2304]{1,0:T(8,128)(2,1)S(1)} %get-tuple-element.134), channel_id=1, source_target_pairs={{0,2},{1,3},{2,4},{3,5},{4,6},{5,7},{6,0},{7,1},{8,10},{9,11},{10,... | collective-permute-start | bytes 331784 | tf_op jit(solution)/shard_map/ppermute | solution.py:103
  19.9 6.1 %collective-permute-start = (f32[8,552]{1,0:T(8,128)S(1)}, f32[8,552]{1,0:T(8,128)S(1)}, u32[]{:S(2)}, u32[]{:S(2)}) collective-permute-start(f32[8,552]{1,0:T(8,128)S(1)} %dynamic_update_slice.32), channel_id=1, source_target_pairs={{0,1},{1,0},{2,3},{3,2},{4,5},{5,4},{6,7},{7,6},{8,9},{9,8},{10,11... | collective-permute-start | bytes 53000 | tf_op jit(solution)/shard_map/ppermute | solution.py:72
  28.9 3.5 collective-permute-start.2
  33.2 12.1 %collective-permute-start.3 = (f32[32,768]{1,0:T(8,128)S(1)}, f32[32,768]{1,0:T(8,128)S(1)}, u32[]{:S(2)}, u32[]{:S(2)}) collective-permute-start(f32[32,768]{1,0:T(8,128)S(1)} %convolution_add_fusion), channel_id=1, source_target_pairs={{0,1},{1,0},{2,3},{3,2},{4,5},{5,4},{6,7},{7,6},{8,9},{9,8},{10,11... | collective-permute-start | bytes 294920 | tf_op jit(solution)/shard_map/ppermute | solution.py:72
  43.9 7.4 %collective-permute-start.10 = (bf16[24,2304]{1,0:T(8,128)(2,1)S(1)}, bf16[24,2304]{1,0:T(8,128)(2,1)S(1)}, u32[]{:S(2)}, u32[]{:S(2)}) collective-permute-start(bf16[24,2304]{1,0:T(8,128)(2,1)S(1)} %collective-permute-done.9), channel_id=1, source_target_pairs={{0,2},{1,3},{2,4},{3,5},{4,6},{5,7},{6,0},{7,1},{8,10},{9,11},{10,... | collective-permute-start | bytes 331784 | tf_op jit(solution)/shard_map/ppermute | solution.py:103
  45.2 10.8 %collective-permute-start.16 = (bf16[224,256]{1,0:T(8,128)(2,1)S(1)}, bf16[224,256]{1,0:T(8,128)(2,1)S(1)}, u32[]{:S(2)}, u32[]{:S(2)}) collective-permute-start(bf16[224,256]{1,0:T(8,128)(2,1)S(1)} %collective-permute-done.15), channel_id=1, source_target_pairs={{0,2},{1,3},{2,4},{3,5},{4,6},{5,7},{6,0},{7,1},{8,10},{9,11},{10,... | collective-permute-start | bytes 344072 | tf_op jit(solution)/shard_map/ppermute | solution.py:103
  45.3 11.5 %collective-permute-start.4 = (f32[32,768]{1,0:T(8,128)S(1)}, f32[32,768]{1,0:T(8,128)S(1)}, u32[]{:S(2)}, u32[]{:S(2)}) collective-permute-start(f32[32,768]{1,0:T(8,128)S(1)} %add.321), channel_id=1, source_target_pairs={{0,2},{1,3},{2,0},{3,1},{4,6},{5,7},{6,4},{7,5},{8,10},{9,11},{10,... | collective-permute-start | bytes 294920 | tf_op jit(solution)/shard_map/ppermute | solution.py:72
  51.3 9.5 %collective-permute-start.11 = (bf16[24,2304]{1,0:T(8,128)(2,1)S(1)}, bf16[24,2304]{1,0:T(8,128)(2,1)S(1)}, u32[]{:S(2)}, u32[]{:S(2)}) collective-permute-start(bf16[24,2304]{1,0:T(8,128)(2,1)S(1)} %collective-permute-done.10), channel_id=1, source_target_pairs={{0,2},{1,3},{2,4},{3,5},{4,6},{5,7},{6,0},{7,1},{8,10},{9,11},{10,... | collective-permute-start | bytes 331784 | tf_op jit(solution)/shard_map/ppermute | solution.py:103
  56.0 13.7 %collective-permute-start.17 = (bf16[224,256]{1,0:T(8,128)(2,1)S(1)}, bf16[224,256]{1,0:T(8,128)(2,1)S(1)}, u32[]{:S(2)}, u32[]{:S(2)}) collective-permute-start(bf16[224,256]{1,0:T(8,128)(2,1)S(1)} %collective-permute-done.16), channel_id=1, source_target_pairs={{0,2},{1,3},{2,4},{3,5},{4,6},{5,7},{6,0},{7,1},{8,10},{9,11},{10,... | collective-permute-start | bytes 344072 | tf_op jit(solution)/shard_map/ppermute | solution.py:103
  56.8 11.7 %collective-permute-start.5 = (f32[32,768]{1,0:T(8,128)S(1)}, f32[32,768]{1,0:T(8,128)S(1)}, u32[]{:S(2)}, u32[]{:S(2)}) collective-permute-start(f32[32,768]{1,0:T(8,128)S(1)} %add.322), channel_id=1, source_target_pairs={{0,4},{1,5},{2,6},{3,7},{4,0},{5,1},{6,2},{7,3},{8,12},{9,13},{10,... | collective-permute-start | bytes 294920 | tf_op jit(solution)/shard_map/ppermute | solution.py:72
  60.8 25.1 %collective-permute-start.12 = (bf16[4,24,2304]{2,1,0:T(8,128)(2,1)S(1)}, bf16[4,24,2304]{2,1,0:T(8,128)(2,1)S(1)}, u32[]{:S(2)}, u32[]{:S(2)}) collective-permute-start(bf16[4,24,2304]{2,1,0:T(8,128)(2,1)S(1)} %bitcast_dynamic-update-slice_fusion.4), channel_id=1, source_target_pairs={{0,1},{1,0},{2,3},{3,2},{4,5},{5,4},{6,7},{7,6},{8,9},{9,8},{10,11... | collective-permute-start | bytes 1327112 | tf_op jit(solution)/shard_map/ppermute | solution.py:72
  69.6 16.1 %collective-permute-start.6 = (bf16[4,4,4608]{2,1,0:T(4,128)(2,1)S(1)}, bf16[4,4,4608]{2,1,0:T(4,128)(2,1)S(1)}, u32[]{:S(2)}, u32[]{:S(2)}) collective-permute-start(bf16[4,4,4608]{2,1,0:T(4,128)(2,1)S(1)} %dynamic-slice_bitcast_fusion.10), channel_id=1, source_target_pairs={{0,4},{1,5},{2,6},{3,7},{4,0},{5,1},{6,2},{7,3},{8,12},{9,13},{10,... | collective-permute-start | bytes 442376 | tf_op jit(solution)/shard_map/ppermute | solution.py:72
  69.7 29.6 %collective-permute-start.18 = (bf16[4,224,256]{2,1,0:T(8,128)(2,1)S(1)}, bf16[4,224,256]{2,1,0:T(8,128)(2,1)S(1)}, u32[]{:S(2)}, u32[]{:S(2)}) collective-permute-start(bf16[4,224,256]{2,1,0:T(8,128)(2,1)S(1)} %bitcast_dynamic-update-slice_fusion), channel_id=1, source_target_pairs={{0,1},{1,0},{2,3},{3,2},{4,5},{5,4},{6,7},{7,6},{8,9},{9,8},{10,11... | collective-permute-start | bytes 1376264 | tf_op jit(solution)/shard_map/ppermute | solution.py:72
  85.8 6.6 %collective-permute-start.7 = (bf16[2,4,4608]{2,1,0:T(4,128)(2,1)S(1)}, bf16[2,4,4608]{2,1,0:T(4,128)(2,1)S(1)}, u32[]{:S(2)}, u32[]{:S(2)}) collective-permute-start(bf16[2,4,4608]{2,1,0:T(4,128)(2,1)S(1)} %dynamic-slice_bitcast_fusion.13), channel_id=1, source_target_pairs={{0,2},{1,3},{2,0},{3,1},{4,6},{5,7},{6,4},{7,5},{8,10},{9,11},{10,... | collective-permute-start | bytes 221192 | tf_op jit(solution)/shard_map/ppermute | solution.py:72
  86.1 16.6 %collective-permute-start.13 = (bf16[8,24,2304]{2,1,0:T(8,128)(2,1)S(1)}, bf16[8,24,2304]{2,1,0:T(8,128)(2,1)S(1)}, u32[]{:S(2)}, u32[]{:S(2)}) collective-permute-start(bf16[8,24,2304]{2,1,0:T(8,128)(2,1)S(1)} %bitcast.432), channel_id=1, source_target_pairs={{0,16},{8,24},{16,0},{24,8},{1,17},{9,25},{17,1},{25,9},{2,18},{10... | collective-permute-start | bytes 2654216 | tf_op jit(solution)/shard_map/ppermute | solution.py:72
  99.5 22.8 %collective-permute-start.19 = (bf16[8,224,256]{2,1,0:T(8,128)(2,1)S(1)}, bf16[8,224,256]{2,1,0:T(8,128)(2,1)S(1)}, u32[]{:S(2)}, u32[]{:S(2)}) collective-permute-start(bf16[8,224,256]{2,1,0:T(8,128)(2,1)S(1)} %bitcast.431), channel_id=1, source_target_pairs={{0,16},{8,24},{16,0},{24,8},{1,17},{9,25},{17,1},{25,9},{2,18},{10... | collective-permute-start | bytes 2752520 | tf_op jit(solution)/shard_map/ppermute | solution.py:72
  103.0 25.9 %collective-permute-start.14 = (bf16[8,2,24,2304]{3,2,1,0:T(8,128)(2,1)S(1)}, bf16[8,2,24,2304]{3,2,1,0:T(8,128)(2,1)S(1)}, u32[]{:S(2)}, u32[]{:S(2)}) collective-permute-start(bf16[8,2,24,2304]{3,2,1,0:T(8,128)(2,1)S(1)} %pad_maximum_fusion.4), channel_id=1, source_target_pairs={{0,8},{8,0},{16,24},{24,16},{1,9},{9,1},{17,25},{25,17},{2,10},{10... | collective-permute-start | bytes 5308424 | tf_op jit(solution)/shard_map/ppermute | solution.py:72
  113.8 14.5 %collective-permute-start.8 = (bf16[1,4,4608]{2,1,0:T(4,128)(2,1)S(1)}, bf16[1,4,4608]{2,1,0:T(4,128)(2,1)S(1)}, u32[]{:S(2)}, u32[]{:S(2)}) collective-permute-start(bf16[1,4,4608]{2,1,0:T(4,128)(2,1)S(1)} %constant_dynamic-slice_fusion.6), channel_id=1, source_target_pairs={{0,1},{1,0},{2,3},{3,2},{4,5},{5,4},{6,7},{7,6},{8,9},{9,8},{10,11... | collective-permute-start | bytes 110600 | tf_op jit(solution)/shard_map/ppermute | solution.py:72
  122.6 9.1 %collective-permute-start.20 = (bf16[8,2,224,256]{3,2,0,1:T(8,128)(2,1)S(1)}, bf16[8,2,224,256]{3,2,0,1:T(8,128)(2,1)S(1)}, u32[]{:S(2)}, u32[]{:S(2)}) collective-permute-start(bf16[8,2,224,256]{3,2,0,1:T(8,128)(2,1)S(1)} %pad_maximum_fusion.3), channel_id=1, source_target_pairs={{0,8},{8,0},{16,24},{24,16},{1,9},{9,1},{17,25},{25,17},{2,10},{10... | collective-permute-start | bytes 5505032 | tf_op jit(solution)/shard_map/ppermute | solution.py:72
  142.2 6.3 %collective-permute-start.21 = (bf16[128,768]{1,0:T(8,128)(2,1)}, bf16[128,768]{1,0:T(8,128)(2,1)S(1)}, u32[]{:S(2)}, u32[]{:S(2)}) collective-permute-start(bf16[128,768]{1,0:T(8,128)(2,1)} %get-tuple-element.65), channel_id=1, source_target_pairs={{0,16},{8,24},{16,0},{24,8},{1,17},{9,25},{17,1},{25,9},{2,18},{10... | collective-permute-start | bytes 589832 | tf_op jit(solution)/shard_map/ppermute | solution.py:72
  161.7 13.1 %collective-permute-start.24 = (bf16[128,768]{1,0:T(8,128)(2,1)S(1)}, bf16[128,768]{1,0:T(8,128)(2,1)S(1)}, u32[]{:S(2)}, u32[]{:S(2)}) collective-permute-start(bf16[128,768]{1,0:T(8,128)(2,1)S(1)} %slice.233), channel_id=1, source_target_pairs={{0,16},{8,24},{16,0},{24,8},{1,17},{9,25},{17,1},{25,9},{2,18},{10... | collective-permute-start | bytes 589832 | tf_op jit(solution)/shard_map/ppermute | solution.py:72
  163.3 56.0 %collective-permute-start.29 = (f32[1,32,98]{2,1,0:T(8,128)S(1)}, f32[1,32,98]{2,1,0:T(8,128)S(1)}, u32[]{:S(2)}, u32[]{:S(2)}) collective-permute-start(f32[1,32,98]{2,1,0:T(8,128)S(1)} %maximum_bitcast_fusion.4), channel_id=1, source_target_pairs={{0,8},{8,0},{16,24},{24,16},{1,9},{9,1},{17,25},{25,17},{2,10},{10... | collective-permute-start | bytes 37640 | tf_op jit(solution)/shard_map/ppermute | solution.py:72
  219.3 6.5 %collective-permute-start.25 = (bf16[128,768]{1,0:T(8,128)(2,1)}, bf16[128,768]{1,0:T(8,128)(2,1)S(1)}, u32[]{:S(2)}, u32[]{:S(2)}) collective-permute-start(bf16[128,768]{1,0:T(8,128)(2,1)} %get-tuple-element.76), channel_id=1, source_target_pairs={{0,16},{8,24},{16,0},{24,8},{1,17},{9,25},{17,1},{25,9},{2,18},{10... | collective-permute-start | bytes 589832 | tf_op jit(solution)/shard_map/ppermute | solution.py:72
  219.4 8.8 %collective-permute-start.30 = (f32[2,32,98]{2,1,0:T(8,128)S(1)}, f32[2,32,98]{2,1,0:T(8,128)S(1)}, u32[]{:S(2)}, u32[]{:S(2)}) collective-permute-start(f32[2,32,98]{2,1,0:T(8,128)S(1)} %maximum_bitcast_fusion.3), channel_id=1, source_target_pairs={{0,16},{8,24},{16,0},{24,8},{1,17},{9,25},{17,1},{25,9},{2,18},{10... | collective-permute-start | bytes 75272 | tf_op jit(solution)/shard_map/ppermute | solution.py:72
  226.7 2.8 collective-permute-start.26
  237.3 16.7 %collective-permute-start.27 = (bf16[256,768]{1,0:T(8,128)(2,1)}, bf16[256,768]{1,0:T(8,128)(2,1)}, u32[]{:S(2)}, u32[]{:S(2)}) collective-permute-start(bf16[256,768]{1,0:T(8,128)(2,1)} %get-tuple-element.80), channel_id=1, source_target_pairs={{0,8},{8,0},{16,24},{24,16},{1,9},{9,1},{17,25},{25,17},{2,10},{10... | collective-permute-start | bytes 1179656 | tf_op jit(solution)/shard_map/ppermute | solution.py:72
  253.9 107.4 %collective-permute-start.60 = (bf16[8,2,154,256]{3,0,2,1:T(8,128)(2,1)}, bf16[8,2,154,256]{3,0,2,1:T(8,128)(2,1)}, u32[]{:S(2)}, u32[]{:S(2)}) collective-permute-start(bf16[8,2,154,256]{3,0,2,1:T(8,128)(2,1)} %dynamic-slice_bitcast_fusion.2), channel_id=1, source_target_pairs={{0,8},{8,0},{16,24},{24,16},{1,9},{9,1},{17,25},{25,17},{2,10},{10... | collective-permute-start | bytes 3784712 | tf_op jit(solution)/shard_map/ppermute | solution.py:72
  255.5 6.8 %collective-permute-start.28 = (bf16[128,768]{1,0:T(8,128)(2,1)S(1)}, bf16[128,768]{1,0:T(8,128)(2,1)S(1)}, u32[]{:S(2)}, u32[]{:S(2)}) collective-permute-start(bf16[128,768]{1,0:T(8,128)(2,1)S(1)} %slice.232), channel_id=1, source_target_pairs={{0,16},{8,24},{16,0},{24,8},{1,17},{9,25},{17,1},{25,9},{2,18},{10... | collective-permute-start | bytes 589832 | tf_op jit(solution)/shard_map/ppermute | solution.py:72
  284.0 5.2 %collective-permute-start.49 = (f32[13,256]{1,0:T(8,128)S(1)}, f32[13,256]{1,0:T(8,128)S(1)}, u32[]{:S(2)}, u32[]{:S(2)}) collective-permute-start(f32[13,256]{1,0:T(8,128)S(1)} %pad_maximum_fusion.23), channel_id=1, source_target_pairs={{0,8},{8,0},{16,24},{24,16},{1,9},{9,1},{17,25},{25,17},{2,10},{10... | collective-permute-start | bytes 39944 | tf_op jit(solution)/shard_map/ppermute | solution.py:72
  284.6 15.1 %collective-permute-start.31 = (bf16[1,4,4608]{2,1,0:T(4,128)(2,1)S(1)}, bf16[1,4,4608]{2,1,0:T(4,128)(2,1)S(1)}, u32[]{:S(2)}, u32[]{:S(2)}) collective-permute-start(bf16[1,4,4608]{2,1,0:T(4,128)(2,1)S(1)} %pad_maximum_fusion.21), channel_id=1, source_target_pairs={{0,1},{1,0},{2,3},{3,2},{4,5},{5,4},{6,7},{7,6},{8,9},{9,8},{10,11... | collective-permute-start | bytes 110600 | tf_op jit(solution)/shard_map/ppermute | solution.py:72
  290.0 8.9 %collective-permute-start.50 = (f32[13,256]{1,0:T(8,128)S(1)}, f32[13,256]{1,0:T(8,128)S(1)}, u32[]{:S(2)}, u32[]{:S(2)}) collective-permute-start(f32[13,256]{1,0:T(8,128)S(1)} %fusion.71), channel_id=1, source_target_pairs={{0,16},{8,24},{16,0},{24,8},{1,17},{9,25},{17,1},{25,9},{2,18},{10... | collective-permute-start | bytes 39944 | tf_op jit(solution)/shard_map/ppermute | solution.py:72
  291.5 106.4 %collective-permute-start.54 = (bf16[4,96,2304]{2,1,0:T(8,128)(2,1)}, bf16[4,96,2304]{2,1,0:T(8,128)(2,1)}, u32[]{:S(2)}, u32[]{:S(2)}) collective-permute-start(bf16[4,96,2304]{2,1,0:T(8,128)(2,1)} %dynamic-slice_bitcast_fusion.1), channel_id=1, source_target_pairs={{0,1},{1,0},{2,3},{3,2},{4,5},{5,4},{6,7},{7,6},{8,9},{9,8},{10,11... | collective-permute-start | bytes 5308424 | tf_op jit(solution)/shard_map/ppermute | solution.py:72
  298.9 32.9 %collective-permute-start.51 = (f32[13,256]{1,0:T(8,128)S(1)}, f32[13,256]{1,0:T(8,128)S(1)}, u32[]{:S(2)}, u32[]{:S(2)}) collective-permute-start(f32[13,256]{1,0:T(8,128)S(1)} %add.366), channel_id=1, source_target_pairs={{0,1},{1,0},{2,3},{3,2},{4,5},{5,4},{6,7},{7,6},{8,9},{9,8},{10,11... | collective-permute-start | bytes 39944 | tf_op jit(solution)/shard_map/ppermute | solution.py:72
  299.8 32.0 %collective-permute-start.32 = (bf16[2,4,4608]{2,1,0:T(4,128)(2,1)S(1)}, bf16[2,4,4608]{2,1,0:T(4,128)(2,1)S(1)}, u32[]{:S(2)}, u32[]{:S(2)}) collective-permute-start(bf16[2,4,4608]{2,1,0:T(4,128)(2,1)S(1)} %maximum_bitcast_fusion.2), channel_id=1, source_target_pairs={{0,2},{1,3},{2,0},{3,1},{4,6},{5,7},{6,4},{7,5},{8,10},{9,11},{10,... | collective-permute-start | bytes 221192 | tf_op jit(solution)/shard_map/ppermute | solution.py:72
  331.8 5.5 %collective-permute-start.52 = (f32[13,256]{1,0:T(8,128)S(1)}, f32[13,256]{1,0:T(8,128)S(1)}, u32[]{:S(2)}, u32[]{:S(2)}) collective-permute-start(f32[13,256]{1,0:T(8,128)S(1)} %add.367), channel_id=1, source_target_pairs={{0,2},{1,3},{2,0},{3,1},{4,6},{5,7},{6,4},{7,5},{8,10},{9,11},{10,... | collective-permute-start | bytes 39944 | tf_op jit(solution)/shard_map/ppermute | solution.py:72
  332.0 8.8 %collective-permute-start.33 = (bf16[4,4,4608]{2,1,0:T(4,128)(2,1)S(1)}, bf16[4,4,4608]{2,1,0:T(4,128)(2,1)S(1)}, u32[]{:S(2)}, u32[]{:S(2)}) collective-permute-start(bf16[4,4,4608]{2,1,0:T(4,128)(2,1)S(1)} %bitcast.454), channel_id=1, source_target_pairs={{0,4},{1,5},{2,6},{3,7},{4,0},{5,1},{6,2},{7,3},{8,12},{9,13},{10,... | collective-permute-start | bytes 442376 | tf_op jit(solution)/shard_map/ppermute | solution.py:72
  335.4 81.0 %collective-permute-start.41 = (bf16[8,2,24,3072]{3,2,1,0:T(8,128)(2,1)}, bf16[8,2,24,3072]{3,2,1,0:T(8,128)(2,1)}, u32[]{:S(2)}, u32[]{:S(2)}) collective-permute-start(bf16[8,2,24,3072]{3,2,1,0:T(8,128)(2,1)} %dynamic-slice_bitcast_fusion), channel_id=1, source_target_pairs={{0,8},{8,0},{16,24},{24,16},{1,9},{9,1},{17,25},{25,17},{2,10},{10... | collective-permute-start | bytes 7077896 | tf_op jit(solution)/shard_map/ppermute | solution.py:72
  337.3 9.8 %collective-permute-start.53 = (f32[13,256]{1,0:T(8,128)S(1)}, f32[13,256]{1,0:T(8,128)S(1)}, u32[]{:S(2)}, u32[]{:S(2)}) collective-permute-start(f32[13,256]{1,0:T(8,128)S(1)} %add.368), channel_id=1, source_target_pairs={{0,4},{1,5},{2,6},{3,7},{4,0},{5,1},{6,2},{7,3},{8,12},{9,13},{10,... | collective-permute-start | bytes 39944 | tf_op jit(solution)/shard_map/ppermute | solution.py:72
  351.9 3.8 collective-permute-start.36
  355.9 7.0 %collective-permute-start.37 = (bf16[1,32,768]{2,1,0:T(8,128)(2,1)S(1)}, bf16[1,32,768]{2,1,0:T(8,128)(2,1)S(1)}, u32[]{:S(2)}, u32[]{:S(2)}) collective-permute-start(bf16[1,32,768]{2,1,0:T(8,128)(2,1)S(1)} %broadcast_in_dim_reshape.3), channel_id=1, source_target_pairs={{0,8},{8,0},{16,24},{24,16},{1,9},{9,1},{17,25},{25,17},{2,10},{10... | collective-permute-start | bytes 147464 | tf_op jit(solution)/shard_map/ppermute | solution.py:72
  363.0 4.6 collective-permute-start.38
  364.3 16.7 %collective-permute-start.61 = (bf16[8,154,256]{2,0,1:T(8,128)(2,1)S(1)}, bf16[8,154,256]{2,0,1:T(8,128)(2,1)S(1)}, u32[]{:S(2)}, u32[]{:S(2)}) collective-permute-start(bf16[8,154,256]{2,0,1:T(8,128)(2,1)S(1)} %dynamic-slice_bitcast_fusion.4), channel_id=1, source_target_pairs={{0,16},{8,24},{16,0},{24,8},{1,17},{9,25},{17,1},{25,9},{2,18},{10... | collective-permute-start | bytes 1892360 | tf_op jit(solution)/shard_map/ppermute | solution.py:72
  365.3 4.4 collective-permute-start.39
  381.4 8.5 %collective-permute-start.62 = (bf16[4,154,256]{2,1,0:T(8,128)(2,1)S(1)}, bf16[4,154,256]{2,1,0:T(8,128)(2,1)S(1)}, u32[]{:S(2)}, u32[]{:S(2)}) collective-permute-start(bf16[4,154,256]{2,1,0:T(8,128)(2,1)S(1)} %dynamic-slice_bitcast_fusion.7), channel_id=1, source_target_pairs={{0,1},{1,0},{2,3},{3,2},{4,5},{5,4},{6,7},{7,6},{8,9},{9,8},{10,11... | collective-permute-start | bytes 946184 | tf_op jit(solution)/shard_map/ppermute | solution.py:72
  382.2 13.8 %collective-permute-start.40 = (bf16[2,32,4608]{2,1,0:T(8,128)(2,1)S(1)}, bf16[2,32,4608]{2,1,0:T(8,128)(2,1)S(1)}, u32[]{:S(2)}, u32[]{:S(2)}) collective-permute-start(bf16[2,32,4608]{2,1,0:T(8,128)(2,1)S(1)} %maximum_bitcast_fusion), channel_id=1, source_target_pairs={{0,16},{8,24},{16,0},{24,8},{1,17},{9,25},{17,1},{25,9},{2,18},{10... | collective-permute-start | bytes 1769480 | tf_op jit(solution)/shard_map/ppermute | solution.py:72
  390.0 5.1 %collective-permute-start.63 = (bf16[154,256]{1,0:T(8,128)(2,1)S(1)}, bf16[154,256]{1,0:T(8,128)(2,1)S(1)}, u32[]{:S(2)}, u32[]{:S(2)}) collective-permute-start(bf16[154,256]{1,0:T(8,128)(2,1)S(1)} %dynamic-slice_bitcast_fusion.12), channel_id=1, source_target_pairs={{0,2},{1,3},{2,4},{3,5},{4,6},{5,7},{6,0},{7,1},{8,10},{9,11},{10,... | collective-permute-start | bytes 236552 | tf_op jit(solution)/shard_map/ppermute | solution.py:103
  395.2 5.7 %collective-permute-start.64 = (bf16[154,256]{1,0:T(8,128)(2,1)S(1)}, bf16[154,256]{1,0:T(8,128)(2,1)S(1)}, u32[]{:S(2)}, u32[]{:S(2)}) collective-permute-start(bf16[154,256]{1,0:T(8,128)(2,1)S(1)} %fusion.19), channel_id=1, source_target_pairs={{0,2},{1,3},{2,4},{3,5},{4,6},{5,7},{6,0},{7,1},{8,10},{9,11},{10,... | collective-permute-start | bytes 236552 | tf_op jit(solution)/shard_map/ppermute | solution.py:103
  401.0 5.1 %collective-permute-start.65 = (bf16[154,256]{1,0:T(8,128)(2,1)S(1)}, bf16[154,256]{1,0:T(8,128)(2,1)S(1)}, u32[]{:S(2)}, u32[]{:S(2)}) collective-permute-start(bf16[154,256]{1,0:T(8,128)(2,1)S(1)} %fusion.18), channel_id=1, source_target_pairs={{0,2},{1,3},{2,4},{3,5},{4,6},{5,7},{6,0},{7,1},{8,10},{9,11},{10,... | collective-permute-start | bytes 236552 | tf_op jit(solution)/shard_map/ppermute | solution.py:103
  401.1 15.1 %collective-permute-start.55 = (bf16[96,2304]{1,0:T(8,128)(2,1)S(1)}, bf16[96,2304]{1,0:T(8,128)(2,1)S(1)}, u32[]{:S(2)}, u32[]{:S(2)}) collective-permute-start(bf16[96,2304]{1,0:T(8,128)(2,1)S(1)} %dynamic-slice_bitcast_fusion.6), channel_id=1, source_target_pairs={{0,2},{1,3},{2,4},{3,5},{4,6},{5,7},{6,0},{7,1},{8,10},{9,11},{10,... | collective-permute-start | bytes 1327112 | tf_op jit(solution)/shard_map/ppermute | solution.py:103
  406.2 3.7 collective-permute-start.66
  409.9 11.5 %collective-permute-start.67 = (bf16[2,154,256]{2,1,0:T(8,128)(2,1)S(1)}, bf16[2,154,256]{2,1,0:T(8,128)(2,1)S(1)}, u32[]{:S(2)}, u32[]{:S(2)}) collective-permute-start(bf16[2,154,256]{2,1,0:T(8,128)(2,1)S(1)} %pad_maximum_fusion.17), channel_id=1, source_target_pairs={{0,8},{8,0},{16,24},{24,16},{1,9},{9,1},{17,25},{25,17},{2,10},{10... | collective-permute-start | bytes 473096 | tf_op jit(solution)/shard_map/ppermute | solution.py:72
  416.3 15.6 %collective-permute-start.56 = (bf16[96,2304]{1,0:T(8,128)(2,1)S(1)}, bf16[96,2304]{1,0:T(8,128)(2,1)}, u32[]{:S(2)}, u32[]{:S(2)}) collective-permute-start(bf16[96,2304]{1,0:T(8,128)(2,1)S(1)} %fusion.11), channel_id=1, source_target_pairs={{0,2},{1,3},{2,4},{3,5},{4,6},{5,7},{6,0},{7,1},{8,10},{9,11},{10,... | collective-permute-start | bytes 1327112 | tf_op jit(solution)/shard_map/ppermute | solution.py:103
  420.2 26.9 %collective-permute-start.42 = (bf16[8,24,3072]{2,1,0:T(8,128)(2,1)}, bf16[8,24,3072]{2,1,0:T(8,128)(2,1)}, u32[]{:S(2)}, u32[]{:S(2)}) collective-permute-start(bf16[8,24,3072]{2,1,0:T(8,128)(2,1)} %dynamic-slice_bitcast_fusion.3), channel_id=1, source_target_pairs={{0,16},{8,24},{16,0},{24,8},{1,17},{9,25},{17,1},{25,9},{2,18},{10... | collective-permute-start | bytes 3538952 | tf_op jit(solution)/shard_map/ppermute | solution.py:72
  433.1 16.3 %collective-permute-start.57 = (bf16[96,2304]{1,0:T(8,128)(2,1)S(1)}, bf16[96,2304]{1,0:T(8,128)(2,1)S(1)}, u32[]{:S(2)}, u32[]{:S(2)}) collective-permute-start(bf16[96,2304]{1,0:T(8,128)(2,1)S(1)} %fusion.10), channel_id=1, source_target_pairs={{0,2},{1,3},{2,4},{3,5},{4,6},{5,7},{6,0},{7,1},{8,10},{9,11},{10,... | collective-permute-start | bytes 1327112 | tf_op jit(solution)/shard_map/ppermute | solution.py:103
  448.8 13.0 %collective-permute-start.43 = (bf16[4,24,3072]{2,1,0:T(8,128)(2,1)S(1)}, bf16[4,24,3072]{2,1,0:T(8,128)(2,1)S(1)}, u32[]{:S(2)}, u32[]{:S(2)}) collective-permute-start(bf16[4,24,3072]{2,1,0:T(8,128)(2,1)S(1)} %dynamic-slice_bitcast_fusion.5), channel_id=1, source_target_pairs={{0,1},{1,0},{2,3},{3,2},{4,5},{5,4},{6,7},{7,6},{8,9},{9,8},{10,11... | collective-permute-start | bytes 1769480 | tf_op jit(solution)/shard_map/ppermute | solution.py:72
  449.5 12.6 %collective-permute-start.58 = (bf16[96,2304]{1,0:T(8,128)(2,1)S(1)}, bf16[96,2304]{1,0:T(8,128)(2,1)S(1)}, u32[]{:S(2)}, u32[]{:S(2)}) collective-permute-start(bf16[96,2304]{1,0:T(8,128)(2,1)S(1)} %fusion.9), channel_id=1, source_target_pairs={{0,16},{8,24},{16,0},{24,8},{1,17},{9,25},{17,1},{25,9},{2,18},{10... | collective-permute-start | bytes 1327112 | tf_op jit(solution)/shard_map/ppermute | solution.py:72
  462.0 5.8 %collective-permute-start.44 = (bf16[24,3072]{1,0:T(8,128)(2,1)S(1)}, bf16[24,3072]{1,0:T(8,128)(2,1)S(1)}, u32[]{:S(2)}, u32[]{:S(2)}) collective-permute-start(bf16[24,3072]{1,0:T(8,128)(2,1)S(1)} %dynamic-slice_bitcast_fusion.8), channel_id=1, source_target_pairs={{0,2},{1,3},{2,4},{3,5},{4,6},{5,7},{6,0},{7,1},{8,10},{9,11},{10,... | collective-permute-start | bytes 442376 | tf_op jit(solution)/shard_map/ppermute | solution.py:103
  467.9 5.8 %collective-permute-start.45 = (bf16[24,3072]{1,0:T(8,128)(2,1)S(1)}, bf16[24,3072]{1,0:T(8,128)(2,1)S(1)}, u32[]{:S(2)}, u32[]{:S(2)}) collective-permute-start(bf16[24,3072]{1,0:T(8,128)(2,1)S(1)} %fusion.15), channel_id=1, source_target_pairs={{0,2},{1,3},{2,4},{3,5},{4,6},{5,7},{6,0},{7,1},{8,10},{9,11},{10,... | collective-permute-start | bytes 442376 | tf_op jit(solution)/shard_map/ppermute | solution.py:103
  468.0 13.0 %collective-permute-start.59 = (bf16[2,96,2304]{2,1,0:T(8,128)(2,1)S(1)}, bf16[2,96,2304]{2,1,0:T(8,128)(2,1)S(1)}, u32[]{:S(2)}, u32[]{:S(2)}) collective-permute-start(bf16[2,96,2304]{2,1,0:T(8,128)(2,1)S(1)} %pad_maximum_fusion.9), channel_id=1, source_target_pairs={{0,8},{8,0},{16,24},{24,16},{1,9},{9,1},{17,25},{25,17},{2,10},{10... | collective-permute-start | bytes 2654216 | tf_op jit(solution)/shard_map/ppermute | solution.py:72
  473.8 6.1 %collective-permute-start.46 = (bf16[24,3072]{1,0:T(8,128)(2,1)S(1)}, bf16[24,3072]{1,0:T(8,128)(2,1)S(1)}, u32[]{:S(2)}, u32[]{:S(2)}) collective-permute-start(bf16[24,3072]{1,0:T(8,128)(2,1)S(1)} %fusion.14), channel_id=1, source_target_pairs={{0,2},{1,3},{2,4},{3,5},{4,6},{5,7},{6,0},{7,1},{8,10},{9,11},{10,... | collective-permute-start | bytes 442376 | tf_op jit(solution)/shard_map/ppermute | solution.py:103
  479.9 4.4 collective-permute-start.47
  484.3 18.2 %collective-permute-start.48 = (bf16[2,24,3072]{2,1,0:T(8,128)(2,1)S(1)}, bf16[2,24,3072]{2,1,0:T(8,128)(2,1)S(1)}, u32[]{:S(2)}, u32[]{:S(2)}) collective-permute-start(bf16[2,24,3072]{2,1,0:T(8,128)(2,1)S(1)} %pad_maximum_fusion.15), channel_id=1, source_target_pairs={{0,8},{8,0},{16,24},{24,16},{1,9},{9,1},{17,25},{25,17},{2,10},{10... | collective-permute-start | bytes 884744 | tf_op jit(solution)/shard_map/ppermute | solution.py:72
  (37 other events, 342.5 us)
Sparse Core Ops, SparseCore 0:
  26.2 84.5 all-gather.1
where the time goes:
time: 519 us; the launch traced here: 512 us
  waiting for transfers between devices  180 us (35%)
  Pallas kernels  112 us (22%)
  starting transfers between devices  89.9 us (17%)
  local copies, waits for them, and re-layouts  74.9 us (14%)
  other arithmetic  31.3 us (6%)
  between operations  15.9 us (3%)
  matrix products  8.01 us (2%)
    ppermute x53, waiting for transfers between devices, swap(): return lax.ppermute(values, axis, [(i, i ^ bit) for i in range(size)])  148 us
    ppermute x53, starting transfers between devices, swap(): return lax.ppermute(values, axis, [(i, i ^ bit) for i in range(size)])  83.7 us
    pallas_call x9, Pallas kernels, call_whole(): pl.pallas_call(kernel, grid=(1,), name=name, in_specs=specs, out_specs=[w...  45.9 us
    pallas_call x1, Pallas kernels, on_device(): pl.pallas_call(pair_kernel, name='pairs', grid=(chains, length // count),...  37.8 us
    ppermute x15, waiting for transfers between devices, shift_ring(): lax.ppermute(values, 'fsdp', [(i, (i + 2) % self.n_f) for i in range(self...  31.9 us
    unnamed x80, local copies, waits for them, and re-layouts  10.8 us
  transfers between devices with their start and end apart: 69, of which 36 were waited for; matrix products, arithmetic and copies ran while one was open for 20% of the time, Pallas kernels for 19%

commit v1 on v0

v1 whole, which is shorter than its diff:
```python
import functools
import math

import jax
import jax.numpy as jnp
from jax import lax
from jax.experimental import pallas as pl
from jax.experimental.pallas import tpu as pltpu
from jax.sharding import PartitionSpec as P

EPSILON = 1e-05
F32 = jnp.float32
BF16 = jnp.bfloat16
VMEM_LIMIT = 56 * 1024 * 1024


def norm_parts(values):
    center = values - jnp.mean(values, -1, keepdims=True)
    inverse = lax.rsqrt(jnp.mean(center * center, -1, keepdims=True) + EPSILON)
    return center * inverse, inverse


def norm_back(normed, inverse, upstream):
    return inverse * (
        upstream
        - jnp.mean(upstream, -1, keepdims=True)
        - normed * jnp.mean(upstream * normed, -1, keepdims=True)
    )


def dot(left, right):
    return jnp.dot(left, right, preferred_element_type=F32)


def dot_nt(left, right):
    return lax.dot_general(left, right, (((1,), (1,)), ((), ())), preferred_element_type=F32)


def dot_tn(left, right):
    return lax.dot_general(left, right, (((0,), (0,)), ((), ())), preferred_element_type=F32)


def params():
    return pltpu.CompilerParams(vmem_limit_bytes=VMEM_LIMIT)


def cost(micros):
    return pl.CostEstimate(flops=int(micros * 1e9), bytes_accessed=0, transcendentals=0)


def whole(shape):
    return pl.BlockSpec(shape, lambda *_: (0,) * len(shape))


SMEM = pl.BlockSpec(memory_space=pltpu.SMEM)


def call_whole(kernel, name, micros, outs, *operands, blocks=None, scratch=()):
    blocks = blocks or {}
    specs = [
        blocks.get(i, SMEM if a.dtype == jnp.int32 else whole(a.shape))
        for i, a in enumerate(operands)
    ]
    return pl.pallas_call(
        kernel,
        grid=(1,),
        name=name,
        in_specs=specs,
        out_specs=[whole(o.shape) for o in outs],
        out_shape=outs,
        scratch_shapes=list(scratch),
        cost_estimate=cost(micros),
        compiler_params=params(),
    )(*operands)


def struct(shape, dtype):
    return jax.ShapeDtypeStruct(shape, dtype)


def swap(values, axis, size, bit):
    return lax.ppermute(values, axis, [(i, i ^ bit) for i in range(size)])


def pick(values, index, axis):
    return lax.dynamic_index_in_dim(values, index, axis, keepdims=False)


def ordered(bit, own, other, axis):
    first = jnp.where(bit == 0, own, other)
    second = jnp.where(bit == 0, other, own)
    return jnp.stack([first, second], axis)


class Place:
    def __init__(self, n_dp, n_f):
        self.n_dp, self.n_f, self.ring = n_dp, n_f, n_f // 2
        self.d = lax.axis_index("dp")
        self.f = lax.axis_index("fsdp")
        self.core, self.x = self.d % 2, self.d // 2
        self.y, self.r = self.f % 2, self.f // 2
        self.ints = jnp.stack([self.d, self.f]).astype(jnp.int32)

    def swap_core(self, values):
        return swap(values, "dp", self.n_dp, 1)

    def swap_x(self, values):
        return swap(values, "dp", self.n_dp, 2)

    def swap_y(self, values):
        return swap(values, "fsdp", self.n_f, 1)

    def shift_ring(self, values):
        return lax.ppermute(
            values, "fsdp", [(i, (i + 2) % self.n_f) for i in range(self.n_f)]
        )

    def to_each_f(self, values):
        return lax.all_to_all(values, "fsdp", split_axis=0, concat_axis=0, tiled=True)

    def to_all_f(self, values):
        return self.to_each_f(jnp.broadcast_to(values[None], (self.n_f,) + values.shape))


    def gather_f(self, shard):
        ring = self.ring
        pieces, moving = [], shard
        for k in range(ring):
            moves = [(self.swap_y, moving)]
            if k < ring - 1:
                moves.append((self.shift_ring, moving))
            got = yield moves
            pieces += [moving, got[0]]
            if k < ring - 1:
                moving = got[1]
        return self.assemble(pieces, 2)

    def gather_all(self, shard):
        ring = self.ring
        rows, width = shard.shape
        halves = lax.dynamic_slice_in_dim(shard, self.core * (width // 2), width // 2, 1)
        halves = halves.reshape(2, rows // 2, width // 2)
        moving, last, pieces = pick(halves, self.x, 0), None, []
        for k in range(ring + 1):
            moves = []
            if k < ring:
                moves.append((self.swap_y, moving))
            if k < ring - 1:
                moves.append((self.shift_ring, moving))
            if k > 0:
                moves.append((self.swap_x, last[1] if k == 1 else jnp.stack(last)))
            got = yield moves
            if k > 0:
                pieces += last
                pieces += [pick(halves, 1 - self.x, 0), got[-1]] if k == 1 else [got[-1]]
            if k < ring:
                last = [moving, got[0]]
            if k < ring - 1:
                moving = got[1]
        held = self.assemble(pieces, 4).reshape(self.n_f * rows, width // 2)
        (other,) = yield [(self.swap_core, held)]
        return held, other

    def assemble(self, pieces, per_step):
        block = pieces[0].shape
        lead = (self.ring, 2) if per_step == 2 else (self.ring, 2, 2)
        (held,) = call_whole(
            functools.partial(assemble_kernel, self.ring, per_step),
            "assemble",
            3.0,
            [struct(lead + block, pieces[0].dtype)],
            self.ints,
            *pieces,
        )
        return held.reshape((self.n_f,) + lead[2:] + block)

    def add(self, keep, got):
        return (keep.astype(F32) + got.astype(F32)).astype(BF16)

    def chunks(self, values):
        give, keep = [], []
        values = values.reshape((self.ring, 2) + values.shape[1:])
        for k in range(self.ring):
            chunk = pick(values, (self.r - 1 - k) % self.ring, 0)
            give.append(pick(chunk, 1 - self.y, 0))
            keep.append(pick(chunk, self.y, 0))
        return give, keep

    def reduce_f(self, give, keep):
        moving = None
        for k in range(self.ring):
            moves = [(self.swap_y, give[k])]
            if k > 0:
                moves.append((self.shift_ring, moving))
            got = yield moves
            total = keep[k].astype(F32)
            for other in got:
                total = total + other.astype(F32)
            moving = total.astype(BF16)
        return (yield from self.spread_d(moving))

    def reduce_x(self, mine, across):
        ring = self.ring
        got = yield [
            (self.swap_x, self.add(pick(mine, 1 - self.x, 1), pick(across, 1 - self.x, 1)))
        ]
        values = (
            pick(mine, self.x, 1).astype(F32)
            + pick(across, self.x, 1).astype(F32)
            + got[0].astype(F32)
        ).astype(BF16)
        values = values.reshape((ring, 2) + values.shape[1:])
        got = yield [(self.swap_y, pick(values, 1 - self.y, 1))]
        values = self.add(pick(values, self.y, 1), got[0])
        moving = pick(values, (self.r - 1) % ring, 0)
        for k in range(1, ring):
            got = yield [(self.shift_ring, moving)]
            moving = self.add(pick(values, (self.r - 1 - k) % ring, 0), got[0])
        return (yield from self.spread_d(moving))

    def spread_d(self, values):
        other, across = yield [(self.swap_x, values), (self.swap_core, values)]
        (both,) = yield [(self.swap_core, other)]
        return values, across, other, both

    def sum_everywhere(self, values):
        for axis, size in (("dp", self.n_dp), ("fsdp", self.n_f)):
            bit = 1
            while bit < size:
                (other,) = yield [(functools.partial(swap, axis=axis, size=size, bit=bit), values)]
                values = values + other
                bit *= 2
        return values


class Chain:
    def __init__(self, moves):
        self.moves, self.result, self.done = moves, None, False
        self.pending = self.advance(None)

    def advance(self, got):
        try:
            return self.moves.send(got)
        except StopIteration as stop:
            self.result, self.done = stop.value, True
            return []


class Slots:
    def __init__(self):
        self.chains, self.token = [], None

    def add(self, moves):
        chain = Chain(moves)
        self.chains.append(chain)
        return chain

    def step(self, *extra):
        moves = list(extra)
        for chain in self.chains:
            moves += chain.pending
        values = tuple(value for _, value in moves)
        if self.token is not None:
            values = lax.optimization_barrier((values, self.token))[0]
        got = [move(value) for (move, _), value in zip(moves, values)]
        got = lax.optimization_barrier(tuple(got))
        self.token = got[0]
        at = len(extra)
        for chain in self.chains:
            count = len(chain.pending)
            chain.pending = chain.advance(list(got[at : at + count]))
            at += count
        self.chains = [chain for chain in self.chains if not chain.done]
        return got[: len(extra)]

    def finish(self, *chains):
        while not all(chain.done for chain in chains):
            self.step()
        return [chain.result for chain in chains]


def choose_matrix(group, part, member):
    row = lax.broadcasted_iota(jnp.int32, (1536, 1), 0)
    col = lax.broadcasted_iota(jnp.int32, (1, 384), 1)
    want = (col // part) * group + member * part + col % part
    return jnp.where(row == want, 1.0, 0.0).astype(BF16)


def assemble_kernel(ring, per_step, place_ref, *refs):
    pieces, out_ref = list(refs[:-1]), refs[-1]
    x, y, r = place_ref[0] // 2, place_ref[1] % 2, place_ref[1] // 2
    for k in range(ring):
        at = lax.rem(r - k + ring, ring)
        own, other = pieces.pop(0), pieces.pop(0)
        if per_step == 2:
            out_ref[at, y] = own[...]
            out_ref[at, 1 - y] = other[...]
            continue
        out_ref[at, y, x] = own[...]
        out_ref[at, 1 - y, x] = other[...]
        if k == 0:
            out_ref[at, y, 1 - x] = pieces.pop(0)[...]
            out_ref[at, 1 - y, 1 - x] = pieces.pop(0)[...]
        else:
            both = pieces.pop(0)
            out_ref[at, y, 1 - x] = both[0]
            out_ref[at, 1 - y, 1 - x] = both[1]


def emit_chunks(place_ref, values_ref, give_refs, keep_refs):
    ring = len(give_refs)
    y, r = place_ref[1] % 2, place_ref[1] // 2
    for k in range(ring):
        at = 2 * lax.rem(r - 1 - k + 2 * ring, ring)
        give_refs[k][...] = values_ref[at + 1 - y]
        keep_refs[k][...] = values_ref[at + y]


def split_kernel(group, part, place_ref, full_ref, out_ref):
    choose = choose_matrix(group, part, place_ref[0])
    for chunk in range(full_ref.shape[1] // 1536):
        out_ref[:, chunk * 384 : chunk * 384 + 384] = dot(
            full_ref[:, chunk * 1536 : chunk * 1536 + 1536], choose
        ).astype(BF16)


def finish_kernel(group, part, place_ref, *refs):
    ffn, attn, pair = refs[0:4], refs[4:8], refs[8:12]
    gate_up_ref, down_ref, qkv_ref, out_ref, outer_w_ref = refs[12:17]
    pair_gate_up_ref, outer_out_ref, pair_down_ref = refs[17:20]
    ffn_all, attn_all, pair_all = refs[20:23]
    d = place_ref[0]
    for pieces, held in ((ffn, ffn_all), (attn, attn_all), (pair, pair_all)):
        for distance in range(4):
            member = d + (1 - 2 * (d % 2)) * (distance % 2)
            member = member + (2 - 4 * (d // 2)) * (distance // 2)
            held[member] = pieces[distance][...]
    width = out_ref.shape[1]
    side = outer_w_ref.shape[1] // 4
    count = down_ref.shape[0] // 4
    quarter = gate_up_ref.shape[1] // 4
    for m in range(4):
        if m < 3:
            qkv_ref[:, m * width : (m + 1) * width] = attn_all[m][:, :width].astype(F32)
        else:
            out_ref[...] = attn_all[m][:, :width].astype(F32)
        outer_w_ref[:, m * side : (m + 1) * side] = attn_all[m][:, width:].astype(F32)
        down_ref[m * count : (m + 1) * count] = ffn_all[m][:, quarter:].astype(F32)
        choose = choose_matrix(group, part, m)
        for chunk in range(quarter // 384):
            span = slice(chunk * 1536, chunk * 1536 + 1536)
            term = dot_nt(ffn_all[m][:, chunk * 384 : chunk * 384 + 384], choose)
            if m == 0:
                gate_up_ref[:, span] = term
            else:
                gate_up_ref[:, span] += term
    half = pair_all.shape[1]
    hidden2, pair_width = pair_gate_up_ref.shape[1], outer_out_ref.shape[1]
    for x in range(2):
        rows = slice(x * half, (x + 1) * half)
        wide = jnp.concatenate([pair_all[2 * x], pair_all[2 * x + 1]], 1).astype(F32)
        pair_gate_up_ref[rows] = wide[:, :hidden2]
        outer_out_ref[rows] = wide[:, hidden2 : hidden2 + pair_width]
        for block in range(4):
            start = hidden2 + (1 + block) * pair_width
            place = 2 * half * block + x * half
            pair_down_ref[place : place + half] = wide[:, start : start + pair_width]


def bias_kernel(pairs_ref, gain_ref, weight_ref, out_ref):
    normed, _ = norm_parts(pairs_ref[...].astype(F32))
    low = (normed * gain_ref[...]).astype(BF16)
    out_ref[...] = dot_nt(weight_ref[...], low)


def head_mask(heads, length, width):
    row = lax.broadcasted_iota(jnp.int32, (heads * length, 1), 0) // length
    col = lax.broadcasted_iota(jnp.int32, (1, width), 1) // (width // heads)
    return row == col


def spread_heads(rows, mask, heads):
    return jnp.where(mask, jnp.concatenate([rows] * heads, 0), jnp.zeros((), rows.dtype))


def fold_heads(wide, mask, heads):
    kept = jnp.where(mask, wide, 0.0)
    return jnp.sum(kept.reshape(heads, wide.shape[0] // heads, wide.shape[1]), 0)


def keep_of(lengths_ref, chain, length):
    row = lax.broadcasted_iota(jnp.int32, (length, 1), 0)
    return (row < lengths_ref[chain]).astype(F32)


def attention_kernel(
    heads,
    lengths_ref,
    place_ref,
    res_ref,
    mod_ref,
    own_w_ref,
    other_w_ref,
    bias_ref,
    first_in_ref,
    qkv_ref,
    prob_ref,
    attended_ref,
    branch_ref,
    first_out_ref,
    second_in_ref,
    by_half,
):
    chains, length, width = res_ref.shape
    core = place_ref[0] % 2
    factor = 1.0 / math.sqrt(width // heads)
    mask = head_mask(heads, length, width)
    for c in range(chains):
        rows = slice(c * length, (c + 1) * length)
        normed, _ = norm_parts(res_ref[c].astype(F32))
        scale = mod_ref[c : c + 1, :width]
        shift = mod_ref[c : c + 1, width : 2 * width]
        first_in_ref[rows] = (normed * (1.0 + scale) + shift).astype(BF16)
    by_half[core] = dot(first_in_ref[...], own_w_ref[...])
    by_half[1 - core] = dot(first_in_ref[...], other_w_ref[...])
    qkv_ref[:, : 2 * width] = by_half[0].astype(BF16)
    qkv_ref[:, 2 * width :] = by_half[1][:, :width].astype(BF16)
    for c in range(chains):
        rows = slice(c * length, (c + 1) * length)
        queries = spread_heads(qkv_ref[rows, :width], mask, heads)
        keys = qkv_ref[rows, width : 2 * width]
        value_rows = qkv_ref[rows, 2 * width :]
        scores = dot_nt(queries, keys) * factor + bias_ref[c]
        column = lax.broadcasted_iota(jnp.int32, scores.shape, 1)
        scores = jnp.where(column < lengths_ref[c], scores, -1000000000.0)
        exps = jnp.exp(scores - jnp.max(scores, -1, keepdims=True))
        prob = exps / jnp.sum(exps, -1, keepdims=True)
        prob_ref[c] = prob
        wide = dot(prob.astype(BF16), value_rows)
        attended_ref[rows] = fold_heads(wide, mask, heads).astype(BF16)
    by_half[core, :, :width] = dot(attended_ref[...], own_w_ref[:, width:])
    by_half[1 - core, :, :width] = dot(attended_ref[...], other_w_ref[:, width:])
    branch_ref[...] = by_half[1, :, :width]
    for c in range(chains):
        rows = slice(c * length, (c + 1) * length)
        keep = keep_of(lengths_ref, c, length)
        gate = mod_ref[c : c + 1, 2 * width : 3 * width]
        first_out = res_ref[c].astype(F32) + keep * gate * branch_ref[rows]
        first_out_ref[rows] = first_out
        normed, _ = norm_parts(first_out)
        scale = mod_ref[c : c + 1, 3 * width : 4 * width]
        shift = mod_ref[c : c + 1, 4 * width : 5 * width]
        second_in_ref[rows] = (normed * (1.0 + scale) + shift).astype(BF16)


def emit_members(place_ref, blocks, keep_ref, give_ref):
    for m, block in enumerate(blocks):

        @pl.when(place_ref[0] // 2 == m // 2)
        def _(m=m, block=block):
            keep_ref[m % 2] = block

        @pl.when(place_ref[0] // 2 != m // 2)
        def _(m=m, block=block):
            give_ref[m % 2] = block


def silu_parts(gate):
    logistic = jax.nn.sigmoid(gate)
    act = gate * logistic
    return act, logistic + act * (1.0 - logistic)


def transition_kernel(
    own_ref,
    other_ref,
    across_ref,
    weight_ref,
    rows_ref,
    gate_ref,
    up_ref,
    hidden_ref,
    mine_ref,
    theirs_ref,
):
    count, width = own_ref.shape
    part = gate_ref.shape[1]
    rows_ref[:count] = own_ref[...]
    rows_ref[count : 2 * count] = other_ref[...]
    rows_ref[2 * count :] = across_ref[...]
    rows = rows_ref[...]
    gate = dot(rows, weight_ref[:, :part])
    up = dot(rows, weight_ref[:, part : 2 * part])
    gate_ref[...] = gate
    up_ref[...] = up
    hidden = (gate * jax.nn.sigmoid(gate) * up).astype(BF16)
    hidden_ref[...] = hidden
    down = weight_ref[:, 2 * part :]
    mine_ref[...] = dot(hidden[: 2 * count], down)
    theirs_ref[...] = dot(hidden[2 * count :], down).astype(BF16)


def outer_kernel(
    lengths_ref,
    first_out_ref,
    branch_own_ref,
    branch_other_ref,
    mod_ref,
    gain_ref,
    weight_ref,
    branch_ref,
    second_out_ref,
    res_out_ref,
    outer_in_ref,
    sides_ref,
):
    chains, width = mod_ref.shape[0], first_out_ref.shape[1]
    length = first_out_ref.shape[0] // chains
    branch = branch_own_ref[...] + branch_other_ref[...].astype(F32)
    branch_ref[...] = branch
    for c in range(chains):
        rows = slice(c * length, (c + 1) * length)
        keep = keep_of(lengths_ref, c, length)
        gate = mod_ref[c : c + 1, 5 * width : 6 * width]
        second_out_ref[rows] = first_out_ref[rows] + keep * gate * branch[rows]
    second_out = second_out_ref[...]
    res_out_ref[...] = second_out.astype(BF16)
    normed, _ = norm_parts(second_out)
    outer_in_ref[...] = (normed * gain_ref[...]).astype(BF16)
    sides_ref[...] = dot(outer_in_ref[...], weight_ref[...])


def pair_kernel(
    owners,
    lengths_ref,
    place_ref,
    left_ref,
    right_ref,
    pairs_ref,
    cot_ref,
    gain_ref,
    outer_w_ref,
    gate_up_ref,
    down_ref,
    pair_out_ref,
    pair_grad_ref,
    left_grad_ref,
    right_grad_ref,
    keep_ref,
    give_ref,
    g_gain_ref,
    acc_gate_up,
    acc_down,
    acc_outer,
    acc_gain,
):
    chain, block = pl.program_id(0), pl.program_id(1)
    _, count, length, width = pairs_ref.shape
    rows = count * length
    hidden = down_ref.shape[0]
    size = lengths_ref[chain]

    @pl.when((chain == 0) & (block == 0))
    def _():
        acc_gate_up[...] = jnp.zeros_like(acc_gate_up)
        acc_down[...] = jnp.zeros_like(acc_down)
        acc_outer[...] = jnp.zeros_like(acc_outer)
        acc_gain[...] = jnp.zeros_like(acc_gain)

    @pl.when(block == 0)
    def _():
        right_grad_ref[...] = jnp.zeros_like(right_grad_ref)

    @pl.when(block * count >= size)
    def _():
        pair_out_ref[...] = pairs_ref[...]
        pair_grad_ref[...] = cot_ref[...].astype(F32)
        left_grad_ref[...] = jnp.zeros_like(left_grad_ref)

    @pl.when(block * count < size)
    def _():
        row_i = lax.broadcasted_iota(jnp.int32, (count, length, width), 0) + block * count
        row_j = lax.broadcasted_iota(jnp.int32, (count, length, width), 1)
        kept = ((row_i < size) & (row_j < size)).reshape(rows, width)
        left = left_ref[0]
        right = right_ref[0]
        outer = (left[:, None, :] * right[None, :, :]).reshape(rows, width).astype(BF16)
        term = dot(outer, outer_w_ref[...])
        pair_one = pairs_ref[0].reshape(rows, width).astype(F32) + jnp.where(kept, term, 0.0)
        normed, inverse = norm_parts(pair_one)
        gain = gain_ref[...]
        low = (normed * gain).astype(BF16)
        both = dot(low, gate_up_ref[...])
        gate, up = both[:, :hidden], both[:, hidden:]
        act, slope = silu_parts(gate)
        hid = (act * up).astype(BF16)
        pair_two = pair_one + jnp.where(kept, dot(hid, down_ref[...]), 0.0)
        pair_out_ref[0] = pair_two.astype(BF16).reshape(count, length, width)
        cot = cot_ref[0].reshape(rows, width)
        branch_grad = jnp.where(kept, cot, jnp.zeros((), BF16))
        acc_down[...] += dot_tn(branch_grad, hid)
        hid_grad = dot_nt(branch_grad, down_ref[...])
        gate_grad = (hid_grad * up * slope).astype(BF16)
        up_grad = (hid_grad * act).astype(BF16)
        acc_gate_up[:, :hidden] += dot_tn(low, gate_grad)
        acc_gate_up[:, hidden:] += dot_tn(low, up_grad)
        low_grad = dot_nt(gate_grad, gate_up_ref[:, :hidden]) + dot_nt(
            up_grad, gate_up_ref[:, hidden:]
        )
        acc_gain[...] += jnp.sum(low_grad * normed, 0, keepdims=True)
        one_grad = cot.astype(F32) + norm_back(normed, inverse, low_grad * gain)
        pair_grad_ref[0] = one_grad.reshape(count, length, width)
        outer_grad = jnp.where(kept, one_grad, 0.0).astype(BF16)
        acc_outer[...] += dot_tn(outer, outer_grad)
        prod = dot_nt(outer_grad, outer_w_ref[...]).reshape(count, length, width)
        left_grad_ref[0] = jnp.sum(prod * right[None], 1)
        right_grad_ref[0] += jnp.sum(prod * left[:, None, :], 0)

    @pl.when((chain == pl.num_programs(0) - 1) & (block == pl.num_programs(1) - 1))
    def _():
        down = acc_down[...].T.astype(BF16)
        down = down.reshape(owners, 4, hidden // (4 * owners), width)
        down = [down[:, i].reshape(hidden // 4, width) for i in range(4)]
        wide = [acc_gate_up[...].astype(BF16), acc_outer[...].astype(BF16)] + down
        wide = jnp.concatenate(wide, 1)
        half = wide.shape[1] // 2

        @pl.when(place_ref[0] % 2 == 0)
        def _():
            keep_ref[...] = wide[:, :half]
            give_ref[...] = wide[:, half:]

        @pl.when(place_ref[0] % 2 == 1)
        def _():
            keep_ref[...] = wide[:, half:]
            give_ref[...] = wide[:, :half]

        g_gain_ref[...] = acc_gain[...]


def outer_back_kernel(
    lengths_ref,
    place_ref,
    left_grad_ref,
    right_grad_ref,
    weight_ref,
    gain_ref,
    second_out_ref,
    cot_ref,
    branch_ref,
    mod_ref,
    keep_ref,
    give_ref,
    g_gain_ref,
    second_grad_ref,
    branch_grad_ref,
    gate_pre_ref,
):
    chains, width = mod_ref.shape[0], second_out_ref.shape[1]
    length = second_out_ref.shape[0] // chains
    sides = jnp.concatenate([left_grad_ref[...], right_grad_ref[...]], 1).astype(BF16)
    upstream = dot_nt(sides, weight_ref[...])
    normed, inverse = norm_parts(second_out_ref[...])
    g_gain_ref[...] = jnp.sum(upstream * normed, 0, keepdims=True)
    second_grad_ref[...] = cot_ref[...].astype(F32) + norm_back(
        normed, inverse, upstream * gain_ref[...]
    )
    for c in range(chains):
        rows = slice(c * length, (c + 1) * length)
        keep = keep_of(lengths_ref, c, length)
        gate = mod_ref[c : c + 1, 5 * width : 6 * width]
        grad = keep * second_grad_ref[rows]
        branch_grad_ref[rows] = (gate * grad).astype(BF16)
        gate_pre_ref[c : c + 1] = (
            jnp.sum(branch_ref[rows] * grad, 0, keepdims=True) * gate * (1.0 - gate)
        )
    span = sides.shape[1] // 4
    emit_members(place_ref, [sides[:, m * span : (m + 1) * span] for m in range(4)], keep_ref, give_ref)


def transition_back_kernel(
    own_ref,
    other_ref,
    across_ref,
    gate_ref,
    up_ref,
    weight_ref,
    grads_ref,
    gate_grad_ref,
    up_grad_ref,
    mine_ref,
    theirs_ref,
):
    count = own_ref.shape[0]
    part = gate_ref.shape[1]
    grads_ref[:count] = own_ref[...]
    grads_ref[count : 2 * count] = other_ref[...]
    grads_ref[2 * count :] = across_ref[...]
    hid_grad = dot_nt(grads_ref[...], weight_ref[:, 2 * part :])
    act, slope = silu_parts(gate_ref[...])
    gate_grad = (hid_grad * up_ref[...] * slope).astype(BF16)
    up_grad = (hid_grad * act).astype(BF16)
    gate_grad_ref[...] = gate_grad
    up_grad_ref[...] = up_grad
    total = dot_nt(gate_grad, weight_ref[:, :part]) + dot_nt(
        up_grad, weight_ref[:, part : 2 * part]
    )
    mine_ref[...] = total[: 2 * count]
    theirs_ref[...] = total[2 * count :].astype(BF16)


def transition_grads_kernel(
    place_ref, rows_ref, hidden_ref, grads_ref, gate_grad_ref, up_grad_ref, *refs
):
    *out_refs, total = refs
    part = gate_grad_ref.shape[1]
    blocks = total.shape[:2] + (part,)
    rows = rows_ref[...]
    total[:, :, :part] = dot_tn(rows, gate_grad_ref[...]).astype(BF16).reshape(blocks)
    total[:, :, part : 2 * part] = dot_tn(rows, up_grad_ref[...]).astype(BF16).reshape(blocks)
    total[:, :, 2 * part :] = dot_tn(hidden_ref[...], grads_ref[...]).astype(BF16).reshape(blocks)
    emit_chunks(place_ref, total, out_refs[: len(out_refs) // 2], out_refs[len(out_refs) // 2 :])


def attention_back_kernel(
    heads,
    lengths_ref,
    place_ref,
    own_ref,
    other_ref,
    mod_ref,
    first_out_ref,
    second_grad_ref,
    branch_ref,
    res_ref,
    qkv_ref,
    prob_ref,
    own_w_ref,
    other_w_ref,
    keep_ref,
    give_ref,
    scores_grad_ref,
    res_grad_ref,
    pre_ref,
    attended_grad,
    first_grad,
    branch_grad_ref,
    qkv_grad_ref,
    by_half,
):
    chains, length, width = res_ref.shape
    core = place_ref[0] % 2
    factor = 1.0 / math.sqrt(width // heads)
    mask = head_mask(heads, length, width)
    for c in range(chains):
        rows = slice(c * length, (c + 1) * length)
        keep = keep_of(lengths_ref, c, length)
        upstream = own_ref[rows] + other_ref[rows].astype(F32)
        normed, inverse = norm_parts(first_out_ref[rows])
        pre_ref[c : c + 1, 3 * width : 4 * width] = jnp.sum(upstream * normed, 0, keepdims=True)
        pre_ref[c : c + 1, 4 * width : 5 * width] = jnp.sum(upstream, 0, keepdims=True)
        scale = mod_ref[c : c + 1, 3 * width : 4 * width]
        grad = second_grad_ref[rows] + norm_back(normed, inverse, upstream * (1.0 + scale))
        first_grad[rows] = grad
        gate = mod_ref[c : c + 1, 2 * width : 3 * width]
        kept = keep * grad
        branch_grad_ref[rows] = (gate * kept).astype(BF16)
        pre_ref[c : c + 1, 2 * width : 3 * width] = (
            jnp.sum(branch_ref[rows] * kept, 0, keepdims=True) * gate * (1.0 - gate)
        )
    by_half[core] = dot_nt(branch_grad_ref[...], own_w_ref[:, width:]).astype(BF16)
    by_half[1 - core] = dot_nt(branch_grad_ref[...], other_w_ref[:, width:]).astype(BF16)
    attended_grad[...] = by_half[1]
    for c in range(chains):
        rows = slice(c * length, (c + 1) * length)
        queries = spread_heads(qkv_ref[rows, :width], mask, heads)
        keys = qkv_ref[rows, width : 2 * width]
        value_rows = qkv_ref[rows, 2 * width :]
        upstream = spread_heads(attended_grad[rows], mask, heads)
        prob = prob_ref[c]
        prob_grad = dot_nt(upstream, value_rows)
        scores_grad = (
            prob * (prob_grad - jnp.sum(prob_grad * prob, -1, keepdims=True))
        ).astype(BF16)
        scores_grad_ref[c] = scores_grad
        query_grad = fold_heads(dot(scores_grad, keys), mask, heads) * factor
        key_grad = dot_tn(scores_grad, queries) * factor
        value_grad = dot_tn(prob.astype(BF16), upstream)
        qkv_grad_ref[0, rows, :width] = query_grad.astype(BF16)
        qkv_grad_ref[0, rows, width:] = key_grad.astype(BF16)
        qkv_grad_ref[1, rows, :width] = value_grad.astype(BF16)
    blocks = [
        qkv_grad_ref[0, :, :width],
        qkv_grad_ref[0, :, width:],
        qkv_grad_ref[1, :, :width],
        branch_grad_ref[...],
    ]
    emit_members(place_ref, blocks, keep_ref, give_ref)
    qkv_grad_ref[1, :, width:] = jnp.zeros((chains * length, width), BF16)
    first_in_grad = dot_nt(qkv_grad_ref[core], own_w_ref[...]) + dot_nt(
        qkv_grad_ref[1 - core], other_w_ref[...]
    )
    for c in range(chains):
        rows = slice(c * length, (c + 1) * length)
        upstream = first_in_grad[rows]
        normed, inverse = norm_parts(res_ref[c].astype(F32))
        pre_ref[c : c + 1, :width] = jnp.sum(upstream * normed, 0, keepdims=True)
        pre_ref[c : c + 1, width : 2 * width] = jnp.sum(upstream, 0, keepdims=True)
        scale = mod_ref[c : c + 1, :width]
        res_grad_ref[rows] = first_grad[rows] + norm_back(
            normed, inverse, upstream * (1.0 + scale)
        )


def attention_grads_kernel(
    place_ref,
    keep_in,
    got_in,
    across_in,
    keep_grad,
    got_grad,
    across_grad,
    outer_own,
    outer_other,
    outer_across,
    keep_side,
    got_side,
    across_side,
    *refs,
):
    *out_refs, total = refs
    core = place_ref[0] % 2
    width = outer_own.shape[1]
    lead = total.shape[:2]
    inputs = jnp.concatenate([keep_in[core], got_in[core], across_in[0], across_in[1]], 0)
    grads = jnp.concatenate([keep_grad[core], got_grad[core], across_grad[0], across_grad[1]], 0)
    total[:, :, :width] = dot_tn(inputs, grads).astype(BF16).reshape(lead + (width,))
    inputs = jnp.concatenate([outer_own[...], outer_other[...], outer_across[...]], 0)
    grads = jnp.concatenate([keep_side[core], got_side[core], across_side[0], across_side[1]], 0)
    term = dot_tn(inputs, grads).astype(BF16)
    total[:, :, width:] = term.reshape(lead + (term.shape[1],))
    emit_chunks(place_ref, total, out_refs[: len(out_refs) // 2], out_refs[len(out_refs) // 2 :])


def whole_chunks_kernel(kernel, place_ref, *refs):
    kernel(place_ref, *refs)


def pair_last_kernel(
    pairs_ref, one_grad_ref, scores_grad_ref, gain_ref, weight_ref, out_ref, g_weight_ref, g_gain_ref
):
    normed, inverse = norm_parts(pairs_ref[...].astype(F32))
    gain = gain_ref[...]
    low = (normed * gain).astype(BF16)
    scores_grad = scores_grad_ref[...]
    upstream = dot_tn(scores_grad, weight_ref[...])
    out_ref[...] = one_grad_ref[...] + norm_back(normed, inverse, upstream * gain)

    @pl.when(pl.program_id(0) == 0)
    def _():
        g_weight_ref[...] = jnp.zeros_like(g_weight_ref)
        g_gain_ref[...] = jnp.zeros_like(g_gain_ref)

    g_weight_ref[...] += dot(scores_grad, low)
    g_gain_ref[...] += jnp.sum(upstream * normed, 0, keepdims=True)


def on_device(
    n_dp,
    n_f,
    residues,
    pairs,
    lengths,
    time_bins,
    cath_labels,
    residue_cotangent,
    pair_cotangent,
    time_table,
    cath_table,
    attn_modulation,
    attn_gate,
    qkv_weight,
    bias_gain,
    bias_weight,
    out_weight,
    ffn_modulation,
    ffn_gate,
    gate_up,
    down_weight,
    outer_gain,
    outer_weight,
    outer_out,
    pair_gain,
    pair_gate_up,
    pair_down,
):
    place = Place(n_dp, n_f)
    d, f = place.d, place.f
    chains, length, width = residues.shape
    rows = chains * length
    heads = bias_weight.shape[1]
    pair_width = outer_out.shape[1]
    pair_rows = chains * length * length
    time_rows, cath_rows = time_table.shape[0], cath_table.shape[0]
    mod_rows = attn_modulation.shape[0]
    hid_rows = down_weight.shape[0]
    hid_part = hid_rows // 4
    part = hid_part * n_f
    place_ints = place.ints

    slots = Slots()

    lanes = pair_gate_up.shape[0]
    attn_weights = slots.add(place.gather_all(jnp.concatenate([qkv_weight, out_weight], 1)))

    (my_gate_up,) = call_whole(
        functools.partial(split_kernel, hid_rows, hid_part),
        "split_gate_up",
        2.0,
        [struct((mod_rows, gate_up.shape[1] // 4), BF16)],
        place_ints,
        gate_up,
    )
    my_down = pick(down_weight.reshape(4, hid_part, width), d, 0)

    small = jnp.concatenate(
        [
            time_bins.astype(F32),
            cath_labels.astype(F32),
            bias_gain.astype(F32),
            pair_gain.astype(F32),
            outer_gain.astype(F32),
            bias_weight.astype(F32).reshape(-1),
        ]
    )
    (small,) = slots.step((place.to_all_f, small))
    at = 0

    def take(size):
        nonlocal at
        piece = small[:, at : at + size]
        at += size
        return piece

    ffn_weights = slots.add(place.gather_f(jnp.concatenate([my_gate_up, my_down], 1)))
    bins = take(chains).reshape(-1).astype(jnp.int32)
    labels = take(chains).reshape(-1).astype(jnp.int32)
    bias_gain_row = take(bias_gain.shape[0]).reshape(1, pair_width)
    pair_gain_row = take(pair_gain.shape[0]).reshape(1, pair_width)
    outer_gain_row = take(outer_gain.shape[0]).reshape(1, width)
    bias_w = take(bias_weight.size).reshape(pair_width, heads)
    bias_w_t = jnp.pad(bias_w.T, ((0, 16 - heads), (0, 0))).astype(BF16)

    n_group = n_f * chains
    time_hot = (
        (bins[:, None] - f * time_rows) == jnp.arange(time_rows)[None, :]
    ).astype(BF16)
    cath_hot = (
        (labels[:, None] - f * cath_rows) == jnp.arange(cath_rows)[None, :]
    ).astype(BF16)
    condition = (dot(time_hot, time_table) + dot(cath_hot, cath_table)).astype(BF16)
    condition = jnp.swapaxes(condition.reshape(n_group, n_f, mod_rows), 0, 1)
    (condition,) = slots.step((place.to_each_f, condition))
    cond_cols = jnp.sum(condition.astype(F32), 0).astype(BF16)
    mod_weights = jnp.concatenate([attn_modulation, attn_gate, ffn_modulation, ffn_gate], 1)
    mods = dot(cond_cols, mod_weights).reshape(n_f, chains, 6 * width)
    first_mods, other_mods = mods[..., : 2 * width], mods[..., 2 * width :]
    (first_mods,) = slots.step((place.to_each_f, first_mods))
    def side_by_side(weight):
        rows_of, width_of = weight.shape
        parts = weight.reshape(rows_of // lanes, lanes, width_of)
        return [parts[i] for i in range(rows_of // lanes)]

    pair_weights = slots.add(
        place.gather_all(
            jnp.concatenate(
                [pair_gate_up] + side_by_side(outer_weight) + [outer_out] + side_by_side(pair_down), 1
            )
        )
    )
    (other_mods,) = slots.step((place.to_each_f, other_mods))
    mods = jnp.concatenate([jnp.sum(first_mods, 0), jnp.sum(other_mods, 0)], 1)
    gated = jnp.arange(6 * width)[None, :] // width
    mods = jnp.where((gated == 2) | (gated == 5), jax.nn.sigmoid(mods), mods)

    ((own_attn, other_attn),) = slots.finish(attn_weights)

    pairs_flat = pairs.reshape(pair_rows, pair_width)
    block = 512
    bias = pl.pallas_call(
        bias_kernel,
        name="pair_bias",
        grid=(pair_rows // block,),
        in_specs=[
            pl.BlockSpec((block, pair_width), lambda i: (i, 0)),
            whole((1, pair_width)),
            whole((16, pair_width)),
        ],
        out_specs=pl.BlockSpec((16, block), lambda i: (0, i)),
        out_shape=struct((16, pair_rows), F32),
        cost_estimate=cost(6.0),
        compiler_params=params(),
    )(pairs_flat, bias_gain_row, bias_w_t)
    bias = bias[:heads].reshape(heads, chains, length, length)
    bias = jnp.transpose(bias, (1, 0, 2, 3)).reshape(chains, heads * length, length)
    first_in, qkv, prob, attended, first_branch, first_out, second_in = call_whole(
        functools.partial(attention_kernel, heads),
        "attention",
        6.0,
        [
            struct((rows, width), BF16),
            struct((rows, 3 * width), BF16),
            struct((chains, heads * length, length), F32),
            struct((rows, width), BF16),
            struct((rows, width), F32),
            struct((rows, width), F32),
            struct((rows, width), BF16),
        ],
        lengths,
        place_ints,
        residues,
        mods,
        own_attn,
        other_attn,
        bias,
        scratch=[pltpu.VMEM((2, rows, 2 * width), F32)],
    )

    slots.step()
    (other_rows,) = slots.step((place.swap_x, second_in))
    (across_rows,) = slots.step((place.swap_core, jnp.concatenate([second_in, other_rows])))
    (ffn_weight,) = slots.finish(ffn_weights)
    ffn_weight = ffn_weight.reshape(width, -1)
    rows_all, gate, up, hidden, mine, theirs = call_whole(
        transition_kernel,
        "transition",
        5.0,
        [
            struct((4 * rows, width), BF16),
            struct((4 * rows, part), F32),
            struct((4 * rows, part), F32),
            struct((4 * rows, part), BF16),
            struct((2 * rows, width), F32),
            struct((2 * rows, width), BF16),
        ],
        second_in,
        other_rows,
        across_rows,
        ffn_weight,
    )
    (across,) = slots.step((place.swap_core, theirs))
    branch_own = mine + across.astype(F32)
    (branch_other,) = slots.step((place.swap_x, branch_own[rows:].astype(BF16)))
    ((own_pair, other_pair),) = slots.finish(pair_weights)
    low_pair = jnp.where(place.core == 0, own_pair, other_pair)
    high_pair = jnp.where(place.core == 0, other_pair, own_pair)
    pair_all = jnp.concatenate([low_pair, high_pair], 1)
    start = pair_gate_up.shape[1]

    def take_cols(shape):
        nonlocal start
        wide = shape[0] * shape[1] // pair_all.shape[0]
        piece = pair_all[:, start : start + wide].reshape(n_f, lanes, wide // shape[1], shape[1])
        start += wide
        return jnp.swapaxes(piece, 1, 2).reshape(shape)

    outer_w_full = take_cols((width, 2 * pair_width))
    outer_out_full = take_cols((pair_width, pair_width))
    pair_down_full = take_cols((pair_down.shape[0] * n_f, pair_width))
    first_half = {2: whole((rows, width))}
    second_branch, second_out, res_out, outer_in, sides = call_whole(
        outer_kernel,
        "outer_sides",
        3.0,
        [
            struct((rows, width), F32),
            struct((rows, width), F32),
            struct((rows, width), BF16),
            struct((rows, width), BF16),
            struct((rows, 2 * pair_width), F32),
        ],
        lengths,
        first_out,
        branch_own,
        branch_other,
        mods,
        outer_gain_row,
        outer_w_full,
        blocks=first_half,
    )

    back_small = jnp.concatenate(
        [bins.astype(F32)[:, None], labels.astype(F32)[:, None], cond_cols.astype(F32)], 1
    )
    keep_in = jnp.stack([first_in, jnp.where(place.x == 1, attended, first_in)])
    give_in = jnp.stack([first_in, jnp.where(place.x == 0, attended, first_in)])
    got_in, other_small, outer_other = slots.step(
        (place.swap_x, give_in), (place.swap_x, back_small), (place.swap_x, outer_in)
    )
    back_small = ordered(place.x, back_small, other_small, 0)

    def toward_core(keep, got):
        return jnp.stack([pick(keep, 1 - place.core, 0), pick(got, 1 - place.core, 0)])


    sides = sides.reshape(chains, length, 2 * pair_width)
    count = 8
    pair_hidden = pair_down_full.shape[0]
    wide_half = (3 * pair_hidden + pair_width) // 2
    pair_block = pl.BlockSpec((1, count, length, pair_width), lambda c, b: (c, b, 0, 0))
    (
        pair_out,
        pair_grad,
        left_grad,
        right_grad,
        keep_pair,
        give_pair,
        g_pair_gain,
    ) = pl.pallas_call(
        functools.partial(pair_kernel, n_f),
        name="pairs",
        grid=(chains, length // count),
        in_specs=[
            SMEM,
            SMEM,
            pl.BlockSpec((1, count, pair_width), lambda c, b: (c, b, 0)),
            pl.BlockSpec((1, length, pair_width), lambda c, b: (c, 0, 1)),
            pair_block,
            pair_block,
            whole((1, pair_width)),
            whole(outer_out_full.shape),
            whole((pair_width, 2 * pair_hidden)),
            whole(pair_down_full.shape),
        ],
        out_specs=[
            pair_block,
            pair_block,
            pl.BlockSpec((1, count, pair_width), lambda c, b: (c, b, 0)),
            pl.BlockSpec((1, length, pair_width), lambda c, b: (c, 0, 0)),
            whole((pair_width, wide_half)),
            whole((pair_width, wide_half)),
            whole((1, pair_width)),
        ],
        out_shape=[
            struct(pairs.shape, BF16),
            struct(pairs.shape, F32),
            struct((chains, length, pair_width), F32),
            struct((chains, length, pair_width), F32),
            struct((pair_width, wide_half), BF16),
            struct((pair_width, wide_half), BF16),
            struct((1, pair_width), F32),
        ],
        scratch_shapes=[
            pltpu.VMEM((pair_width, 2 * pair_hidden), F32),
            pltpu.VMEM((pair_width, pair_hidden), F32),
            pltpu.VMEM((pair_width, pair_width), F32),
            pltpu.VMEM((1, pair_width), F32),
        ],
        cost_estimate=cost(35.0),
        compiler_params=params(),
    )(
        lengths,
        place_ints,
        sides,
        sides,
        pairs,
        pair_cotangent,
        pair_gain_row,
        outer_out_full,
        pair_all,
        pair_down_full,
    )

    keep_side, give_side, g_outer_gain, second_grad, branch_two_grad, second_pre = call_whole(
        outer_back_kernel,
        "outer_sides_back",
        3.0,
        [
            struct((2, rows, pair_width // 2), BF16),
            struct((2, rows, pair_width // 2), BF16),
            struct((1, width), F32),
            struct((rows, width), F32),
            struct((rows, width), BF16),
            struct((chains, width), F32),
        ],
        lengths,
        place_ints,
        left_grad.reshape(rows, pair_width),
        right_grad.reshape(rows, pair_width),
        outer_w_full,
        outer_gain_row,
        second_out,
        residue_cotangent.reshape(rows, width),
        second_branch,
        mods,
    )

    other_grads, got_side, across_in, other_small, outer_across, across_pair = slots.step(
        (place.swap_x, branch_two_grad),
        (place.swap_x, give_side),
        (place.swap_core, toward_core(keep_in, got_in)),
        (place.swap_core, back_small),
        (place.swap_core, jnp.concatenate([outer_in, outer_other])),
        (place.swap_core, give_pair),
    )
    back_small = ordered(place.core, back_small, other_small, 1).reshape(n_dp * n_group, -1)
    bins_all = back_small[:, 0].astype(jnp.int32)
    labels_all = back_small[:, 1].astype(jnp.int32)
    cond_all = back_small[:, 2:].astype(BF16)
    across_grads, across_side = slots.step(
        (place.swap_core, jnp.concatenate([branch_two_grad, other_grads])),
        (place.swap_core, toward_core(keep_side, got_side)),
    )
    grads_all, gate_grad, up_grad, mine, theirs = call_whole(
        transition_back_kernel,
        "transition_back",
        6.0,
        [
            struct((4 * rows, width), BF16),
            struct((4 * rows, part), BF16),
            struct((4 * rows, part), BF16),
            struct((2 * rows, width), F32),
            struct((2 * rows, width), BF16),
        ],
        branch_two_grad,
        other_grads,
        across_grads,
        gate,
        up,
        ffn_weight,
    )
    (across,) = slots.step((place.swap_core, theirs))
    own = mine + across.astype(F32)

    def chunk_call(kernel, name, micros, shape, *operands):
        if shape[0] % 16 == 0:
            chunks = call_whole(
                kernel,
                name,
                micros,
                [struct(shape, BF16)] * (2 * place.ring),
                place_ints,
                *operands,
                scratch=[pltpu.VMEM((n_f,) + shape, BF16)],
            )
            return chunks[: place.ring], chunks[place.ring :]
        (total,) = call_whole(
            functools.partial(whole_chunks_kernel, kernel),
            name,
            micros,
            [struct((1, n_f * shape[0], shape[1]), BF16)],
            place_ints,
            *operands,
        )
        return place.chunks(total.reshape((n_f,) + shape))

    ffn_chunks = chunk_call(
        transition_grads_kernel,
        "transition_grads",
        5.0,
        (mod_rows, 2 * part + width),
        rows_all,
        hidden,
        grads_all,
        gate_grad,
        up_grad,
    )
    (other,) = slots.step((place.swap_x, own[rows:].astype(BF16)))
    ffn_sums = slots.add(place.reduce_f(*ffn_chunks))
    pair_shape = (n_f, 2, lanes // 2, wide_half)
    pair_sums = slots.add(
        place.reduce_x(keep_pair.reshape(pair_shape), across_pair.reshape(pair_shape))
    )

    keep_grad, give_grad, scores_grad, res_grad, pre = call_whole(
        functools.partial(attention_back_kernel, heads),
        "attention_back",
        9.0,
        [
            struct((2, rows, width), BF16),
            struct((2, rows, width), BF16),
            struct((chains, heads * length, length), BF16),
            struct((rows, width), F32),
            struct((chains, 5 * width), F32),
        ],
        lengths,
        place_ints,
        own,
        other,
        mods,
        first_out,
        second_grad,
        first_branch,
        residues,
        qkv,
        prob,
        own_attn,
        other_attn,
        blocks=first_half,
        scratch=[
            pltpu.VMEM((rows, width), BF16),
            pltpu.VMEM((rows, width), F32),
            pltpu.VMEM((rows, width), BF16),
            pltpu.VMEM((2, rows, 2 * width), BF16),
            pltpu.VMEM((2, rows, width), BF16),
        ],
    )
    slots.step()

    pre = jnp.concatenate([pre, second_pre], 1).astype(BF16)
    got_grad, pre_group = slots.step((place.swap_x, give_grad), (place.to_all_f, pre))
    scores_t = jnp.transpose(
        scores_grad.reshape(chains, heads, length, length), (1, 0, 2, 3)
    ).reshape(heads, pair_rows)
    scores_t = jnp.pad(scores_t, ((0, 16 - heads), (0, 0)))
    pairs_grad, g_bias_w, g_bias_gain = pl.pallas_call(
        pair_last_kernel,
        name="pairs_last",
        grid=(pair_rows // block,),
        in_specs=[
            pl.BlockSpec((block, pair_width), lambda i: (i, 0)),
            pl.BlockSpec((block, pair_width), lambda i: (i, 0)),
            pl.BlockSpec((16, block), lambda i: (0, i)),
            whole((1, pair_width)),
            whole((16, pair_width)),
        ],
        out_specs=[
            pl.BlockSpec((block, pair_width), lambda i: (i, 0)),
            whole((16, pair_width)),
            whole((1, pair_width)),
        ],
        out_shape=[
            struct((pair_rows, pair_width), F32),
            struct((16, pair_width), F32),
            struct((1, pair_width), F32),
        ],
        cost_estimate=cost(9.0),
        compiler_params=params(),
    )(pairs_flat, pair_grad.reshape(pair_rows, pair_width), scores_t, bias_gain_row, bias_w_t)

    small_terms = jnp.concatenate(
        [g_bias_w[:heads], g_bias_gain, g_pair_gain, g_outer_gain.reshape(-1, pair_width)], 0
    )
    small_terms = slots.add(place.sum_everywhere(small_terms))
    pre_group = pre_group.reshape(n_group, 6 * width)
    cond_grad = dot_nt(pre_group, mod_weights)
    across_grad, cond_grad, pre_other = slots.step(
        (place.swap_core, toward_core(keep_grad, got_grad)),
        (place.to_all_f, cond_grad.astype(BF16)),
        (place.swap_x, pre_group),
    )
    attn_chunks = chunk_call(
        attention_grads_kernel,
        "attention_grads",
        4.0,
        (mod_rows, width + pair_width // 2),
        keep_in,
        got_in,
        across_in,
        keep_grad,
        got_grad,
        across_grad,
        outer_in,
        outer_other,
        outer_across,
        keep_side,
        got_side,
        across_side,
    )
    attn_sums = slots.add(place.reduce_f(*attn_chunks))
    pre_all = ordered(place.x, pre_group, pre_other, 0)
    cond_grad = jnp.swapaxes(cond_grad, 0, 1).reshape(n_group, width)
    pre_other, cond_other = slots.step((place.swap_core, pre_all), (place.swap_x, cond_grad))
    pre_all = ordered(place.core, pre_all, pre_other, 1).reshape(n_dp * n_group, 6 * width)
    cond_grad = ordered(place.x, cond_grad, cond_other, 0)
    (cond_other,) = slots.step((place.swap_core, cond_grad))
    cond_grad = ordered(place.core, cond_grad, cond_other, 1).reshape(n_dp * n_group, width)
    g_mods = dot_tn(cond_all, pre_all)
    time_all = (
        (bins_all[:, None] - f * time_rows) == jnp.arange(time_rows)[None, :]
    ).astype(BF16)
    cath_all = (
        (labels_all[:, None] - f * cath_rows) == jnp.arange(cath_rows)[None, :]
    ).astype(BF16)
    out_time = dot_tn(time_all, cond_grad)
    out_cath = dot_tn(cath_all, cond_grad)

    attn_sums, ffn_sums, pair_sums, small_terms = slots.finish(
        attn_sums, ffn_sums, pair_sums, small_terms
    )
    (
        out_gate_up,
        out_down,
        out_qkv,
        out_out,
        out_outer_w,
        out_pair_gate_up,
        out_outer_out,
        out_pair_down,
    ) = call_whole(
        functools.partial(finish_kernel, hid_rows, hid_part),
        "finish",
        8.0,
        [
            struct(w.shape, F32)
            for w in (
                gate_up,
                down_weight,
                qkv_weight,
                out_weight,
                outer_weight,
                pair_gate_up,
                outer_out,
                pair_down,
            )
        ],
        place_ints,
        *ffn_sums,
        *attn_sums,
        *pair_sums,
        scratch=[pltpu.VMEM((4,) + sums[0].shape, BF16) for sums in (ffn_sums, attn_sums, pair_sums)],
    )
    bias_rows = bias_weight.shape[0]
    small_own = lax.dynamic_slice_in_dim(small_terms, f * bias_rows, bias_rows, 1)
    out_bias_w = small_own[:heads].T
    out_bias_gain = small_own[heads]
    out_pair_gain = small_own[heads + 1]
    out_outer_gain = lax.dynamic_slice_in_dim(
        small_terms[heads + 2 :].reshape(-1), f * mod_rows, mod_rows, 0
    )

    return (
        res_out.reshape(residues.shape),
        pair_out,
        res_grad.reshape(residues.shape),
        pairs_grad.reshape(pairs.shape),
        out_time,
        out_cath,
        g_mods[:, : 2 * width],
        g_mods[:, 2 * width : 3 * width],
        out_qkv,
        out_bias_gain,
        out_bias_w,
        out_out,
        g_mods[:, 3 * width : 5 * width],
        g_mods[:, 5 * width :],
        out_gate_up,
        out_down,
        out_outer_gain,
        out_outer_w,
        out_outer_out,
        out_pair_gain,
        out_pair_gate_up,
        out_pair_down,
    )


def solution(mesh):
    chains3 = P(("dp", "fsdp"), None, None)
    chains4 = P(("dp", "fsdp"), None, None, None)
    chains1 = P(("dp", "fsdp"))
    table = P("fsdp", None)
    line = P("fsdp")
    weights = (
        table,
        table,
        table,
        table,
        table,
        line,
        table,
        table,
        table,
        table,
        table,
        table,
        line,
        table,
        table,
        line,
        table,
        table,
    )
    return jax.shard_map(
        functools.partial(on_device, mesh.shape["dp"], mesh.shape["fsdp"]),
        mesh=mesh,
        in_specs=(chains3, chains4, chains1, chains1, chains1, chains3, chains4) + weights,
        out_specs=(chains3, chains4, chains3, chains4) + weights,
        check_vma=False,
    )
```

time: 519 us -> 413 us (0.80)
  waiting for transfers between devices: 180 us -> 118 us
  local copies, waits for them, and re-layouts: 74.9 us -> 32.1 us
  starting transfers between devices: 89.9 us -> 106 us
  Pallas kernels: 112 us -> 128 us
  other arithmetic: 31.3 us -> 15.9 us
  between operations: 15.9 us -> 3 us
    ppermute x53 -> x69, waiting for transfers between devices: 148 us -> 75.1 us  [swap(): return lax.ppermute(values, axis, [(i, i ^ bit) for i in range(size)])]
    all_to_all x0 -> x6, starting transfers between devices: none -> 27 us  [to_each_f(): lax.all_to_all(values, 'fsdp', split_axis=0, concat_axis=0, tiled=True)]
    pallas_call x9 -> x13, Pallas kernels: 45.9 us -> 69.5 us  [call_whole(): pl.pallas_call(kernel, grid=(1,), name=name, in_specs=specs, out_specs=[w...]
    ppermute x53 -> x69, starting transfers between devices: 83.7 us -> 65.3 us  [swap(): return lax.ppermute(values, axis, [(i, i ^ bit) for i in range(size)])]
    slice x22 -> x12, local copies, waits for them, and re-layouts: 18.7 us -> 3.81 us  [the longest x1 1.17 us: on_device(): g_mods[:, 3 * width:5 * width]]
    all_to_all x0 -> x6, waiting for transfers between devices: none -> 10.6 us  [to_each_f(): lax.all_to_all(values, 'fsdp', split_axis=0, concat_axis=0, tiled=True)]
    concatenate x10 -> x2, local copies, waits for them, and re-layouts: 10.4 us -> 0.01 us  [the longest x1 0.01 us: on_device(): jnp.concatenate([attn_modulation, attn_gate, ffn_modulation, ffn_gate], 1)]
    ppermute x15 -> x18, starting transfers between devices: 6.2 us -> 13.7 us  [shift_ring(): lax.ppermute(values, 'fsdp', [(i, (i + 2) % self.n_f) for i in range(self...]
  transfers between devices with their start and end apart: 69 -> 93, of which waited for: 36 -> 37; matrix products, arithmetic and copies ran while one was open for 20% -> 7% of each run, Pallas kernels for 19% -> 20%
where the time goes in v1:
time: 413 us; the launch traced here: 407 us
  Pallas kernels  128 us (31%)
  waiting for transfers between devices  118 us (29%)
  starting transfers between devices  106 us (26%)
  local copies, waits for them, and re-layouts  32.1 us (8%)
  other arithmetic  15.9 us (4%)
    ppermute x69, waiting for transfers between devices, swap(): return lax.ppermute(values, axis, [(i, i ^ bit) for i in range(size)])  75.1 us
    pallas_call x13, Pallas kernels, call_whole(): pl.pallas_call(kernel, grid=(1,), name=name, in_specs=specs, out_specs=[w...  69.5 us
    ppermute x69, starting transfers between devices, swap(): return lax.ppermute(values, axis, [(i, i ^ bit) for i in range(size)])  65.3 us
    pallas_call x1, Pallas kernels, on_device(): pl.pallas_call(functools.partial(pair_kernel, n_f), name='pairs', grid=(c...  43.3 us
    ppermute x18, waiting for transfers between devices, shift_ring(): lax.ppermute(values, 'fsdp', [(i, (i + 2) % self.n_f) for i in range(self...  32 us
    all_to_all x6, starting transfers between devices, to_each_f(): lax.all_to_all(values, 'fsdp', split_axis=0, concat_axis=0, tiled=True)  27 us
    ppermute x18, starting transfers between devices, shift_ring(): lax.ppermute(values, 'fsdp', [(i, (i + 2) % self.n_f) for i in range(self...  13.7 us
    all_to_all x6, waiting for transfers between devices, to_each_f(): lax.all_to_all(values, 'fsdp', split_axis=0, concat_axis=0, tiled=True)  10.6 us
  transfers between devices with their start and end apart: 93, of which 37 were waited for; matrix products, arithmetic and copies ran while one was open for 7% of the time, Pallas kernels for 20%

profile of v1, /device:TPU:1, one launch (start us, length us, event | category | flops | bytes accessed | tf_op | source)
XLA Modules:
  0.0 406.5 jit_solution(7637912293444248006)
XLA Ops:
  2.7 2.1 collective-permute-start
  9.0 3.6 all-to-all-start
  13.5 3.0 split_gate_up.1
  24.5 4.3 %all-to-all-start.1 = ((bf16[8,32,96]{2,1,0:T(8,128)(2,1)}), bf16[8,32,96]{2,1,0:T(8,128)(2,1)S(1)}, u32[]{:S(2)}, u32[]{:S(2)}) async-start(bf16[8,32,96]{2,1,0:T(8,128)(2,1)} %bitcast.149), calls=%async_computation.1 | async-start | bytes 131072 | tf_op jit(solution)/shard_map/all_to_all | solution.py:119
  28.8 10.2 %all-to-all-done.1 = bf16[8,32,96]{2,1,0:T(8,128)(2,1)S(1)} async-done(((bf16[8,32,96]{2,1,0:T(8,128)(2,1)}), bf16[8,32,96]{2,1,0:T(8,128)(2,1)S(1)}, u32[]{:S(2)}, u32[]{:S(2)}) %all-to-all-start.1) | async-done | bytes 49184 | tf_op jit(solution)/shard_map/all_to_all | solution.py:119
  40.8 3.4 all-to-all-start.2
  50.2 10.3 %collective-permute-done.7.refs_8_ = bf16[48,1536]{1,0:T(8,128)(2,1)S(1)} collective-permute-done((bf16[48,1536]{1,0:T(8,128)(2,1)S(1)}, bf16[48,1536]{1,0:T(8,128)(2,1)S(1)}, u32[]{:S(2)}, u32[]{:S(2)}) %collective-permute-start.7) | collective-permute-done | bytes 147488 | tf_op jit(solution)/shard_map/ppermute | solution.py:82
  60.6 2.8 collective-permute-done.8.refs_10_
  64.4 3.5 all-to-all-start.3
  73.1 11.4 %collective-permute-done.16.refs_1_ = bf16[16,2432]{1,0:T(8,128)(2,1)S(1)} collective-permute-done((bf16[16,2432]{1,0:T(8,128)(2,1)S(1)}, bf16[16,2432]{1,0:T(8,128)(2,1)S(1)}, u32[]{:S(2)}, u32[]{:S(2)}) %collective-permute-start.16) | collective-permute-done | bytes 77856 | tf_op jit(solution)/shard_map/ppermute | solution.py:82
  84.8 5.1 %collective-permute-done.17.refs_4_ = bf16[16,2432]{1,0:T(8,128)(2,1)S(1)} collective-permute-done((bf16[16,2432]{1,0:T(8,128)(2,1)S(1)}, bf16[16,2432]{1,0:T(8,128)(2,1)S(1)}, u32[]{:S(2)}, u32[]{:S(2)}) %collective-permute-start.17) | collective-permute-done | bytes 77856 | tf_op jit(solution)/shard_map/ppermute | solution.py:114
  93.9 6.3 %collective-permute-done.20.refs_5_ = bf16[16,2432]{1,0:T(8,128)(2,1)S(1)} collective-permute-done((bf16[16,2432]{1,0:T(8,128)(2,1)S(1)}, bf16[16,2432]{1,0:T(8,128)(2,1)S(1)}, u32[]{:S(2)}, u32[]{:S(2)}) %collective-permute-start.20) | collective-permute-done | bytes 77856 | tf_op jit(solution)/shard_map/ppermute | solution.py:82
  101.0 3.3 assemble.3
  104.3 5.3 %collective-permute-start.23 = (bf16[768,1536]{1,0:T(8,128)(2,1)}, bf16[768,1536]{1,0:T(8,128)(2,1)}, u32[]{:S(2)}, u32[]{:S(2)}) collective-permute-start(bf16[768,1536]{1,0:T(8,128)(2,1)} %bitcast.200), channel_id=1, source_target_pairs={{0,8},{8,0},{16,24},{24,16},{1,9},{9,1},{17,25},{25,17},{2,10},{10... | collective-permute-start | bytes 7077896 | tf_op jit(solution)/shard_map/ppermute | solution.py:82
  111.3 6.7 %pair_bias.1 = f32[16,4096]{1,0:T(8,128)} custom-call(bf16[4096,256]{1,0:T(8,128)(2,1)} %bitcast.203, f32[1,256]{1,0:T(1,128)} %reshape.283.gain_ref, bf16[16,256]{1,0:T(8,128)(2,1)} %pad.9.weight_ref), custom_call_target="tpu_custom_call" | custom-call | flops 6000000000 | tf_op jit(solution)/shard_map/pair_bias/pallas_call | solution.py:990
  122.8 1.5 collective-permute-done.24.refs_8_
  124.2 2.0 collective-permute-done.25.refs_10_
  128.6 7.2 %attention.1 = (bf16[128,768]{1,0:T(8,128)(2,1)}, bf16[128,2304]{1,0:T(8,128)(2,1)}, f32[4,384,32]{2,1,0:T(8,128)}, bf16[128,768]{1,0:T(8,128)(2,1)}, f32[128,76...) custom-call(s32[4]{0:T(128)} %lengths_ref.9, s32[2]{0:T(128)} %pad_add_fusion.place_ref, ...), custom_call_target="tpu_custom_call" | custom-call | flops 6000000000 | tf_op jit(solution)/shard_map/attention/pallas_call | solution.py:64
  137.4 6.8 %collective-permute-done.30.refs_12_ = bf16[2,16,2432]{2,1,0:T(8,128)(2,1)S(1)} collective-permute-done((bf16[2,16,2432]{2,1,0:T(8,128)(2,1)S(1)}, bf16[2,16,2432]{2,1,0:T(8,128)(2,1)S(1)}, u32[]{:S(2)}, u32[]{:S(2)}) %collective-permute-start.30) | collective-permute-done | bytes 155680 | tf_op jit(solution)/shard_map/ppermute | solution.py:82
  145.3 2.5 assemble.4
  147.9 2.6 collective-permute-start.32
  152.1 4.1 assemble.5
  159.4 5.6 %transition.1 = (bf16[512,768]{1,0:T(8,128)(2,1)}, f32[512,768]{1,0:T(8,128)}, f32[512,768]{1,0:T(8,128)}, bf16[512,768]{1,0:T(8,128)(2,1)}, f32[256,768]{1,0:T(8,128)}, /*index=5*/bf16[256,768]{1,0:T(8,128)(2,1)}) custom-call(bf16[128,768]{1,0:T(8,128)(2,1)} %get-tuple-element.326.own_ref, bf16[128,768]{1,0:T(8,128)(2,1)} %copy-done.23, ...), custom_call_target="tpu_custom_call" | custom-call | flops 5000000000 | tf_op jit(solution)/shard_map/transition/pallas_call | solution.py:64
  165.1 1.7 pad_maximum_fusion.gate_up_ref
  171.1 3.2 collective-permute-done.34.branch_other_ref
  174.3 2.7 outer_sides.1
  178.8 43.3 %pairs.1 = (bf16[4,32,32,256]{3,2,1,0:T(8,128)(2,1)}, f32[4,32,32,256]{3,2,1,0:T(8,128)}, f32[4,32,256]{2,1,0:T(8,128)}, f32[4,32,256]{2,1,0:T(8,128)}, bf16[256...) custom-call(s32[4]{0:T(128)} %lengths_ref.9, s32[2]{0:T(128)} %pad_add_fusion.place_ref, ...), custom_call_target="tpu_custom_call" | custom-call | flops 35000000512 | tf_op jit(solution)/shard_map/pairs/pallas_call | solution.py:1119
  222.1 3.5 outer_sides_back.1
  227.9 2.5 collective-permute-done.41
  230.6 4.2 %collective-permute-done.39.got_side = bf16[2,128,128]{2,1,0:T(8,128)(2,1)S(1)} collective-permute-done((bf16[2,128,128]{2,1,0:T(8,128)(2,1)S(1)}, bf16[2,128,128]{2,1,0:T(8,128)(2,1)S(1)}, u32[]{:S(2)}, u32[]{:S(2)}) %collective-permute-start.39) | collective-permute-done | bytes 65568 | tf_op jit(solution)/shard_map/ppermute | solution.py:82
  234.9 1.4 collective-permute-start.44
  236.4 1.4 collective-permute-done.45.across_side
  238.6 6.9 %transition_back.1 = (bf16[512,768]{1,0:T(8,128)(2,1)}, bf16[512,768]{1,0:T(8,128)(2,1)}, bf16[512,768]{1,0:T(8,128)(2,1)}, f32[256,768]{1,0:T(8,128)}, bf16[256,768]{1,0:T(8,128)(2,1)}) custom-call(bf16[128,768]{1,0:T(8,128)(2,1)} %get-tuple-element.364.own_ref, bf16[128,768]{1,0:T(8,128)(2,1)} %copy-done.25, bf16[256,768]{1,0:T(8,128)(2,1)} %copy-done.85, ...), custom_call_target="tpu_custom_call" | custom-call | flops 6000000000 | tf_op jit(solution)/shard_map/transition_back/pallas_call | solution.py:64
  247.7 6.1 %transition_grads.1 = (bf16[96,2304]{1,0:T(8,128)(2,1)}, bf16[96,2304]{1,0:T(8,128)(2,1)}, bf16[96,2304]{1,0:T(8,128)(2,1)}, bf16[96,2304]{1,0:T(8,128)(2,1)}, b...) custom-call(s32[2]{0:T(128)} %pad_add_fusion.place_ref, ...), custom_call_target="tpu_custom_call" | custom-call | flops 5000000000 | tf_op jit(solution)/shard_map/transition_grads/pallas_call | solution.py:64
  254.6 10.4 %attention_back.1 = (bf16[2,128,768]{2,1,0:T(8,128)(2,1)}, bf16[2,128,768]{2,1,0:T(8,128)(2,1)}, bf16[4,384,32]{2,1,0:T(8,128)(2,1)}, f32[128,768]{1,0:T(8,128)}, f32[4,3840]{1,0:T(4,128)}) custom-call(s32[4]{0:T(128)} %lengths_ref.9, s32[2]{0:T(128)} %pad_add_fusion.place_ref, f32[256,768]{1,0:T(8,128)} %copy-done.4, bf16[128,768]{1,0:T(8,128)(2,1)} %copy-done.89, ...), custom_call_target="tpu_custom_call" | custom-call | flops 8999999488 | tf_op jit(solution)/shard_map/attention_back/pallas_call | solution.py:64
  267.2 1.4 collective-permute-start.49
  268.6 9.0 %collective-permute-done.49 = bf16[8,16,1664]{2,1,0:T(8,128)(2,1)S(1)} collective-permute-done((bf16[8,16,1664]{2,1,0:T(8,128)(2,1)}, bf16[8,16,1664]{2,1,0:T(8,128)(2,1)S(1)}, u32[]{:S(2)}, u32[]{:S(2)}) %collective-permute-start.49) | collective-permute-done | bytes 426016 | tf_op jit(solution)/shard_map/ppermute | solution.py:82
  278.1 1.9 add_convert_fusion.3
  280.0 2.0 collective-permute-start.50
  282.8 8.1 %all-to-all-start.4 = ((bf16[8,4,4608]{2,1,0:T(4,128)(2,1)}), bf16[8,4,4608]{2,1,0:T(4,128)(2,1)S(1)}, u32[]{:S(2)}, u32[]{:S(2)}) async-start(bf16[8,4,4608]{2,1,0:T(4,128)(2,1)} %broadcast_in_dim.16), calls=%async_computation.4 | async-start | bytes 589824 | tf_op jit(solution)/shard_map/all_to_all | solution.py:119
  290.8 1.5 collective-permute-start.51
  292.3 1.4 collective-permute-start.52
  293.7 8.8 %pairs_last.1 = (f32[4096,256]{1,0:T(8,128)}, f32[16,256]{1,0:T(8,128)}, f32[1,256]{1,0:T(1,128)}) custom-call(bf16[4096,256]{1,0:T(8,128)(2,1)} %bitcast.204, f32[4096,256]{1,0:T(8,128)} %bitcast.207, bf16[16,4096]{1,0:T(8,128)(2,1)} %pad.10.scores_grad_ref, f32[1,256]{1,0:T(1,128)} %reshape.283.gain_ref, bf16[16,256]{1,0:T(8,128)(2,1)} %pad.9.weight_ref), custom_call_target="tpu_custom_call" | custom-call | flops 8999999488 | tf_op jit(solution)/shard_map/pairs_last/pallas_call | solution.py:1316
  303.8 4.8 %collective-permute-done.53 = bf16[4,16,1664]{2,1,0:T(8,128)(2,1)S(1)} collective-permute-done((bf16[4,16,1664]{2,1,0:T(8,128)(2,1)S(1)}, bf16[4,16,1664]{2,1,0:T(8,128)(2,1)S(1)}, u32[]{:S(2)}, u32[]{:S(2)}) %collective-permute-start.53) | collective-permute-done | bytes 213024 | tf_op jit(solution)/shard_map/ppermute | solution.py:82
  313.3 3.9 collective-permute-start.54
  319.2 4.3 %all-to-all-start.5 = ((bf16[8,32,96]{2,1,0:T(8,128)(2,1)}), bf16[8,32,96]{2,1,0:T(8,128)(2,1)S(1)}, u32[]{:S(2)}, u32[]{:S(2)}) async-start(bf16[8,32,96]{2,1,0:T(8,128)(2,1)} %broadcast_in_dim.17), calls=%async_computation.5 | async-start | bytes 131072 | tf_op jit(solution)/shard_map/all_to_all | solution.py:119
  324.8 1.7 collective-permute-start.58
  326.6 3.9 collective-permute-done.58
  331.0 4.0 attention_grads.1
  335.8 1.6 collective-permute-start.62
  339.0 1.4 collective-permute-done.65
  341.8 10.0 %collective-permute-done.64 = bf16[16,1664]{1,0:T(8,128)(2,1)S(1)} collective-permute-done((bf16[16,1664]{1,0:T(8,128)(2,1)S(1)}, bf16[16,1664]{1,0:T(8,128)(2,1)S(1)}, u32[]{:S(2)}, u32[]{:S(2)}) %collective-permute-start.64) | collective-permute-done | bytes 53280 | tf_op jit(solution)/shard_map/ppermute | solution.py:114
  356.5 1.4 collective-permute-done.71
  360.9 1.9 collective-permute-done.72
  362.7 3.0 collective-permute-done.73
  366.2 2.3 collective-permute-start.74
  370.3 1.5 collective-permute-start.79
  375.4 2.4 collective-permute-done.79
  380.8 2.1 collective-permute-done.81
  382.9 2.1 collective-permute-done.82
  384.9 2.0 collective-permute-done.83
  388.3 1.6 collective-permute-start.85
  391.7 2.3 collective-permute-start.86
  395.9 10.1 %finish.1 = (f32[96,6144]{1,0:T(8,128)}, f32[384,768]{1,0:T(8,128)}, f32[96,2304]{1,0:T(8,128)}, f32[96,768]{1,0:T(8,128)}, f32[96,512]{1,0:T(8,128)}, /*index=5...) custom-call(s32[2]{0:T(128)} %pad_add_fusion.place_ref, bf16[96,2304]{1,0:T(8,128)(2,1)} %copy-done.11, ...), custom_call_target="tpu_custom_call" | custom-call | flops 8000000000 | tf_op jit(solution)/shard_map/finish/pallas_call | solution.py:64
  (505 shorter events, 100.6 us)
Async XLA Ops:
  2.7 15.3 %collective-permute-start = (bf16[48,1536]{1,0:T(8,128)(2,1)S(1)}, bf16[48,1536]{1,0:T(8,128)(2,1)}, u32[]{:S(2)}, u32[]{:S(2)}) collective-permute-start(bf16[48,1536]{1,0:T(8,128)(2,1)S(1)} %get-tuple-element.529.refs_0_), channel_id=1, source_target_pairs={{0,1},{1,0},{2,3},{3,2},{4,5},{5,4},{6,7},{7,6},{8,9},{9,8},{10,11... | collective-permute-start | bytes 442376 | tf_op jit(solution)/shard_map/ppermute | solution.py:82
  4.8 13.3 %collective-permute-start.1 = (bf16[48,1536]{1,0:T(8,128)(2,1)S(1)}, bf16[48,1536]{1,0:T(8,128)(2,1)S(1)}, u32[]{:S(2)}, u32[]{:S(2)}) collective-permute-start(bf16[48,1536]{1,0:T(8,128)(2,1)S(1)} %get-tuple-element.529.refs_0_), channel_id=1, source_target_pairs={{0,2},{1,3},{2,4},{3,5},{4,6},{5,7},{6,0},{7,1},{8,10},{9,11},{10,... | collective-permute-start | bytes 442376 | tf_op jit(solution)/shard_map/ppermute | solution.py:114
  9.0 9.0 %all-to-all-start = ((f32[8,1,552]{2,1,0:T(1,128)}), f32[8,1,552]{2,1,0:T(1,128)S(1)}, u32[]{:S(2)}, u32[]{:S(2)}) async-start(f32[8,1,552]{2,1,0:T(1,128)} %broadcast_in_dim.15), calls=%async_computation | async-start | bytes 40960 | tf_op jit(solution)/shard_map/all_to_all | solution.py:119
  19.5 19.5 %collective-permute-start.5 = (bf16[96,2304]{1,0:T(8,128)(2,1)S(1)}, bf16[96,2304]{1,0:T(8,128)(2,1)S(1)}, u32[]{:S(2)}, u32[]{:S(2)}) collective-permute-start(bf16[96,2304]{1,0:T(8,128)(2,1)S(1)} %pad_maximum_fusion.5.refs_0_), channel_id=1, source_target_pairs={{0,1},{1,0},{2,3},{3,2},{4,5},{5,4},{6,7},{7,6},{8,9},{9,8},{10,11... | collective-permute-start | bytes 1327112 | tf_op jit(solution)/shard_map/ppermute | solution.py:82
  20.6 18.4 %collective-permute-start.6 = (bf16[96,2304]{1,0:T(8,128)(2,1)S(1)}, bf16[96,2304]{1,0:T(8,128)(2,1)}, u32[]{:S(2)}, u32[]{:S(2)}) collective-permute-start(bf16[96,2304]{1,0:T(8,128)(2,1)S(1)} %pad_maximum_fusion.5.refs_0_), channel_id=1, source_target_pairs={{0,2},{1,3},{2,4},{3,5},{4,6},{5,7},{6,0},{7,1},{8,10},{9,11},{10,... | collective-permute-start | bytes 1327112 | tf_op jit(solution)/shard_map/ppermute | solution.py:114
  21.8 17.1 %collective-permute-start.2 = (bf16[48,1536]{1,0:T(8,128)(2,1)S(1)}, bf16[48,1536]{1,0:T(8,128)(2,1)S(1)}, u32[]{:S(2)}, u32[]{:S(2)}) collective-permute-start(bf16[48,1536]{1,0:T(8,128)(2,1)S(1)} %collective-permute-done.1.refs_4_), channel_id=1, source_target_pairs={{0,1},{1,0},{2,3},{3,2},{4,5},{5,4},{6,7},{7,6},{8,9},{9,8},{10,11... | collective-permute-start | bytes 442376 | tf_op jit(solution)/shard_map/ppermute | solution.py:82
  22.1 16.9 %collective-permute-start.3 = (bf16[48,1536]{1,0:T(8,128)(2,1)S(1)}, bf16[48,1536]{1,0:T(8,128)(2,1)S(1)}, u32[]{:S(2)}, u32[]{:S(2)}) collective-permute-start(bf16[48,1536]{1,0:T(8,128)(2,1)S(1)} %collective-permute-done.1.refs_4_), channel_id=1, source_target_pairs={{0,2},{1,3},{2,4},{3,5},{4,6},{5,7},{6,0},{7,1},{8,10},{9,11},{10,... | collective-permute-start | bytes 442376 | tf_op jit(solution)/shard_map/ppermute | solution.py:114
  23.3 15.7 %collective-permute-start.4 = (bf16[48,1536]{1,0:T(8,128)(2,1)}, bf16[48,1536]{1,0:T(8,128)(2,1)S(1)}, u32[]{:S(2)}, u32[]{:S(2)}) collective-permute-start(bf16[48,1536]{1,0:T(8,128)(2,1)} %collective-permute-done.refs_1_), channel_id=1, source_target_pairs={{0,16},{8,24},{16,0},{24,8},{1,17},{9,25},{17,1},{25,9},{2,18},{10... | collective-permute-start | bytes 442376 | tf_op jit(solution)/shard_map/ppermute | solution.py:82
  24.5 14.5 %all-to-all-start.1 = ((bf16[8,32,96]{2,1,0:T(8,128)(2,1)}), bf16[8,32,96]{2,1,0:T(8,128)(2,1)S(1)}, u32[]{:S(2)}, u32[]{:S(2)}) async-start(bf16[8,32,96]{2,1,0:T(8,128)(2,1)} %bitcast.149), calls=%async_computation.1 | async-start | bytes 131072 | tf_op jit(solution)/shard_map/all_to_all | solution.py:119
  40.8 22.5 %all-to-all-start.2 = ((f32[8,4,1536]{2,1,0:T(4,128)}), f32[8,4,1536]{2,1,0:T(4,128)S(1)}, u32[]{:S(2)}, u32[]{:S(2)}) async-start(f32[8,4,1536]{2,1,0:T(4,128)} %copy.92), calls=%async_computation.2 | async-start | bytes 393216 | tf_op jit(solution)/shard_map/all_to_all | solution.py:119
  44.2 19.1 %collective-permute-start.10 = (bf16[96,2304]{1,0:T(8,128)(2,1)}, bf16[96,2304]{1,0:T(8,128)(2,1)}, u32[]{:S(2)}, u32[]{:S(2)}) collective-permute-start(bf16[96,2304]{1,0:T(8,128)(2,1)} %collective-permute-done.6.refs_2_), channel_id=1, source_target_pairs={{0,1},{1,0},{2,3},{3,2},{4,5},{5,4},{6,7},{7,6},{8,9},{9,8},{10,11... | collective-permute-start | bytes 1327112 | tf_op jit(solution)/shard_map/ppermute | solution.py:82
  45.6 17.8 %collective-permute-start.11 = (bf16[96,2304]{1,0:T(8,128)(2,1)}, bf16[96,2304]{1,0:T(8,128)(2,1)}, u32[]{:S(2)}, u32[]{:S(2)}) collective-permute-start(bf16[96,2304]{1,0:T(8,128)(2,1)} %collective-permute-done.6.refs_2_), channel_id=1, source_target_pairs={{0,2},{1,3},{2,4},{3,5},{4,6},{5,7},{6,0},{7,1},{8,10},{9,11},{10,... | collective-permute-start | bytes 1327112 | tf_op jit(solution)/shard_map/ppermute | solution.py:114
  46.8 13.8 %collective-permute-start.7 = (bf16[48,1536]{1,0:T(8,128)(2,1)S(1)}, bf16[48,1536]{1,0:T(8,128)(2,1)S(1)}, u32[]{:S(2)}, u32[]{:S(2)}) collective-permute-start(bf16[48,1536]{1,0:T(8,128)(2,1)S(1)} %collective-permute-done.3.refs_7_), channel_id=1, source_target_pairs={{0,1},{1,0},{2,3},{3,2},{4,5},{5,4},{6,7},{7,6},{8,9},{9,8},{10,11... | collective-permute-start | bytes 442376 | tf_op jit(solution)/shard_map/ppermute | solution.py:82
  47.1 16.2 %collective-permute-start.8 = (bf16[48,1536]{1,0:T(8,128)(2,1)S(1)}, bf16[48,1536]{1,0:T(8,128)(2,1)S(1)}, u32[]{:S(2)}, u32[]{:S(2)}) collective-permute-start(bf16[48,1536]{1,0:T(8,128)(2,1)S(1)} %collective-permute-done.3.refs_7_), channel_id=1, source_target_pairs={{0,2},{1,3},{2,4},{3,5},{4,6},{5,7},{6,0},{7,1},{8,10},{9,11},{10,... | collective-permute-start | bytes 442376 | tf_op jit(solution)/shard_map/ppermute | solution.py:114
  48.3 15.0 %collective-permute-start.9 = (bf16[2,48,1536]{2,1,0:T(8,128)(2,1)S(1)}, bf16[2,48,1536]{2,1,0:T(8,128)(2,1)S(1)}, u32[]{:S(2)}, u32[]{:S(2)}) collective-permute-start(bf16[2,48,1536]{2,1,0:T(8,128)(2,1)S(1)} %pad_maximum_fusion.11), channel_id=1, source_target_pairs={{0,16},{8,24},{16,0},{24,8},{1,17},{9,25},{17,1},{25,9},{2,18},{10... | collective-permute-start | bytes 884744 | tf_op jit(solution)/shard_map/ppermute | solution.py:82
  64.4 26.4 %all-to-all-start.3 = ((f32[8,4,3072]{2,1,0:T(4,128)}), f32[8,4,3072]{2,1,0:T(4,128)S(1)}, u32[]{:S(2)}, u32[]{:S(2)}) async-start(f32[8,4,3072]{2,1,0:T(4,128)} %copy.93), calls=%async_computation.3 | async-start | bytes 786432 | tf_op jit(solution)/shard_map/all_to_all | solution.py:119
  67.9 22.1 %collective-permute-start.14 = (bf16[96,2304]{1,0:T(8,128)(2,1)}, bf16[96,2304]{1,0:T(8,128)(2,1)S(1)}, u32[]{:S(2)}, u32[]{:S(2)}) collective-permute-start(bf16[96,2304]{1,0:T(8,128)(2,1)} %collective-permute-done.11.refs_4_), channel_id=1, source_target_pairs={{0,1},{1,0},{2,3},{3,2},{4,5},{5,4},{6,7},{7,6},{8,9},{9,8},{10,11... | collective-permute-start | bytes 1327112 | tf_op jit(solution)/shard_map/ppermute | solution.py:82
  69.2 21.6 %collective-permute-start.15 = (bf16[96,2304]{1,0:T(8,128)(2,1)}, bf16[96,2304]{1,0:T(8,128)(2,1)}, u32[]{:S(2)}, u32[]{:S(2)}) collective-permute-start(bf16[96,2304]{1,0:T(8,128)(2,1)} %collective-permute-done.11.refs_4_), channel_id=1, source_target_pairs={{0,2},{1,3},{2,4},{3,5},{4,6},{5,7},{6,0},{7,1},{8,10},{9,11},{10,... | collective-permute-start | bytes 1327112 | tf_op jit(solution)/shard_map/ppermute | solution.py:114
  70.4 19.5 %collective-permute-start.13 = (bf16[2,48,1536]{2,1,0:T(8,128)(2,1)S(1)}, bf16[2,48,1536]{2,1,0:T(8,128)(2,1)S(1)}, u32[]{:S(2)}, u32[]{:S(2)}) collective-permute-start(bf16[2,48,1536]{2,1,0:T(8,128)(2,1)S(1)} %pad_maximum_fusion.12), channel_id=1, source_target_pairs={{0,16},{8,24},{16,0},{24,8},{1,17},{9,25},{17,1},{25,9},{2,18},{10... | collective-permute-start | bytes 884744 | tf_op jit(solution)/shard_map/ppermute | solution.py:82
  71.6 12.9 %collective-permute-start.16 = (bf16[16,2432]{1,0:T(8,128)(2,1)S(1)}, bf16[16,2432]{1,0:T(8,128)(2,1)S(1)}, u32[]{:S(2)}, u32[]{:S(2)}) collective-permute-start(bf16[16,2432]{1,0:T(8,128)(2,1)S(1)} %get-tuple-element.297.refs_0_), channel_id=1, source_target_pairs={{0,1},{1,0},{2,3},{3,2},{4,5},{5,4},{6,7},{7,6},{8,9},{9,8},{10,11... | collective-permute-start | bytes 233480 | tf_op jit(solution)/shard_map/ppermute | solution.py:82
  71.9 18.0 %collective-permute-start.12 = (bf16[48,1536]{1,0:T(8,128)(2,1)S(1)}, bf16[48,1536]{1,0:T(8,128)(2,1)S(1)}, u32[]{:S(2)}, u32[]{:S(2)}) collective-permute-start(bf16[48,1536]{1,0:T(8,128)(2,1)S(1)} %collective-permute-done.8.refs_10_), channel_id=1, source_target_pairs={{0,1},{1,0},{2,3},{3,2},{4,5},{5,4},{6,7},{7,6},{8,9},{9,8},{10,11... | collective-permute-start | bytes 442376 | tf_op jit(solution)/shard_map/ppermute | solution.py:82
  90.9 9.3 %collective-permute-start.19 = (bf16[96,2304]{1,0:T(8,128)(2,1)}, bf16[96,2304]{1,0:T(8,128)(2,1)S(1)}, u32[]{:S(2)}, u32[]{:S(2)}) collective-permute-start(bf16[96,2304]{1,0:T(8,128)(2,1)} %collective-permute-done.15.refs_6_), channel_id=1, source_target_pairs={{0,1},{1,0},{2,3},{3,2},{4,5},{5,4},{6,7},{7,6},{8,9},{9,8},{10,11... | collective-permute-start | bytes 1327112 | tf_op jit(solution)/shard_map/ppermute | solution.py:82
  91.4 8.8 %collective-permute-start.18 = (bf16[2,48,1536]{2,1,0:T(8,128)(2,1)S(1)}, bf16[2,48,1536]{2,1,0:T(8,128)(2,1)S(1)}, u32[]{:S(2)}, u32[]{:S(2)}) collective-permute-start(bf16[2,48,1536]{2,1,0:T(8,128)(2,1)S(1)} %pad_maximum_fusion.13), channel_id=1, source_target_pairs={{0,16},{8,24},{16,0},{24,8},{1,17},{9,25},{17,1},{25,9},{2,18},{10... | collective-permute-start | bytes 884744 | tf_op jit(solution)/shard_map/ppermute | solution.py:82
  92.6 7.6 %collective-permute-start.20 = (bf16[16,2432]{1,0:T(8,128)(2,1)S(1)}, bf16[16,2432]{1,0:T(8,128)(2,1)S(1)}, u32[]{:S(2)}, u32[]{:S(2)}) collective-permute-start(bf16[16,2432]{1,0:T(8,128)(2,1)S(1)} %collective-permute-done.17.refs_4_), channel_id=1, source_target_pairs={{0,1},{1,0},{2,3},{3,2},{4,5},{5,4},{6,7},{7,6},{8,9},{9,8},{10,11... | collective-permute-start | bytes 233480 | tf_op jit(solution)/shard_map/ppermute | solution.py:82
  93.6 6.6 %collective-permute-start.21 = (bf16[16,2432]{1,0:T(8,128)(2,1)S(1)}, bf16[16,2432]{1,0:T(8,128)(2,1)S(1)}, u32[]{:S(2)}, u32[]{:S(2)}) collective-permute-start(bf16[16,2432]{1,0:T(8,128)(2,1)S(1)} %collective-permute-done.17.refs_4_), channel_id=1, source_target_pairs={{0,2},{1,3},{2,4},{3,5},{4,6},{5,7},{6,0},{7,1},{8,10},{9,11},{10,... | collective-permute-start | bytes 233480 | tf_op jit(solution)/shard_map/ppermute | solution.py:114
  93.6 6.6 %collective-permute-start.22 = (bf16[16,2432]{1,0:T(8,128)(2,1)S(1)}, bf16[16,2432]{1,0:T(8,128)(2,1)S(1)}, u32[]{:S(2)}, u32[]{:S(2)}) collective-permute-start(bf16[16,2432]{1,0:T(8,128)(2,1)S(1)} %collective-permute-done.16.refs_1_), channel_id=1, source_target_pairs={{0,16},{8,24},{16,0},{24,8},{1,17},{9,25},{17,1},{25,9},{2,18},{10... | collective-permute-start | bytes 233480 | tf_op jit(solution)/shard_map/ppermute | solution.py:82
  104.3 22.0 %collective-permute-start.23 = (bf16[768,1536]{1,0:T(8,128)(2,1)}, bf16[768,1536]{1,0:T(8,128)(2,1)}, u32[]{:S(2)}, u32[]{:S(2)}) collective-permute-start(bf16[768,1536]{1,0:T(8,128)(2,1)} %bitcast.200), channel_id=1, source_target_pairs={{0,8},{8,0},{16,24},{24,16},{1,9},{9,1},{17,25},{25,17},{2,10},{10... | collective-permute-start | bytes 7077896 | tf_op jit(solution)/shard_map/ppermute | solution.py:82
  126.3 9.5 %collective-permute-start.27 = (bf16[16,2432]{1,0:T(8,128)(2,1)S(1)}, bf16[16,2432]{1,0:T(8,128)(2,1)S(1)}, u32[]{:S(2)}, u32[]{:S(2)}) collective-permute-start(bf16[16,2432]{1,0:T(8,128)(2,1)S(1)} %collective-permute-done.25.refs_10_), channel_id=1, source_target_pairs={{0,1},{1,0},{2,3},{3,2},{4,5},{5,4},{6,7},{7,6},{8,9},{9,8},{10,11... | collective-permute-start | bytes 233480 | tf_op jit(solution)/shard_map/ppermute | solution.py:82
  127.4 8.4 %collective-permute-start.28 = (bf16[2,16,2432]{2,1,0:T(8,128)(2,1)S(1)}, bf16[2,16,2432]{2,1,0:T(8,128)(2,1)S(1)}, u32[]{:S(2)}, u32[]{:S(2)}) collective-permute-start(bf16[2,16,2432]{2,1,0:T(8,128)(2,1)S(1)} %pad_maximum_fusion.16), channel_id=1, source_target_pairs={{0,16},{8,24},{16,0},{24,8},{1,17},{9,25},{17,1},{25,9},{2,18},{10... | collective-permute-start | bytes 466952 | tf_op jit(solution)/shard_map/ppermute | solution.py:82
  135.9 8.3 %collective-permute-start.29 = (bf16[128,768]{1,0:T(8,128)(2,1)}, bf16[128,768]{1,0:T(8,128)(2,1)S(1)}, u32[]{:S(2)}, u32[]{:S(2)}) collective-permute-start(bf16[128,768]{1,0:T(8,128)(2,1)} %get-tuple-element.326.own_ref), channel_id=1, source_target_pairs={{0,16},{8,24},{16,0},{24,8},{1,17},{9,25},{17,1},{25,9},{2,18},{10... | collective-permute-start | bytes 589832 | tf_op jit(solution)/shard_map/ppermute | solution.py:82
  136.2 8.0 %collective-permute-start.30 = (bf16[2,16,2432]{2,1,0:T(8,128)(2,1)S(1)}, bf16[2,16,2432]{2,1,0:T(8,128)(2,1)S(1)}, u32[]{:S(2)}, u32[]{:S(2)}) collective-permute-start(bf16[2,16,2432]{2,1,0:T(8,128)(2,1)S(1)} %pad_maximum_fusion.17), channel_id=1, source_target_pairs={{0,16},{8,24},{16,0},{24,8},{1,17},{9,25},{17,1},{25,9},{2,18},{10... | collective-permute-start | bytes 466952 | tf_op jit(solution)/shard_map/ppermute | solution.py:82
  147.9 10.1 %collective-permute-start.32 = (bf16[256,2432]{1,0:T(8,128)(2,1)}, bf16[256,2432]{1,0:T(8,128)(2,1)S(1)}, u32[]{:S(2)}, u32[]{:S(2)}) collective-permute-start(bf16[256,2432]{1,0:T(8,128)(2,1)} %bitcast.163), channel_id=1, source_target_pairs={{0,8},{8,0},{16,24},{24,16},{1,9},{9,1},{17,25},{25,17},{2,10},{10... | collective-permute-start | bytes 3735560 | tf_op jit(solution)/shard_map/ppermute | solution.py:82
  167.8 6.6 %collective-permute-start.34 = (bf16[128,768]{1,0:T(8,128)(2,1)}, bf16[128,768]{1,0:T(8,128)(2,1)}, u32[]{:S(2)}, u32[]{:S(2)}) collective-permute-start(bf16[128,768]{1,0:T(8,128)(2,1)} %slice.194), channel_id=1, source_target_pairs={{0,16},{8,24},{16,0},{24,8},{1,17},{9,25},{17,1},{25,9},{2,18},{10... | collective-permute-start | bytes 589832 | tf_op jit(solution)/shard_map/ppermute | solution.py:82
  177.1 48.6 %collective-permute-start.35 = (bf16[2,128,768]{2,1,0:T(8,128)(2,1)S(1)}, bf16[2,128,768]{2,1,0:T(8,128)(2,1)S(1)}, u32[]{:S(2)}, u32[]{:S(2)}) collective-permute-start(bf16[2,128,768]{2,1,0:T(8,128)(2,1)S(1)} %copy-done.16), channel_id=1, source_target_pairs={{0,16},{8,24},{16,0},{24,8},{1,17},{9,25},{17,1},{25,9},{2,18},{10... | collective-permute-start | bytes 1179656 | tf_op jit(solution)/shard_map/ppermute | solution.py:82
  177.3 48.3 %collective-permute-start.36 = (f32[32,98]{1,0:T(8,128)S(1)}, f32[32,98]{1,0:T(8,128)S(1)}, u32[]{:S(2)}, u32[]{:S(2)}) collective-permute-start(f32[32,98]{1,0:T(8,128)S(1)} %pad_maximum_fusion.25), channel_id=1, source_target_pairs={{0,16},{8,24},{16,0},{24,8},{1,17},{9,25},{17,1},{25,9},{2,18},{10... | collective-permute-start | bytes 37640 | tf_op jit(solution)/shard_map/ppermute | solution.py:82
  178.5 47.1 %collective-permute-start.37 = (bf16[128,768]{1,0:T(8,128)(2,1)}, bf16[128,768]{1,0:T(8,128)(2,1)S(1)}, u32[]{:S(2)}, u32[]{:S(2)}) collective-permute-start(bf16[128,768]{1,0:T(8,128)(2,1)} %get-tuple-element.359.outer_own), channel_id=1, source_target_pairs={{0,16},{8,24},{16,0},{24,8},{1,17},{9,25},{17,1},{25,9},{2,18},{10... | collective-permute-start | bytes 589832 | tf_op jit(solution)/shard_map/ppermute | solution.py:82
  226.9 7.9 %collective-permute-start.43 = (bf16[256,1664]{1,0:T(8,128)(2,1)S(1)}, bf16[256,1664]{1,0:T(8,128)(2,1)S(1)}, u32[]{:S(2)}, u32[]{:S(2)}) collective-permute-start(bf16[256,1664]{1,0:T(8,128)(2,1)S(1)} %copy-done.75), channel_id=1, source_target_pairs={{0,8},{8,0},{16,24},{24,16},{1,9},{9,1},{17,25},{25,17},{2,10},{10... | collective-permute-start | bytes 2555912 | tf_op jit(solution)/shard_map/ppermute | solution.py:82
  226.9 7.9 %collective-permute-start.40 = (bf16[2,128,768]{2,1,0:T(8,128)(2,1)S(1)}, bf16[2,128,768]{2,1,0:T(8,128)(2,1)S(1)}, u32[]{:S(2)}, u32[]{:S(2)}) collective-permute-start(bf16[2,128,768]{2,1,0:T(8,128)(2,1)S(1)} %pad_maximum_fusion.7), channel_id=1, source_target_pairs={{0,8},{8,0},{16,24},{24,16},{1,9},{9,1},{17,25},{25,17},{2,10},{10... | collective-permute-start | bytes 1179656 | tf_op jit(solution)/shard_map/ppermute | solution.py:82
  227.4 7.4 %collective-permute-start.42 = (bf16[256,768]{1,0:T(8,128)(2,1)S(1)}, bf16[256,768]{1,0:T(8,128)(2,1)S(1)}, u32[]{:S(2)}, u32[]{:S(2)}) collective-permute-start(bf16[256,768]{1,0:T(8,128)(2,1)S(1)} %pad_maximum_fusion.8), channel_id=1, source_target_pairs={{0,8},{8,0},{16,24},{24,16},{1,9},{9,1},{17,25},{25,17},{2,10},{10... | collective-permute-start | bytes 1179656 | tf_op jit(solution)/shard_map/ppermute | solution.py:82
  227.4 7.4 %collective-permute-start.38 = (bf16[128,768]{1,0:T(8,128)(2,1)S(1)}, bf16[128,768]{1,0:T(8,128)(2,1)S(1)}, u32[]{:S(2)}, u32[]{:S(2)}) collective-permute-start(bf16[128,768]{1,0:T(8,128)(2,1)S(1)} %copy-done.22), channel_id=1, source_target_pairs={{0,16},{8,24},{16,0},{24,8},{1,17},{9,25},{17,1},{25,9},{2,18},{10... | collective-permute-start | bytes 589832 | tf_op jit(solution)/shard_map/ppermute | solution.py:82
  247.7 6.2 %collective-permute-start.47 = (bf16[128,768]{1,0:T(8,128)(2,1)S(1)}, bf16[128,768]{1,0:T(8,128)(2,1)S(1)}, u32[]{:S(2)}, u32[]{:S(2)}) collective-permute-start(bf16[128,768]{1,0:T(8,128)(2,1)S(1)} %slice.193), channel_id=1, source_target_pairs={{0,16},{8,24},{16,0},{24,8},{1,17},{9,25},{17,1},{25,9},{2,18},{10... | collective-permute-start | bytes 589832 | tf_op jit(solution)/shard_map/ppermute | solution.py:82
  267.2 10.8 %collective-permute-start.48 = (bf16[96,2304]{1,0:T(8,128)(2,1)}, bf16[96,2304]{1,0:T(8,128)(2,1)S(1)}, u32[]{:S(2)}, u32[]{:S(2)}) collective-permute-start(bf16[96,2304]{1,0:T(8,128)(2,1)} %get-tuple-element.405), channel_id=1, source_target_pairs={{0,1},{1,0},{2,3},{3,2},{4,5},{5,4},{6,7},{7,6},{8,9},{9,8},{10,11... | collective-permute-start | bytes 1327112 | tf_op jit(solution)/shard_map/ppermute | solution.py:82
  267.2 10.4 %collective-permute-start.49 = (bf16[8,16,1664]{2,1,0:T(8,128)(2,1)}, bf16[8,16,1664]{2,1,0:T(8,128)(2,1)S(1)}, u32[]{:S(2)}, u32[]{:S(2)}) collective-permute-start(bf16[8,16,1664]{2,1,0:T(8,128)(2,1)} %fusion.5), channel_id=1, source_target_pairs={{0,16},{8,24},{16,0},{24,8},{1,17},{9,25},{17,1},{25,9},{2,18},{10... | collective-permute-start | bytes 1277960 | tf_op jit(solution)/shard_map/ppermute | solution.py:82
  280.0 28.7 %collective-permute-start.50 = (bf16[2,128,768]{2,1,0:T(8,128)(2,1)}, bf16[2,128,768]{2,1,0:T(8,128)(2,1)}, u32[]{:S(2)}, u32[]{:S(2)}) collective-permute-start(bf16[2,128,768]{2,1,0:T(8,128)(2,1)} %get-tuple-element.409), channel_id=1, source_target_pairs={{0,16},{8,24},{16,0},{24,8},{1,17},{9,25},{17,1},{25,9},{2,18},{10... | collective-permute-start | bytes 1179656 | tf_op jit(solution)/shard_map/ppermute | solution.py:82
  282.8 26.7 %all-to-all-start.4 = ((bf16[8,4,4608]{2,1,0:T(4,128)(2,1)}), bf16[8,4,4608]{2,1,0:T(4,128)(2,1)S(1)}, u32[]{:S(2)}, u32[]{:S(2)}) async-start(bf16[8,4,4608]{2,1,0:T(4,128)(2,1)} %broadcast_in_dim.16), calls=%async_computation.4 | async-start | bytes 589824 | tf_op jit(solution)/shard_map/all_to_all | solution.py:119
  290.8 17.8 %collective-permute-start.51 = (bf16[96,2304]{1,0:T(8,128)(2,1)}, bf16[96,2304]{1,0:T(8,128)(2,1)S(1)}, u32[]{:S(2)}, u32[]{:S(2)}) collective-permute-start(bf16[96,2304]{1,0:T(8,128)(2,1)} %get-tuple-element.411), channel_id=1, source_target_pairs={{0,1},{1,0},{2,3},{3,2},{4,5},{5,4},{6,7},{7,6},{8,9},{9,8},{10,11... | collective-permute-start | bytes 1327112 | tf_op jit(solution)/shard_map/ppermute | solution.py:82
  292.3 16.4 %collective-permute-start.52 = (bf16[96,2304]{1,0:T(8,128)(2,1)}, bf16[96,2304]{1,0:T(8,128)(2,1)S(1)}, u32[]{:S(2)}, u32[]{:S(2)}) collective-permute-start(bf16[96,2304]{1,0:T(8,128)(2,1)} %add_convert_fusion.3), channel_id=1, source_target_pairs={{0,2},{1,3},{2,4},{3,5},{4,6},{5,7},{6,0},{7,1},{8,10},{9,11},{10,... | collective-permute-start | bytes 1327112 | tf_op jit(solution)/shard_map/ppermute | solution.py:114
  302.5 6.2 %collective-permute-start.53 = (bf16[4,16,1664]{2,1,0:T(8,128)(2,1)S(1)}, bf16[4,16,1664]{2,1,0:T(8,128)(2,1)S(1)}, u32[]{:S(2)}, u32[]{:S(2)}) collective-permute-start(bf16[4,16,1664]{2,1,0:T(8,128)(2,1)S(1)} %dynamic-slice_bitcast_fusion), channel_id=1, source_target_pairs={{0,1},{1,0},{2,3},{3,2},{4,5},{5,4},{6,7},{7,6},{8,9},{9,8},{10,11... | collective-permute-start | bytes 638984 | tf_op jit(solution)/shard_map/ppermute | solution.py:82
  312.0 18.4 %collective-permute-start.56 = (bf16[96,2304]{1,0:T(8,128)(2,1)}, bf16[96,2304]{1,0:T(8,128)(2,1)S(1)}, u32[]{:S(2)}, u32[]{:S(2)}) collective-permute-start(bf16[96,2304]{1,0:T(8,128)(2,1)} %get-tuple-element.428), channel_id=1, source_target_pairs={{0,1},{1,0},{2,3},{3,2},{4,5},{5,4},{6,7},{7,6},{8,9},{9,8},{10,11... | collective-permute-start | bytes 1327112 | tf_op jit(solution)/shard_map/ppermute | solution.py:82
  312.5 17.9 %collective-permute-start.57 = (bf16[96,2304]{1,0:T(8,128)(2,1)S(1)}, bf16[96,2304]{1,0:T(8,128)(2,1)S(1)}, u32[]{:S(2)}, u32[]{:S(2)}) collective-permute-start(bf16[96,2304]{1,0:T(8,128)(2,1)S(1)} %add_convert_fusion.2), channel_id=1, source_target_pairs={{0,2},{1,3},{2,4},{3,5},{4,6},{5,7},{6,0},{7,1},{8,10},{9,11},{10,... | collective-permute-start | bytes 1327112 | tf_op jit(solution)/shard_map/ppermute | solution.py:114
  313.3 17.1 %collective-permute-start.54 = (bf16[2,128,768]{2,1,0:T(8,128)(2,1)}, bf16[2,128,768]{2,1,0:T(8,128)(2,1)}, u32[]{:S(2)}, u32[]{:S(2)}) collective-permute-start(bf16[2,128,768]{2,1,0:T(8,128)(2,1)} %pad_maximum_fusion.10), channel_id=1, source_target_pairs={{0,8},{8,0},{16,24},{24,16},{1,9},{9,1},{17,25},{25,17},{2,10},{10... | collective-permute-start | bytes 1179656 | tf_op jit(solution)/shard_map/ppermute | solution.py:82
  317.3 13.1 %collective-permute-start.55 = (bf16[32,4608]{1,0:T(8,128)(2,1)S(1)}, bf16[32,4608]{1,0:T(8,128)(2,1)S(1)}, u32[]{:S(2)}, u32[]{:S(2)}) collective-permute-start(bf16[32,4608]{1,0:T(8,128)(2,1)S(1)} %reshape.307), channel_id=1, source_target_pairs={{0,16},{8,24},{16,0},{24,8},{1,17},{9,25},{17,1},{25,9},{2,18},{10... | collective-permute-start | bytes 884744 | tf_op jit(solution)/shard_map/ppermute | solution.py:82
  319.2 11.3 %all-to-all-start.5 = ((bf16[8,32,96]{2,1,0:T(8,128)(2,1)}), bf16[8,32,96]{2,1,0:T(8,128)(2,1)S(1)}, u32[]{:S(2)}, u32[]{:S(2)}) async-start(bf16[8,32,96]{2,1,0:T(8,128)(2,1)} %broadcast_in_dim.17), calls=%async_computation.5 | async-start | bytes 131072 | tf_op jit(solution)/shard_map/all_to_all | solution.py:119
  335.0 16.7 %collective-permute-start.60 = (bf16[2,32,4608]{2,1,0:T(8,128)(2,1)S(1)}, bf16[2,32,4608]{2,1,0:T(8,128)(2,1)S(1)}, u32[]{:S(2)}, u32[]{:S(2)}) collective-permute-start(bf16[2,32,4608]{2,1,0:T(8,128)(2,1)S(1)} %pad_maximum_fusion.2), channel_id=1, source_target_pairs={{0,8},{8,0},{16,24},{24,16},{1,9},{9,1},{17,25},{25,17},{2,10},{10... | collective-permute-start | bytes 1769480 | tf_op jit(solution)/shard_map/ppermute | solution.py:82
  335.8 15.9 %collective-permute-start.62 = (bf16[96,2304]{1,0:T(8,128)(2,1)}, bf16[96,2304]{1,0:T(8,128)(2,1)S(1)}, u32[]{:S(2)}, u32[]{:S(2)}) collective-permute-start(bf16[96,2304]{1,0:T(8,128)(2,1)} %get-tuple-element.447), channel_id=1, source_target_pairs={{0,1},{1,0},{2,3},{3,2},{4,5},{5,4},{6,7},{7,6},{8,9},{9,8},{10,11... | collective-permute-start | bytes 1327112 | tf_op jit(solution)/shard_map/ppermute | solution.py:82
  337.5 14.3 %collective-permute-start.63 = (bf16[96,2304]{1,0:T(8,128)(2,1)S(1)}, bf16[96,2304]{1,0:T(8,128)(2,1)S(1)}, u32[]{:S(2)}, u32[]{:S(2)}) collective-permute-start(bf16[96,2304]{1,0:T(8,128)(2,1)S(1)} %add_convert_fusion.1), channel_id=1, source_target_pairs={{0,2},{1,3},{2,4},{3,5},{4,6},{5,7},{6,0},{7,1},{8,10},{9,11},{10,... | collective-permute-start | bytes 1327112 | tf_op jit(solution)/shard_map/ppermute | solution.py:114
  340.4 11.3 %collective-permute-start.66 = (bf16[96,896]{1,0:T(8,128)(2,1)}, bf16[96,896]{1,0:T(8,128)(2,1)S(1)}, u32[]{:S(2)}, u32[]{:S(2)}) collective-permute-start(bf16[96,896]{1,0:T(8,128)(2,1)} %get-tuple-element.451), channel_id=1, source_target_pairs={{0,1},{1,0},{2,3},{3,2},{4,5},{5,4},{6,7},{7,6},{8,9},{9,8},{10,11... | collective-permute-start | bytes 516104 | tf_op jit(solution)/shard_map/ppermute | solution.py:82
  341.0 10.7 %collective-permute-start.64 = (bf16[16,1664]{1,0:T(8,128)(2,1)S(1)}, bf16[16,1664]{1,0:T(8,128)(2,1)S(1)}, u32[]{:S(2)}, u32[]{:S(2)}) collective-permute-start(bf16[16,1664]{1,0:T(8,128)(2,1)S(1)} %fusion.12), channel_id=1, source_target_pairs={{0,2},{1,3},{2,4},{3,5},{4,6},{5,7},{6,0},{7,1},{8,10},{9,11},{10,... | collective-permute-start | bytes 159752 | tf_op jit(solution)/shard_map/ppermute | solution.py:114
  353.0 7.9 %collective-permute-start.67 = (bf16[2,32,768]{2,1,0:T(8,128)(2,1)S(1)}, bf16[2,32,768]{2,1,0:T(8,128)(2,1)S(1)}, u32[]{:S(2)}, u32[]{:S(2)}) collective-permute-start(bf16[2,32,768]{2,1,0:T(8,128)(2,1)S(1)} %pad_maximum_fusion.18), channel_id=1, source_target_pairs={{0,8},{8,0},{16,24},{24,16},{1,9},{9,1},{17,25},{25,17},{2,10},{10... | collective-permute-start | bytes 294920 | tf_op jit(solution)/shard_map/ppermute | solution.py:82
  354.3 11.7 %collective-permute-start.68 = (bf16[96,2304]{1,0:T(8,128)(2,1)S(1)}, bf16[96,2304]{1,0:T(8,128)(2,1)S(1)}, u32[]{:S(2)}, u32[]{:S(2)}) collective-permute-start(bf16[96,2304]{1,0:T(8,128)(2,1)S(1)} %add_convert_fusion.refs_0_), channel_id=1, source_target_pairs={{0,16},{8,24},{16,0},{24,8},{1,17},{9,25},{17,1},{25,9},{2,18},{10... | collective-permute-start | bytes 1327112 | tf_op jit(solution)/shard_map/ppermute | solution.py:82
  354.5 11.5 %collective-permute-start.69 = (bf16[96,2304]{1,0:T(8,128)(2,1)S(1)}, bf16[96,2304]{1,0:T(8,128)(2,1)S(1)}, u32[]{:S(2)}, u32[]{:S(2)}) collective-permute-start(bf16[96,2304]{1,0:T(8,128)(2,1)S(1)} %add_convert_fusion.refs_0_), channel_id=1, source_target_pairs={{0,8},{8,0},{16,24},{24,16},{1,9},{9,1},{17,25},{25,17},{2,10},{10... | collective-permute-start | bytes 1327112 | tf_op jit(solution)/shard_map/ppermute | solution.py:82
  366.2 11.6 %collective-permute-start.74 = (bf16[96,2304]{1,0:T(8,128)(2,1)S(1)}, bf16[96,2304]{1,0:T(8,128)(2,1)S(1)}, u32[]{:S(2)}, u32[]{:S(2)}) collective-permute-start(bf16[96,2304]{1,0:T(8,128)(2,1)S(1)} %collective-permute-done.68.refs_2_), channel_id=1, source_target_pairs={{0,8},{8,0},{16,24},{24,16},{1,9},{9,1},{17,25},{25,17},{2,10},{10... | collective-permute-start | bytes 1327112 | tf_op jit(solution)/shard_map/ppermute | solution.py:82
  370.3 7.5 %collective-permute-start.79 = (bf16[96,896]{1,0:T(8,128)(2,1)S(1)}, bf16[96,896]{1,0:T(8,128)(2,1)S(1)}, u32[]{:S(2)}, u32[]{:S(2)}) collective-permute-start(bf16[96,896]{1,0:T(8,128)(2,1)S(1)} %add_convert_fusion.7), channel_id=1, source_target_pairs={{0,2},{1,3},{2,4},{3,5},{4,6},{5,7},{6,0},{7,1},{8,10},{9,11},{10,... | collective-permute-start | bytes 516104 | tf_op jit(solution)/shard_map/ppermute | solution.py:114
  379.6 7.3 %collective-permute-start.83 = (bf16[96,896]{1,0:T(8,128)(2,1)S(1)}, bf16[96,896]{1,0:T(8,128)(2,1)S(1)}, u32[]{:S(2)}, u32[]{:S(2)}) collective-permute-start(bf16[96,896]{1,0:T(8,128)(2,1)S(1)} %add_convert_fusion.6), channel_id=1, source_target_pairs={{0,2},{1,3},{2,4},{3,5},{4,6},{5,7},{6,0},{7,1},{8,10},{9,11},{10,... | collective-permute-start | bytes 516104 | tf_op jit(solution)/shard_map/ppermute | solution.py:114
  (136 other events, 1168.3 us)
